TPU v7x, 32 devices: a whole 2x2x4 slice. The times are simulated.
32 devices in a mesh: section: 2 (over core), dp: 4 (over z), mp: 4 (over y, x).
Axes of the slice: x: 2, y: 2, z: 4, core: 2. Of those that a mesh axis runs over, the one named last changes fastest.
Arguments:
- inputs: bfloat16 [8, 1024, 1024], P('dp', 'mp'), may hold values from -1 to 1
- cotangent: bfloat16 [8, 1024, 1024], P('dp', 'mp'), may hold values from -11 to 11
- doc_ids: int32 [8, 1024], P('dp'), may hold values from 0 to 3, never falling along the last dimension, each value on 1 to 512 neighbouring positions
- attention_in: float32 [2, 3, 1024, 1024], P('section', None, None, ('mp', 'dp')), may hold values from -0.1875 to 0.1875
- attention_out: float32 [2, 1024, 1024], P('section', ('mp', 'dp')), may hold values from -0.1875 to 0.1875
- feedforward_in: float32 [2, 2, 1024, 4096], P('section', None, None, ('mp', 'dp')), may hold values from -0.1875 to 0.1875
- feedforward_out: float32 [2, 4096, 1024], P('section', ('mp', 'dp')), may hold values from -0.1875 to 0.1875
- unit_scales: float32 [2, 4, 2304], P('section', 'mp', 'dp'), may hold values from 0.75 to 3
- mix_rates: float32 [2, 2, 1024], P('section', None, 'dp'), may hold values from 0.25 to 0.75
- first_attention_in: float32 [2, 3, 1024, 1024], P('section', None, None, ('mp', 'dp')), may hold values from -1 to 1
- second_attention_in: float32 [2, 3, 1024, 1024], P('section', None, None, ('mp', 'dp')), may hold values from 0 to 1
- first_attention_out: float32 [2, 1024, 1024], P('section', ('mp', 'dp')), may hold values from -1 to 1
- second_attention_out: float32 [2, 1024, 1024], P('section', ('mp', 'dp')), may hold values from 0 to 1
- first_feedforward_in: float32 [2, 2, 1024, 4096], P('section', None, None, ('mp', 'dp')), may hold values from -1 to 1
- second_feedforward_in: float32 [2, 2, 1024, 4096], P('section', None, None, ('mp', 'dp')), may hold values from 0 to 1
- first_feedforward_out: float32 [2, 4096, 1024], P('section', ('mp', 'dp')), may hold values from -1 to 1
- second_feedforward_out: float32 [2, 4096, 1024], P('section', ('mp', 'dp')), may hold values from 0 to 1
- first_unit_scales: float32 [2, 4, 2304], P('section', 'mp', 'dp'), may hold values from -1 to 1
- second_unit_scales: float32 [2, 4, 2304], P('section', 'mp', 'dp'), may hold values from 0 to 1
- first_mix_rates: float32 [2, 2, 1024], P('section', None, 'dp'), may hold values from -1 to 1
- second_mix_rates: float32 [2, 2, 1024], P('section', None, 'dp'), may hold values from 0 to 1
Outputs:
- boundary_states: float32 [2, 8, 1024, 1024], P('section', 'dp', 'mp')
- gradient_norm: float32 [], replicated
- next_first_attention_in: float32 [2, 3, 1024, 1024], P('section', None, None, ('mp', 'dp'))
- next_second_attention_in: float32 [2, 3, 1024, 1024], P('section', None, None, ('mp', 'dp'))
- next_attention_in: float32 [2, 3, 1024, 1024], P('section', None, None, ('mp', 'dp'))
- next_first_attention_out: float32 [2, 1024, 1024], P('section', ('mp', 'dp'))
- next_second_attention_out: float32 [2, 1024, 1024], P('section', ('mp', 'dp'))
- next_attention_out: float32 [2, 1024, 1024], P('section', ('mp', 'dp'))
- next_first_feedforward_in: float32 [2, 2, 1024, 4096], P('section', None, None, ('mp', 'dp'))
- next_second_feedforward_in: float32 [2, 2, 1024, 4096], P('section', None, None, ('mp', 'dp'))
- next_feedforward_in: float32 [2, 2, 1024, 4096], P('section', None, None, ('mp', 'dp'))
- next_first_feedforward_out: float32 [2, 4096, 1024], P('section', ('mp', 'dp'))
- next_second_feedforward_out: float32 [2, 4096, 1024], P('section', ('mp', 'dp'))
- next_feedforward_out: float32 [2, 4096, 1024], P('section', ('mp', 'dp'))
- next_first_unit_scales: float32 [2, 4, 2304], P('section', 'mp', 'dp')
- next_second_unit_scales: float32 [2, 4, 2304], P('section', 'mp', 'dp')
- next_unit_scales: float32 [2, 4, 2304], P('section', 'mp', 'dp')
- next_first_mix_rates: float32 [2, 2, 1024], P('section', None, 'dp')
- next_second_mix_rates: float32 [2, 2, 1024], P('section', None, 'dp')
- next_mix_rates: float32 [2, 2, 1024], P('section', None, 'dp')
Inputs may be any that keep to these rules, and one draw needn't show every extreme that they name: `doc_ids`: never falls along a sequence; each document holds 1 to 512 positions and one holds exactly 512.
All inputs are finite; a program needn't handle non-finite values.
Results may differ from a plain program's by a relative error of at most 0.033.
The roundings to bfloat16 on the way count: a program that leaves them out, or rounds other values in their place, can miss the bound.
Values may be sent and summed in bfloat16 or wider, within the bound.
No kernel may reach another device: no remote copies, remote signals or barrier semaphores. Data moves between devices by JAX's collectives and lax.ppermute only.
A program may use at most 384 MiB of HBM per device.

v0:
```python
import functools
import math

import jax
import jax.numpy as jnp
from jax import lax
from jax.experimental import pallas as pl
from jax.experimental.pallas import tpu as pltpu
from jax.sharding import PartitionSpec as P

HD = 64
STEP = 10

NORM_EPSILON = 1e-06
ROPE_BASE = 10000.0
CLIP_NORM = 0.1
LEARN_RATE = 0.05
SCALE_RATE = 1.25
MIXING_RATE = 0.4
BETA_FIRST = 0.9
BETA_SECOND = 0.95
ADAM_EPSILON = 1e-08

BF16 = jnp.bfloat16
F32 = jnp.float32


def exchange(block, axis, bit):
    route = [(i, i ^ bit) for i in range(lax.axis_size(axis))]
    return lax.ppermute(block, axis, route)


def gray(place):
    return place ^ (place >> 1)


def ring_place(index, size):
    shift = 1
    while shift < size:
        index = index ^ (index >> shift)
        shift *= 2
    return index


def ring_step(block, axis):
    size = lax.axis_size(axis)
    route = []
    for place in range(size):
        route.append((gray(place), gray((place + 1) % size)))
        route.append((size + gray(place), size + gray((place - 1) % size)))
    return lax.ppermute(block, ("section", axis), route)


def ring_sources(axis):
    size = lax.axis_size(axis)
    place = ring_place(lax.axis_index(axis), size)
    way = 1 - 2 * lax.axis_index("section")
    return [gray((place - way * step + size) % size) for step in range(size)]


def spread_rows(block, axis="mp"):
    blocks = [block]
    for _ in range(lax.axis_size(axis) - 1):
        blocks.append(ring_step(blocks[-1], axis))
    return blocks


def sum_over(values, axis):
    bit = 1
    while bit < lax.axis_size(axis):
        values = values + exchange(values, axis, bit)
        bit *= 2
    return values


def gather_small(values, axis):
    index = lax.axis_index(axis)
    gathered = values[None]
    bit = 1
    while bit < lax.axis_size(axis):
        other = exchange(gathered, axis, bit)
        low = (index & bit) == 0
        gathered = jnp.concatenate(
            [jnp.where(low, gathered, other), jnp.where(low, other, gathered)], axis=0
        )
        bit *= 2
    return gathered


def unit_norm(values):
    return values * lax.rsqrt(jnp.sum(values * values, axis=-1, keepdims=True) + NORM_EPSILON)


def document_starts(doc_row):
    position = jnp.arange(doc_row.shape[-1], dtype=jnp.int32)
    change = jnp.concatenate([jnp.ones((1,), dtype=jnp.bool_), doc_row[1:] != doc_row[:-1]])
    return lax.cummax(jnp.where(change, position, 0), axis=0)


def rope_tables(offsets):
    half_width = HD // 2
    inverse = 1.0 / ROPE_BASE ** (jnp.arange(half_width, dtype=F32) * (2.0 / HD))
    angles = inverse[:, None] * offsets.astype(F32)[..., None, :]
    angles = jnp.concatenate([angles, angles], axis=-2)
    return jnp.cos(angles), jnp.sin(angles)


def mix_residual(hidden, branch, mixing):
    return unit_norm(hidden + mixing * (unit_norm(branch) - hidden))


NT = (((1,), (1,)), ((), ()))
TN = (((0,), (0,)), ((), ()))
NN = (((1,), (0,)), ((), ()))
VMEM = pltpu.VMEM
WHOLE, NEAR = "whole", "near"
SCALARS = pl.BlockSpec(memory_space=pltpu.SMEM)


def mul(left, right, dims=NN):
    return lax.dot_general(left, right, dims, preferred_element_type=F32)


def block_of(array):
    zeros = (0,) * len(array.shape)
    return pl.BlockSpec(array.shape, lambda *place: zeros)


def call(body, out_shape, in_specs, flops, moved, scratch=(), grid=(1,), out_specs=None, loose=()):
    def run(*args):
        specs = [
            block_of(arg) if spec in (WHOLE, NEAR) else spec for spec, arg in zip(in_specs, args)
        ]
        args = [
            arg if spec in (SCALARS, NEAR) else pltpu.with_memory_space_constraint(arg, pltpu.HBM)
            for spec, arg in zip(in_specs, args)
        ]
        return pl.pallas_call(
            body,
            out_shape=[
                out if at in loose else pltpu.HBM(out.shape, out.dtype)
                for at, out in enumerate(out_shape)
            ],
            grid=grid,
            in_specs=specs,
            out_specs=out_specs or [block_of(out) for out in out_shape],
            scratch_shapes=list(scratch),
            compiler_params=pltpu.CompilerParams(vmem_limit_bytes=50 << 20),
            cost_estimate=pl.CostEstimate(flops=flops, bytes_accessed=moved, transcendentals=0),
        )(*args)

    return run


def shape(dims, dtype):
    return jax.ShapeDtypeStruct(dims, dtype)


def turned(raw, cosine, sine):
    half = HD // 2
    first, second = raw[:half], raw[half:]
    return jnp.concatenate(
        [
            first * cosine[:half] - second * sine[:half],
            second * cosine[half:] + first * sine[half:],
        ],
        axis=0,
    )


def turned_back(grad, cosine, sine):
    half = HD // 2
    first, second = grad[:half], grad[half:]
    return jnp.concatenate(
        [
            first * cosine[:half] + second * sine[half:],
            second * cosine[half:] - first * sine[:half],
        ],
        axis=0,
    )


def rows_at(places):
    return [row for at in places for row in ((at,) if at < 3 else (3, 4))]


def side_by_side(refs):
    return refs[0][...] if len(refs) == 1 else jnp.concatenate([ref[...] for ref in refs], axis=0)


def project_kernel(places, *refs):
    count = len(rows_at(places))
    weight, cosine, sine, gains = refs[count : count + 4]
    tokens = cosine.shape[2]
    x, outs = side_by_side(refs[:count]), refs[count + 4 :]
    for n, at in enumerate(places):
        raw_out, query, keys, values = outs[4 * n : 4 * n + 4]
        width = query.shape[0]
        raw = mul(weight[...], x[n * tokens : (n + 1) * tokens], NT)
        raw_out[...] = raw[: 2 * width]
        values[...] = raw[2 * width :].astype(BF16)
        for part, out in ((0, query), (1, keys)):
            for top in range(0, width, HD):
                turn = turned(
                    raw[part * width + top : part * width + top + HD], cosine[at], sine[at]
                )
                scale = lax.rsqrt(jnp.sum(turn * turn, axis=0, keepdims=True) + NORM_EPSILON)
                head = (turn * scale * gains[top : top + HD]).astype(BF16)
                out[top : top + HD] = head * math.sqrt(HD) if part == 0 else head


def project_blocks(places, x, weight, cosine, sine, gains):
    tokens, depth, count = cosine.shape[2], weight.shape[1], len(places)
    width = weight.shape[0] // 3
    low = shape((width, tokens), BF16)
    outs = call(
        functools.partial(project_kernel, places),
        [shape((2 * width, tokens), F32), low, low, low] * count,
        [NEAR] * len(x) + [WHOLE] * 4,
        2 * tokens * depth * 3 * width * count,
        2 * 3 * width * depth,
    )(*x, weight, cosine, sine, gains)
    return [outs[4 * n : 4 * n + 4] for n in range(count)]


def near(info, at, other, tokens):
    return (info[other] <= info[at]) & ((info[other] + 1) * tokens > info[4 + at])


def seen(info, at, other, starts, tokens):
    key_place = info[other] * tokens + lax.broadcasted_iota(jnp.int32, (tokens, tokens), 0)
    query_place = info[at] * tokens + lax.broadcasted_iota(jnp.int32, (tokens, tokens), 1)
    return (key_place <= query_place) & (key_place >= starts)


def share_out(partial, value):
    partial[...] = value.astype(partial.dtype)


def partial_shape(at, tokens, depth):
    return shape((tokens, depth), BF16 if at else F32)


def attend_kernel(places, info, starts, *refs):
    count = len(places)
    query, rest = refs[:count], refs[count:]
    keys, values, weight, outs, (total, sums) = rest[:4], rest[4:8], rest[8], rest[9:-2], rest[-2:]
    width, tokens = query[0].shape
    for n, at in enumerate(places):
        attended, logsums, partial = outs[3 * n : 3 * n + 3]
        total[n] = jnp.zeros((width, tokens), F32)
        sums[n] = jnp.ones((8, tokens), F32)
        sums[n, : width // HD] = jnp.zeros((width // HD, tokens), F32)
        for other in range(4):

            @pl.when(near(info, at, other, tokens))
            def _():
                allowed = seen(info, at, other, starts[at : at + 1], tokens)
                for head in range(width // HD):
                    rows = slice(head * HD, head * HD + HD)
                    shares = jnp.exp(mul(keys[other][rows], query[n][rows], TN))
                    shares = jnp.where(allowed, shares, 0.0)
                    sums[n, head : head + 1] += jnp.sum(shares, axis=0, keepdims=True)
                    total[n, rows] += mul(values[other][rows], shares.astype(BF16))

        logsums[...] = jnp.log(sums[n])
        inverse = 1.0 / sums[n]
        for head in range(width // HD):
            rows = slice(head * HD, head * HD + HD)
            attended[rows] = (total[n, rows] * inverse[head : head + 1]).astype(BF16)
        share_out(partial, mul(attended[...], weight[...], TN))


def attend_blocks(places, info, starts, query, keys, values, weight):
    width, tokens = query[0].shape
    depth, count = weight.shape[1], len(places)
    outs = call(
        functools.partial(attend_kernel, places),
        [
            out
            for at in places
            for out in (
                shape((width, tokens), BF16),
                shape((8, tokens), F32),
                partial_shape(at, tokens, depth),
            )
        ],
        [SCALARS] + [WHOLE] * (10 + count),
        2 * tokens * (depth * width + 10 * tokens * 256) * count,
        2 * depth * width,
        [VMEM((count, width, tokens), F32), VMEM((count, 8, tokens), F32)],
        loose=[3 * n + 2 for n, at in enumerate(places) if at],
    )(info, starts, *[query[at] for at in places], *keys, *values, weight)
    return [outs[3 * n : 3 * n + 3] for n in range(count)]


def attend_back_kernel(info, starts, *refs):
    query, keys, values, attended, logsums, raw = (refs[4 * n : 4 * n + 4] for n in range(6))
    grads, (w_out, w_in, cosine, sine, gains) = refs[24:29], refs[29:34]
    low, partial, gain_grad = refs[34:38], refs[38:42], refs[42]
    pulled, deltas, grad_query, grad_keys, grad_values = refs[43:]
    width, tokens = query[0].shape
    heads = width // HD
    grad_query[...] = jnp.zeros_like(grad_query)
    grad_keys[...] = jnp.zeros_like(grad_keys)
    grad_values[...] = jnp.zeros_like(grad_values)
    deltas[...] = jnp.zeros_like(deltas)
    for at in range(4):
        rows = side_by_side([grads[row] for row in rows_at((at,))])
        grad = mul(w_out[...], rows, NT).astype(BF16)
        pulled[at] = grad
        product = grad.astype(F32) * attended[at][...].astype(F32)
        for head in range(heads):
            rows = slice(head * HD, head * HD + HD)
            deltas[at, head : head + 1] = jnp.sum(product[rows], axis=0, keepdims=True)
    for at in range(4):
        for other in range(4):

            @pl.when(near(info, at, other, tokens))
            def _():
                allowed = seen(info, at, other, starts[at : at + 1], tokens)
                for head in range(heads):
                    rows = slice(head * HD, head * HD + HD)
                    grad_rows, query_rows = pulled[at, rows], query[at][rows]
                    scores = mul(keys[other][rows], query_rows, TN) - logsums[at][head : head + 1]
                    shares = jnp.where(allowed, jnp.exp(scores), 0.0)
                    grad_shares = mul(values[other][rows], grad_rows, TN)
                    grad_scores = shares * (grad_shares - deltas[at, head : head + 1])
                    grad_scores = grad_scores.astype(BF16)
                    grad_values[other, rows] += mul(grad_rows, shares.astype(BF16), NT)
                    grad_keys[other, rows] += mul(query_rows, grad_scores, NT)
                    grad_query[at, rows] += mul(keys[other][rows], grad_scores)

    gain_total = [0.0] * heads
    for at in range(4):
        cos, sin = cosine[at], sine[at]
        for part, source, factor in ((0, grad_query, math.sqrt(HD)), (1, grad_keys, 1.0)):
            for head in range(heads):
                rows = slice(head * HD, head * HD + HD)
                turn = turned(raw[at][part * width + head * HD : part * width + head * HD + HD], cos, sin)
                scale = lax.rsqrt(jnp.sum(turn * turn, axis=0, keepdims=True) + NORM_EPSILON)
                unit = turn * scale
                grad = source[at, rows] * factor
                gain_total[head] = gain_total[head] + grad * unit
                grad = grad * gains[rows]
                grad = scale * (grad - unit * jnp.sum(unit * grad, axis=0, keepdims=True))
                low[at][part * width + head * HD : part * width + head * HD + HD] = turned_back(
                    grad, cos, sin
                ).astype(BF16)
        low[at][2 * width :] = grad_values[at].astype(BF16)
        share_out(partial[at], mul(low[at][...], w_in[...], TN))
    for head in range(heads):
        gain_grad[head * HD : head * HD + HD] = jnp.sum(gain_total[head], axis=1, keepdims=True)


def attend_back(info, starts, query, keys, values, attended, logsums, raw, grads,
                w_out, w_in, cosine, sine, gains):
    width, tokens = query[0].shape
    depth = w_out.shape[1]
    low = shape((3 * width, tokens), BF16)
    block = VMEM((4, width, tokens), F32)
    outs = call(
        attend_back_kernel,
        [low] * 4
        + [partial_shape(at, tokens, depth) for at in range(4)]
        + [shape((width, 1), F32)],
        [SCALARS] + [WHOLE] * 25 + [NEAR] * 5 + [WHOLE] * 5,
        2 * 4 * tokens * (depth * width * 4 + 60 * tokens * 256),
        2 * depth * width * 12,
        [VMEM((4, width, tokens), BF16), VMEM((4, 8, tokens), F32), block, block, block],
        loose=(5, 6, 7),
    )(info, starts, *query, *keys, *values, *attended, *logsums, *raw, *grads,
      w_out, w_in, cosine, sine, gains)
    return outs[:4], outs[4:8], outs[8]


CHUNK = 256
GATE_WIDTH = math.sqrt(1024)


def started(copies, arrived, first=0):
    copies = [
        pltpu.make_async_copy(source, target, arrived.at[first + n])
        for n, (source, target) in enumerate(copies)
    ]
    for copy in copies:
        copy.start()
    return copies


def fetch_weights(own, other, weights, arrived):
    half = own.shape[1]
    size = min(CHUNK, half)
    places = [(index, start) for index in range(2) for start in range(0, half, size)]
    copies = started(
        [
            ((own, other)[index].at[:, pl.ds(start, size)], weights.at[index, :, pl.ds(start, size)])
            for index, start in places
        ],
        arrived,
    )
    return [
        (copy, index, slice(start, start + size), slice(index * half + start, index * half + start + size))
        for copy, (index, start) in zip(copies, places)
    ]


def feed_kernel(given, count, *refs):
    x, refs = refs[:given], refs[given:]
    (own, other, scales_in), outs, partial = refs[:3], refs[3 : 3 * count + 3], refs[3 * count + 3 : 4 * count + 3]
    weights, scales, ups, gates, gated, gated_turned, arrived, came, left = refs[4 * count + 3 :]
    half, tokens = own.shape[1], ups.shape[0] // count
    (scales_copy,) = started([(scales_in, scales)], came)
    chunks = fetch_weights(own, other, weights, arrived)
    block = side_by_side(x)
    scales_copy.wait()
    leaving = []
    for copy, index, rows, units in chunks:
        copy.wait()
        up, gate = mul(block, weights[index, 0, rows], NT), mul(block, weights[index, 1, rows], NT)
        ups[:, units] = up.astype(BF16)
        gates[:, units] = gate.astype(BF16)
        z = gate * (scales[1:2, units] * GATE_WIDTH)
        silu = z * (0.5 + 0.5 * jnp.tanh(0.5 * z))
        mixed = (up * scales[0:1, units] * silu).astype(BF16)
        gated[:, units] = mixed
        gated_turned[units] = mixed.T
        if rows.stop == half:
            columns = pl.ds(index * half, half)
            for n in range(count):
                places = pl.ds(n * tokens, tokens)
                leaving += started(
                    [
                        (ups.at[places, columns], outs[3 * n].at[:, columns]),
                        (gates.at[places, columns], outs[3 * n + 1].at[:, columns]),
                        (gated_turned.at[columns, places], outs[3 * n + 2].at[columns]),
                    ],
                    left,
                    3 * (index * count + n),
                )
    total = mul(gated[:, :half], weights[0, 2]) + mul(gated[:, half:], weights[1, 2])
    for n in range(count):
        share_out(partial[n], total[n * tokens : (n + 1) * tokens])
    for copy in leaving:
        copy.wait()


def feed_back_kernel(given, count, *refs):
    g, refs = refs[:given], refs[given:]
    (own, other, scales_in), kept = refs[:3], refs[3 : 2 * count + 3]
    outs, scale_grad = refs[2 * count + 3 : 4 * count + 3], refs[4 * count + 3]
    partial = refs[4 * count + 4 : 5 * count + 4]
    weights, scales, ups, gates, low_up, low_gate, up_turned, gate_turned = refs[5 * count + 4 : -3]
    arrived, came, left = refs[-3:]
    half, tokens = own.shape[1], ups.shape[0] // count
    (scales_copy,) = started([(scales_in, scales)], came)
    chunks = fetch_weights(own, other, weights, arrived)
    coming = [
        started(
            [
                (ref.at[:, pl.ds(index * half, half)],
                 into.at[pl.ds(n * tokens, tokens), pl.ds(index * half, half)])
                for n in range(count)
                for ref, into in ((kept[2 * n], ups), (kept[2 * n + 1], gates))
            ],
            came,
            1 + 2 * count * index,
        )
        for index in range(2)
    ]
    block = side_by_side(g)
    scales_copy.wait()
    leaving = []
    for copy, index, rows, units in chunks:
        copy.wait()
        grad = mul(block, weights[index, 2, rows], NT)
        if rows.start == 0:
            for copy in coming[index]:
                copy.wait()
        up, gate = ups[:, units].astype(F32), gates[:, units].astype(F32)
        s_up, s_gate = scales[0:1, units], scales[1:2, units] * GATE_WIDTH
        z = gate * s_gate
        sigmoid = 0.5 + 0.5 * jnp.tanh(0.5 * z)
        silu = z * sigmoid
        grad_silu = grad * silu
        grad_z = grad * (up * s_up) * (sigmoid + silu * (1.0 - sigmoid))
        grad_up, grad_gate = (grad_silu * s_up).astype(BF16), (grad_z * s_gate).astype(BF16)
        low_up[:, units], low_gate[:, units] = grad_up, grad_gate
        up_turned[units], gate_turned[units] = grad_up.T, grad_gate.T
        scale_grad[0:1, units] = jnp.sum(grad_silu * up, axis=0, keepdims=True)
        scale_grad[1:2, units] = jnp.sum(grad_z * gate, axis=0, keepdims=True) * GATE_WIDTH
        if rows.stop == half:
            columns = pl.ds(index * half, half)
            for n in range(count):
                places = pl.ds(n * tokens, tokens)
                leaving += started(
                    [
                        (up_turned.at[columns, places], outs[2 * n].at[columns]),
                        (gate_turned.at[columns, places], outs[2 * n + 1].at[columns]),
                    ],
                    left,
                    2 * (index * count + n),
                )
    total = mul(low_up[:, :half], weights[0, 0]) + mul(low_up[:, half:], weights[1, 0])
    total = total + mul(low_gate[:, :half], weights[0, 1]) + mul(low_gate[:, half:], weights[1, 1])
    for n in range(count):
        share_out(partial[n], total[n * tokens : (n + 1) * tokens])
    for copy in leaving:
        copy.wait()


HELD = pl.BlockSpec(memory_space=pl.ANY)


def feed_call(body, places, x, weights, scales, kept, held, pair, low, turned_count):
    half, count = weights[0].shape[1], len(places)
    tokens, depth = sum(block.shape[0] for block in x) // count, x[0].shape[1]
    partial = [partial_shape(at, tokens, depth) for at in places]
    semaphores = pltpu.SemaphoreType.DMA
    return call(
        functools.partial(body, len(x), count),
        held + pair + partial,
        [NEAR] * len(x) + [HELD] * (3 + len(kept)),
        2 * 6 * tokens * depth * half * count,
        2 * 6 * depth * half,
        [VMEM((2, 3, half, depth), BF16), VMEM(scales.shape, F32)]
        + [VMEM((count * tokens, 2 * half), BF16)] * low
        + [VMEM((2 * half, count * tokens), BF16)] * turned_count
        + [
            semaphores((2 * half // min(CHUNK, half),)),
            semaphores((1 + 2 * len(kept),)),
            semaphores((2 * len(held),)),
        ],
        out_specs=[HELD] * len(held) + [block_of(out) for out in pair + partial],
        loose=[len(held + pair) + n for n, at in enumerate(places) if at],
    )(*x, *weights, scales, *kept)


def feed_blocks(places, x, weights, scales):
    count = len(places)
    dims = (sum(block.shape[0] for block in x) // count, 2 * weights[0].shape[1])
    held = [shape(dims, BF16), shape(dims, BF16), shape(dims[::-1], BF16)] * count
    outs = feed_call(feed_kernel, places, x, weights, scales, (), held, [], 3, 1)
    return [[*outs[3 * n : 3 * n + 3], outs[3 * count + n]] for n in range(count)]


def feed_back_blocks(places, g, weights, scales, ups, gates):
    count = len(places)
    held = [shape(ups[0].shape[::-1], BF16)] * (2 * count)
    pair = [shape((2, ups[0].shape[1]), F32)]
    kept = [array for at in places for array in (ups[at], gates[at])]
    outs = feed_call(feed_back_kernel, places, g, weights, scales, kept, held, pair, 4, 2)
    return [
        [*outs[2 * n : 2 * n + 2], outs[2 * count] if n == 0 else None, outs[2 * count + 1 + n]]
        for n in range(count)
    ]


def feed_grad_kernel(has_other, *refs):
    middle, mixed, (ups, gates, gated) = refs[:5], refs[5:10], (refs[10:14], refs[14:18], refs[18:22])
    out = refs[-1]
    for row, (units, right) in enumerate(((ups, middle), (gates, middle), (gated, mixed))):
        left = jnp.concatenate([block[...] for block in units], axis=1)
        total = mul(left, side_by_side(right))
        if has_other:
            total = total + refs[22][row].astype(F32)
        out[row] = total.astype(BF16)


def feed_grads(half_at, middle, mixed, ups, gates, gated, other=None):
    units, tokens = ups[0].shape
    depth, half = middle[0].shape[1], units // 2
    part = pl.BlockSpec((half, tokens), lambda i: (half_at, 0))
    more = () if other is None else (other,)
    return call(
        functools.partial(feed_grad_kernel, bool(more)),
        [shape((3, half, depth), BF16)],
        [WHOLE] * 5 + [NEAR] * 5 + [part] * 12 + [NEAR] * len(more),
        2 * 3 * 4 * tokens * half * depth,
        2 * 12 * tokens * (half + depth),
    )(*middle, *mixed, *ups, *gates, *gated, *more)[0]


def attend_grad_kernel(section, *refs):
    low, attended, hidden, grads = refs[:4], refs[4:8], refs[8:13], refs[13:18]
    own, other = refs[18:]
    width, half = attended[0].shape[0], own.shape[1]
    for lefts, rights, top in ((low, hidden, 0), (attended, grads, 3 * width)):
        right = side_by_side(rights)
        for start in range(0, lefts[0].shape[0], width):
            total = mul(
                jnp.concatenate([left[start : start + width] for left in lefts], axis=1), right
            )
            rows = slice(top + start, top + start + width)
            for place in range(2):
                columns = total[:, place * half : place * half + half]

                @pl.when(section[0] == place)
                def _():
                    own[rows] = columns

                @pl.when(section[0] != place)
                def _():
                    other[rows] = columns.astype(BF16)


def attend_grads(section, low, attended, hidden, grads):
    width, tokens = attended[0].shape
    depth = hidden[0].shape[1]
    return call(
        attend_grad_kernel,
        [shape((4 * width, depth // 2), F32), shape((4 * width, depth // 2), BF16)],
        [SCALARS] + [WHOLE] * 13 + [NEAR] * 5,
        2 * 4 * 4 * tokens * width * depth,
        2 * 16 * tokens * depth,
    )(section, *low, *attended, *hidden, *grads)


def adam_kernel(axis, factor, weight, first, second, gradient, first_out, second_out, weight_out):
    clipped = gradient[...].astype(F32) * factor[0]
    first_new = BETA_FIRST * first[...] + (1.0 - BETA_FIRST) * clipped
    second_new = BETA_SECOND * second[...] + (1.0 - BETA_SECOND) * clipped * clipped
    first_out[...] = first_new
    second_out[...] = second_new
    first_hat = first_new / (1.0 - BETA_FIRST**STEP)
    second_hat = second_new / (1.0 - BETA_SECOND**STEP)
    moved = weight[...] - LEARN_RATE * first_hat / (jnp.sqrt(second_hat) + ADAM_EPSILON)
    scale = lax.rsqrt(jnp.sum(moved * moved, axis=axis, keepdims=True) + NORM_EPSILON)
    weight_out[...] = moved * scale


def adam_matrix(factor, weight, first, second, gradient, axis, block, place, grid):
    spec = pl.BlockSpec(block, place)
    return call(
        functools.partial(adam_kernel, axis),
        [shape(weight.shape, F32)] * 3,
        [SCALARS] + [spec] * 4,
        20 * weight.size,
        28 * weight.size,
        grid=grid,
        out_specs=[spec] * 3,
    )(factor, weight, first, second, gradient)


def add_parts(parts):
    total = parts[0][...].astype(F32)
    for part in parts[1:]:
        total = total + part[...].astype(F32)
    return total


def mix_kernel(count, hidden, rate, *refs):
    branch_out, result, result_low = refs[count:]
    branch = add_parts(refs[:count])
    branch_out[...] = branch
    mixed = mix_residual(hidden[...].astype(F32), branch, rate[...])
    result[...] = mixed
    result_low[...] = mixed.astype(BF16)


def mix_block(hidden, rate, parts):
    dims = hidden.shape
    return call(
        functools.partial(mix_kernel, len(parts)),
        [shape(dims, F32), shape(dims, F32), shape(dims, BF16)],
        [WHOLE] * 2 + [WHOLE if part.dtype == F32 else NEAR for part in parts],
        10 * dims[0] * dims[1],
        8 * dims[0] * dims[1],
    )(hidden, rate, *parts)


def mix_back_kernel(count, rounded, hidden, branch, rate, *refs):
    grad_hidden, grad_branch, grad_rate = refs[count:]
    upstream = add_parts(refs[:count])
    if rounded:
        upstream = upstream.astype(BF16).astype(F32)
    h, b, r = hidden[...].astype(F32), branch[...], rate[...]
    scale = lax.rsqrt(jnp.sum(b * b, axis=-1, keepdims=True) + NORM_EPSILON)
    unit = b * scale
    apart = unit - h
    mixed = h + r * apart
    mixed_scale = lax.rsqrt(jnp.sum(mixed * mixed, axis=-1, keepdims=True) + NORM_EPSILON)
    mixed = mixed * mixed_scale
    grad = mixed_scale * (upstream - mixed * jnp.sum(mixed * upstream, axis=-1, keepdims=True))
    grad_rate[...] = jnp.sum(grad * apart, axis=0, keepdims=True)
    grad_unit = grad * r
    grad_hidden[...] = grad - grad_unit
    grad_unit = scale * (grad_unit - unit * jnp.sum(unit * grad_unit, axis=-1, keepdims=True))
    grad_branch[...] = grad_unit.astype(BF16)


def mix_back_block(hidden, branch, rate, parts, rounded=False):
    dims = hidden.shape
    return call(
        functools.partial(mix_back_kernel, len(parts), rounded),
        [shape(dims, F32), shape(dims, BF16), shape((1, dims[1]), F32)],
        [WHOLE] * 3 + [WHOLE if part.dtype == F32 else NEAR for part in parts],
        20 * dims[0] * dims[1],
        12 * dims[0] * dims[1],
    )(hidden, branch, rate, *parts)


def tie(*values):
    return lax.optimization_barrier(values)


def to(block, at):
    return exchange(block, "mp", at)


def pass_halves(first, second):
    half = first.shape[0] // 2
    return [to(second[:half], 1), to(first[half:], 2)]


def layer_forward(hidden, low, params, tables, tied, feed_own, later=None):
    attend_in, attend_out, gains, scales, mixing = params
    cosine, sine, starts, info = tables
    project = lambda *places: project_blocks(
        places, [blocks[row] for row in rows_at(places)], attend_in, cosine, sine, gains
    )
    blocks = [low, to(low, 1), to(low, 2)]
    if tied:
        heads = project(0)
        *blocks, heads = tie(*blocks, heads)
        blocks += pass_halves(*blocks[1:])
        heads += project(1, 2)
        *blocks, heads = tie(*blocks, heads)
        heads += project(3)
    else:
        blocks += pass_halves(*blocks[1:])
        heads = project(0, 1, 2, 3)
    raw, query, keys, values = zip(*heads)
    attend = lambda *places: attend_blocks(places, info, starts, query, keys, values, attend_out)
    far = attend(3)
    sent = [to(far[0][-1], 3)]
    near_blocks = attend(1, 2)
    sent += [to(block[-1], at) for at, block in zip((1, 2), near_blocks)]
    attended = attend(0) + near_blocks + far
    sent, attended[0], feed_own = tie(sent, attended[0], feed_own)
    feed_weights = (feed_own, exchange(feed_own, "section", 1))
    branch, middle, middle_low = mix_block(hidden, mixing[:1], (attended[0][-1], *sent))
    blocks_middle, fed, parts = feed_exchange(
        middle_low, lambda places, x: feed_blocks(places, x, feed_weights, scales)
    )
    mixed, result, result_low = mix_block(middle, mixing[1:], parts)
    if later is not None:
        result_low, later = tie(result_low, later)
        later = (later, exchange(later, "section", 1))
    ups, gates, gated, _ = zip(*fed)
    attended, logsums, _ = zip(*attended)
    stored = (
        (hidden, branch, blocks, raw, query, keys, values, attended, logsums),
        (middle, mixed, blocks_middle, ups, gates, gated),
    )
    return result, result_low, stored, feed_weights, later


def feed_exchange(block, work):
    blocks = [block, to(block, 1), to(block, 2)]
    done = work((0,), blocks[:1])
    *blocks, done = tie(*blocks, done)
    blocks += pass_halves(*blocks[1:])
    done += work((1, 2), blocks[1:3])
    sent = [to(done[at][-1], at) for at in (1, 2)]
    *blocks, done = tie(*blocks, done)
    done += work((3,), blocks[3:])
    sent.append(to(done[3][-1], 3))
    return blocks, done, (done[0][-1], *sent)


def layer_backward(stored, upstream, rounded, params, tables, feed_weights, section, hooks=()):
    attend_in, attend_out, gains, scales, mixing = params
    cosine, sine, starts, info = tables
    attend_stored, (middle, mixed, blocks_middle, ups, gates, gated) = stored
    hidden, branch, blocks_hidden, raw, query, keys, values, attended, logsums = attend_stored
    grad_middle, grad_mixed, rate_two = mix_back_block(
        middle, mixed, mixing[1:], upstream, rounded
    )
    blocks_mixed, done, parts = feed_exchange(
        grad_mixed, lambda places, g: feed_back_blocks(places, g, feed_weights, scales, ups, gates)
    )
    low_ups, low_gates, scale_grads, _ = zip(*done)
    operands = (blocks_middle, blocks_mixed, low_ups, low_gates, gated)
    other = feed_grads(1, *operands)
    parts, other = tie(parts, other)
    other = exchange(other, "section", 1)
    grad_hidden, grad_branch, rate_one = mix_back_block(
        hidden, branch, mixing[:1], (grad_middle, *parts)
    )
    grads = [grad_branch, to(grad_branch, 1), to(grad_branch, 2)]
    feed_sums = feed_grads(0, *operands, other)
    grads, _ = tie(grads, feed_sums)
    grads += pass_halves(*grads[1:])
    small = (scale_grads[0] + scale_grads[1] + scale_grads[3], rate_one[0], rate_two[0])
    if hooks:
        small = hooks[0](small)
    low, partial, gain_grad = attend_back(
        info, starts, query, keys, values, attended, logsums, raw, grads,
        attend_out, attend_in, cosine, sine, gains,
    )
    sent = [to(partial[at], at) for at in (3, 1, 2)]
    if hooks:
        low, small = hooks[1](low, small, gain_grad[:, 0])
    own, other = attend_grads(section, low, attended, blocks_hidden, grads)
    if hooks:
        other, small = hooks[2](other, small)
    other = exchange(other, "section", 1)
    attend_sums = (own + other.astype(F32)).astype(BF16).reshape(4, -1, own.shape[1])
    return (grad_hidden, partial[0], *sent), feed_sums, attend_sums, gain_grad[:, 0], small


def adam_update(weight, first, second, gradient, factor, rate):
    clipped = gradient * factor
    first_new = BETA_FIRST * first + (1.0 - BETA_FIRST) * clipped
    second_new = BETA_SECOND * second + (1.0 - BETA_SECOND) * clipped * clipped
    first_hat = first_new / (1.0 - BETA_FIRST**STEP)
    second_hat = second_new / (1.0 - BETA_SECOND**STEP)
    moved = weight - rate * first_hat / (jnp.sqrt(second_hat) + ADAM_EPSILON)
    return (first_new, second_new, moved)


def per_device(
    inputs,
    cotangent,
    doc_ids,
    attention_in,
    attention_out,
    feedforward_in,
    feedforward_out,
    unit_scales,
    mix_rates,
    first_attention_in,
    second_attention_in,
    first_attention_out,
    second_attention_out,
    first_feedforward_in,
    second_feedforward_in,
    first_feedforward_out,
    second_feedforward_out,
    first_unit_scales,
    second_unit_scales,
    first_mix_rates,
    second_mix_rates,
):
    section = lax.axis_index("section")
    is_first = section == 0
    dp_index = lax.axis_index("dp")
    dp_size = lax.axis_size("dp")
    local_rows = inputs.shape[1]

    def ordered(own, other):
        return jnp.where(is_first, own, other), jnp.where(is_first, other, own)

    def halves(array, dim):
        width = array.shape[dim] // 2
        own = lax.dynamic_slice_in_dim(array, section * width, width, dim)
        other = lax.dynamic_slice_in_dim(array, (1 - section) * width, width, dim)
        return own, other

    hidden_low = lax.dynamic_index_in_dim(inputs, section, 0, False)

    attend_rows = jnp.concatenate(
        [jnp.swapaxes(attention_in[0], 1, 2), attention_out], axis=0
    ).astype(BF16)
    small = jnp.concatenate([unit_scales.reshape(-1), mix_rates.reshape(-1)]).astype(BF16)
    def gather_ring(half):
        if dp_size != 4:
            whole = lax.all_gather(half, "dp", axis=1, tiled=True)
            return whole, whole
        blocks, count = spread_rows(half, "dp"), half.shape[1]
        whole = jnp.zeros((half.shape[0], dp_size * count, half.shape[2]), BF16)
        for source, block in zip(ring_sources("dp"), blocks):
            whole = lax.dynamic_update_slice_in_dim(whole, block, source * count, 1)
        return whole, blocks[-2]

    own, other = halves(attend_rows, 2)
    attend_pieces = ordered(own, exchange(other, "section", 1))
    attend_pieces, feedforward_in_here, feedforward_out_here = tie(
        attend_pieces, feedforward_in, feedforward_out
    )
    feed_rows = jnp.concatenate(
        [jnp.swapaxes(feedforward_in_here[0].astype(BF16), 1, 2), feedforward_out_here.astype(BF16)], axis=0
    )
    own, other = halves(feed_rows, 1)
    feed_pieces = ordered(own, exchange(other, "section", 1))
    attend_first, came = gather_ring(attend_pieces[0])
    attend_second, *feed_pieces, _ = tie(attend_pieces[1], *feed_pieces, came)
    attend_owns = (attend_first, lax.all_gather(attend_second, "dp", axis=1, tiled=True))
    small = jnp.stack(ordered(small, exchange(small, "section", 1))).reshape(-1)
    small = gather_small(small, "dp").astype(F32)
    small = small.reshape(dp_size, 2, -1)
    units_here = unit_scales.shape[2]

    def units_apart(values):
        parts = values.reshape(dp_size, 2, -1)
        own, other = ordered(parts[:, 0], parts[:, 1])
        return jnp.concatenate([own.reshape(-1), other.reshape(-1)])

    def units_back(values):
        parts = values.reshape(2, dp_size, -1)
        own, other = ordered(parts[0], parts[1])
        return jnp.stack([own, other], axis=1).reshape(-1)

    layers, feed_owns = [], []
    for layer in range(2):
        feed_own = lax.all_gather(feed_pieces[layer], "dp", axis=1, tiled=True)
        units = small[:, layer, :units_here].reshape(-1)
        mixing = small[:, layer, units_here:].reshape(dp_size, 2, -1)
        mixing = jnp.swapaxes(mixing, 0, 1).reshape(2, -1)
        width_qk, width_ff = attend_owns[0].shape[1], 2 * feed_own.shape[1]
        layers.append((
            units[:width_qk, None],
            jnp.stack([
                units_apart(units[width_qk : width_qk + width_ff]),
                units_apart(units[width_qk + width_ff :]),
            ]),
            mixing,
        ))
        feed_owns.append(feed_own)

    doc_row = lax.dynamic_index_in_dim(doc_ids, section, 0, False)
    starts_all = document_starts(doc_row)
    mp_index = lax.axis_index("mp")
    sources = [mp_index ^ offset for offset in range(4)]
    places = jnp.arange(local_rows, dtype=jnp.int32)
    starts = jnp.stack([
        lax.dynamic_slice_in_dim(starts_all, source * local_rows, local_rows, 0)
        for source in sources
    ])
    sources = jnp.stack(sources).astype(jnp.int32)
    cosine, sine = rope_tables(sources[:, None] * local_rows + places - starts)
    info = jnp.concatenate([sources, starts[:, 0]])
    tables = (cosine, sine, starts, info)

    def scatter(sums):
        return lax.psum_scatter(sums, "dp", scatter_dimension=1, tiled=True)

    def scatter_direct(sums):
        if dp_size != 4:
            return scatter(sums)
        count = sums.shape[1] // dp_size
        parts = [
            lax.dynamic_slice_in_dim(sums, (dp_index ^ bits) * count, count, 1)
            for bits in range(dp_size)
        ]
        parts[1:] = [exchange(part, "dp", bits) for bits, part in enumerate(parts[1:], 1)]
        return sum(part.astype(F32) for part in parts).astype(BF16)

    def small_vector(scales, rate_one, rate_two):
        return jnp.concatenate([units_back(scales[0]), units_back(scales[1]), rate_one, rate_two])

    def attend_params(own, other):
        attend = jnp.concatenate(ordered(own, other), axis=2)
        return attend[:3].reshape(-1, attend.shape[2]), attend[3]

    first, second = layers
    own = attend_owns[0]
    first = (*attend_params(own, exchange(own, "section", 1)), *first)
    section_ref = section.astype(jnp.int32).reshape(1)
    grad = lax.dynamic_index_in_dim(cotangent, section, 0, False)
    _, hidden_second, stored_first, weights_first, later = layer_forward(
        hidden_low, hidden_low, first, tables, False, feed_owns[0], attend_owns[1]
    )
    second = (*attend_params(*later), *second)
    result, _, stored_second, weights_second, _ = layer_forward(
        hidden_second, hidden_second, second, tables, True, feed_owns[1]
    )
    parts, feed_second, attend_second, gains_second, small_second = layer_backward(
        stored_second, (grad,), False, second, tables, weights_second, section_ref
    )
    feed_second = scatter(feed_second)
    parts, attend_second = tie(parts, attend_second)
    attend_second = scatter(attend_second)

    def start_small(small_first):
        values = jnp.concatenate(
            [small_vector(*small_first), small_vector(*small_second), gains_second]
        )
        return values, exchange(values, "section", 1)

    def next_small(low, small, gains):
        low, (values, coming) = tie(low, small)
        values = jnp.concatenate([values + coming, gains])
        return low, (values, exchange(values, "dp", 1))

    def last_small(other, small):
        other, (values, coming) = tie(other, small)
        values, bit = values + coming, 2
        while 2 * bit < dp_size:
            values = values + exchange(values, "dp", bit)
            bit *= 2
        return other, (values, exchange(values, "dp", bit))

    parts, feed_first, attend_first, _, small = layer_backward(
        stored_first, parts, True, first, tables, weights_first, section_ref,
        (start_small, next_small, last_small),
    )
    feed_first = scatter(feed_first)
    attend_first, feed_second, attend_second, small = tie(
        attend_first, feed_second, attend_second, small
    )
    attend_first = scatter_direct(attend_first)

    reduced_first = (attend_first, feed_first)
    reduced_second = (attend_second, feed_second)
    squares = sum(
        jnp.sum(jnp.square(part.astype(F32))) for part in (*reduced_first, *reduced_second)
    )
    gradients = []
    for one, two, dim in zip(reduced_first, reduced_second, (2, 1)):
        own, other = jnp.where(is_first, one, two), jnp.where(is_first, two, one)
        other = exchange(other, "section", 1)
        gradients.append(jnp.concatenate(ordered(own, other), axis=dim))

    sums = small[0] + small[1]
    width_qk, width_rates = gains_second.shape[0], 2 * dp_size * mix_rates.shape[2]
    layer_sums = sums[: -2 * width_qk].reshape(2, -1)
    gain_first = sums[-width_qk:]
    gain_sums = jnp.stack([gain_first + exchange(gain_first, "section", 1), sums[-2 * width_qk : -width_qk]])
    scale_sums, rate_sums = layer_sums[:, :-width_rates], layer_sums[:, -width_rates:]
    rate_sums = sum_over(rate_sums, "mp").reshape(2, 2, -1)
    unit_grads = jnp.concatenate([gain_sums, scale_sums], axis=1)
    unit_grads = jnp.where(is_first, unit_grads[0], unit_grads[1])
    unit_grads = lax.dynamic_slice_in_dim(unit_grads, dp_index * units_here, units_here, 0)
    unit_grads = unit_grads[None, None]
    rates_here = mix_rates.shape[2]
    rate_grads = jnp.where(is_first, rate_sums[0], rate_sums[1])
    rate_grads = lax.dynamic_slice_in_dim(rate_grads, dp_index * rates_here, rates_here, 1)[None]

    turn = lambda array: jnp.swapaxes(array, 1, 2)
    attend_grad, feed_grad = gradients
    feed_in_grad = turn(feed_grad[:2])
    squares, attend_grad, feed_grad, feed_in_grad = tie(
        squares, attend_grad, feed_grad, feed_in_grad
    )
    leading = (mp_index == 0).astype(F32)
    squares = squares + jnp.sum(unit_grads * unit_grads)
    squares = squares + leading * jnp.sum(rate_grads * rate_grads)
    squares = squares.reshape(1)
    squares, parts = tie(squares, parts)
    squares = squares + exchange(squares, "section", 1)
    squares = sum_over(sum_over(squares, "mp"), "dp")
    gradient_norm = jnp.sqrt(squares[0])
    factor = CLIP_NORM / jnp.maximum(gradient_norm, CLIP_NORM)

    grad = sum(part.astype(F32) for part in parts)
    to_send = jnp.where(is_first, result, grad)
    kept = jnp.where(is_first, grad, result)
    arrived = exchange(to_send, "section", 1)
    boundary_states = jnp.stack(ordered(kept, arrived))[None]

    scalar = factor.reshape(1)
    head_rows, width = attention_out.shape[1:]
    feed_units = feedforward_out.shape[1]
    rows, columns = min(32, head_rows), min(128, feed_units)
    updates = []
    new = adam_matrix(
        scalar, turn(attention_in[0]), turn(first_attention_in[0]), turn(second_attention_in[0]),
        attend_grad[:3], 2, (1, rows, width), lambda i, j: (i, j, 0), (3, head_rows // rows),
    )
    updates.extend(turn(part)[None] for part in new)
    updates.extend(adam_matrix(
        scalar, attention_out, first_attention_out, second_attention_out, attend_grad[3:],
        2, (1, rows, width), lambda i: (0, i, 0), (head_rows // rows,),
    ))
    new = adam_matrix(
        scalar, feedforward_in[0], first_feedforward_in[0], second_feedforward_in[0],
        feed_in_grad, 1, (1, width, columns), lambda i, j: (i, 0, j), (2, feed_units // columns),
    )
    updates.extend(part[None] for part in new)
    rows = min(64, feed_units)
    updates.extend(adam_matrix(
        scalar, feedforward_out, first_feedforward_out, second_feedforward_out, feed_grad[2:],
        2, (1, rows, width), lambda i: (0, i, 0), (feed_units // rows,),
    ))
    updates.extend(
        adam_update(
            unit_scales, first_unit_scales, second_unit_scales, unit_grads, factor, SCALE_RATE
        )
    )
    updates.extend(
        adam_update(
            mix_rates, first_mix_rates, second_mix_rates, rate_grads, factor, MIXING_RATE
        )
    )
    return (boundary_states, gradient_norm, *updates)


def solution(mesh):
    in_specs = (
        P("dp", "mp", None),
        P("dp", "mp", None),
        P("dp", None),
        P("section", None, None, ("mp", "dp")),
        P("section", ("mp", "dp"), None),
        P("section", None, None, ("mp", "dp")),
        P("section", ("mp", "dp"), None),
        P("section", "mp", "dp"),
        P("section", None, "dp"),
        P("section", None, None, ("mp", "dp")),
        P("section", None, None, ("mp", "dp")),
        P("section", ("mp", "dp"), None),
        P("section", ("mp", "dp"), None),
        P("section", None, None, ("mp", "dp")),
        P("section", None, None, ("mp", "dp")),
        P("section", ("mp", "dp"), None),
        P("section", ("mp", "dp"), None),
        P("section", "mp", "dp"),
        P("section", "mp", "dp"),
        P("section", None, "dp"),
        P("section", None, "dp"),
    )
    out_specs = (
        P("section", "dp", "mp", None),
        P(),
        P("section", None, None, ("mp", "dp")),
        P("section", None, None, ("mp", "dp")),
        P("section", None, None, ("mp", "dp")),
        P("section", ("mp", "dp"), None),
        P("section", ("mp", "dp"), None),
        P("section", ("mp", "dp"), None),
        P("section", None, None, ("mp", "dp")),
        P("section", None, None, ("mp", "dp")),
        P("section", None, None, ("mp", "dp")),
        P("section", ("mp", "dp"), None),
        P("section", ("mp", "dp"), None),
        P("section", ("mp", "dp"), None),
        P("section", "mp", "dp"),
        P("section", "mp", "dp"),
        P("section", "mp", "dp"),
        P("section", None, "dp"),
        P("section", None, "dp"),
        P("section", None, "dp"),
    )
    return jax.shard_map(
        per_device, mesh=mesh, in_specs=in_specs, out_specs=out_specs, check_vma=False
    )
```

profile of v0, /device:TPU:0, one launch (start us, length us, event | category | flops | bytes accessed | tf_op | source)
XLA Modules:
  0.0 669.7 jit_solution(10103803313956677308)
XLA Ops:
  23.2 8.5 %collective-permute-done.5 = bf16[4,64,512]{2,1,0:T(8,128)(2,1)} collective-permute-done((bf16[4,64,512]{2,1,0:T(8,128)(2,1)S(1)}, bf16[4,64,512]{2,1,0:T(8,128)(2,1)}, u32[]{:S(2)}, u32[]{:S(2)}) %collective-permute-start.5) | collective-permute-done | bytes 262176 | tf_op jit(solution)/shard_map/ppermute | solution.py:51
  52.9 15.2 %collective-permute-done.7 = bf16[4,64,512]{2,1,0:T(8,128)(2,1)S(1)} collective-permute-done((bf16[4,64,512]{2,1,0:T(8,128)(2,1)}, bf16[4,64,512]{2,1,0:T(8,128)(2,1)S(1)}, u32[]{:S(2)}, u32[]{:S(2)}) %collective-permute-start.7) | collective-permute-done | bytes 262176 | tf_op jit(solution)/shard_map/ppermute | solution.py:51
  105.8 10.9 %collective-permute-done.14.refs_3_ = bf16[256,1024]{1,0:T(8,128)(2,1)S(1)} collective-permute-done((bf16[256,1024]{1,0:T(8,128)(2,1)S(1)}, bf16[256,1024]{1,0:T(8,128)(2,1)S(1)}, u32[]{:S(2)}, u32[]{:S(2)}) %collective-permute-start.14) | collective-permute-done | bytes 524320 | tf_op jit(solution)/shard_map/ppermute | solution.py:30
  139.8 7.6 %shard_map.362 = (bf16[256,1024]{1,0:T(8,128)(2,1)}, bf16[256,1024]{1,0:T(8,128)(2,1)}, bf16[1024,256]{1,0:T(8,128)(2,1)}, bf16[256,1024]{1,0:T(8,128)(2,1)}, bf...) custom-call(bf16[256,1024]{1,0:T(8,128)(2,1)S(1)} %collective-permut, ...), custom_call_target="tpu_custom_call" | custom-call | flops 3221225472 | bytes 6291456 | tf_op jit(solution)/shard_map/pallas_call | solution.py:138
  162.4 9.5 %collective-permute-done.22.refs_2_ = bf16[256,1024]{1,0:T(8,128)(2,1)S(1)} collective-permute-done((bf16[256,1024]{1,0:T(8,128)(2,1)S(1)}, bf16[256,1024]{1,0:T(8,128)(2,1)S(1)}, u32[]{:S(2)}, u32[]{:S(2)}) %collective-permute-start.22) | collective-permute-done | bytes 524320 | tf_op jit(solution)/shard_map/ppermute | solution.py:30
  224.2 9.7 %collective-permute-done.31.refs_3_ = bf16[256,1024]{1,0:T(8,128)(2,1)S(1)} collective-permute-done((bf16[256,1024]{1,0:T(8,128)(2,1)S(1)}, bf16[256,1024]{1,0:T(8,128)(2,1)S(1)}, u32[]{:S(2)}, u32[]{:S(2)}) %collective-permute-start.31) | collective-permute-done | bytes 524320 | tf_op jit(solution)/shard_map/ppermute | solution.py:30
  255.8 7.6 %shard_map.373 = (bf16[256,1024]{1,0:T(8,128)(2,1)}, bf16[256,1024]{1,0:T(8,128)(2,1)}, bf16[1024,256]{1,0:T(8,128)(2,1)}, bf16[256,1024]{1,0:T(8,128)(2,1)}, bf...) custom-call(bf16[256,1024]{1,0:T(8,128)(2,1)S(1)} %collective-permut, ...), custom_call_target="tpu_custom_call" | custom-call | flops 3221225472 | bytes 6291456 | tf_op jit(solution)/shard_map/pallas_call | solution.py:138
  278.3 9.4 %collective-permute-done.38.refs_2_ = bf16[256,1024]{1,0:T(8,128)(2,1)S(1)} collective-permute-done((bf16[256,1024]{1,0:T(8,128)(2,1)S(1)}, bf16[256,1024]{1,0:T(8,128)(2,1)S(1)}, u32[]{:S(2)}, u32[]{:S(2)}) %collective-permute-start.38) | collective-permute-done | bytes 524320 | tf_op jit(solution)/shard_map/ppermute | solution.py:30
  297.7 7.3 %shard_map.377 = (bf16[1024,256]{1,0:T(8,128)(2,1)}, bf16[1024,256]{1,0:T(8,128)(2,1)}, f32[2,1024]{1,0:T(2,128)}, f32[256,1024]{1,0:T(8,128)}) custom-call(bf16[256,1024]{1,0:T(8,128)(2,1)S(1)} %copy-done.6, bf16[3,512,1024]{2,1,0:T(8,128)(2,1)} %all-gather.8.cloned.1.call-done.refs_1_.refs_2_, ...), custom_call_target="tpu_custom_call" | custom-call | flops 1610612736 | bytes 6291456 | tf_op jit(solution)/shard_map/pallas_call | solution.py:138
  309.7 9.8 %shard_map.378 = (bf16[1024,256]{1,0:T(8,128)(2,1)}, bf16[1024,256]{1,0:T(8,128)(2,1)}, bf16[1024,256]{1,0:T(8,128)(2,1)}, bf16[1024,256]{1,0:T(8,128)(2,1)}, f3...) custom-call(bf16[256,1024]{1,0:T(8,128)(2,1)S(1)} %collective-permute-done.40.refs_0_.refs_6_, ...), custom_call_target="tpu_custom_call" | custom-call | flops 3221225472 | bytes 6291456 | tf_op jit(solution)/shard_map/pallas_call | solution.py:138
  329.7 7.6 %shard_map.380 = bf16[3,512,1024]{2,1,0:T(8,128)(2,1)} custom-call(bf16[256,1024]{1,0:T(8,128)(2,1)} %get-tuple-element.548.refs_0_, bf16[256,1024]{1,0:T(8,128)(2,1)} %copy-done.12, bf16[256,1024]{1,0:T(8,128)(2,1)} %copy-done.13, bf16[128,1024]{1,0:T(8,128)(2,1)} %copy-done.16, bf16[128,1024]{1,0:T(8,128)(2,1)} %copy-done.17, ...), custom_call_target="tpu_custom_call" | custom-call | flops 3221225472 | bytes 9437184 | tf_op jit(solution)/shard_map/pallas_call | solution.py:138
  349.5 8.6 %shard_map.382 = bf16[3,512,1024]{2,1,0:T(8,128)(2,1)} custom-call(bf16[256,1024]{1,0:T(8,128)(2,1)} %get-tuple-element.548.refs_0_, bf16[256,1024]{1,0:T(8,128)(2,1)} %copy-done.12, bf16[256,1024]{1,0:T(8,128)(2,1)} %copy-done.13, bf16[128,1024]{1,0:T(8,128)(2,1)} %copy-done.16, bf16[128,1024]{1,0:T(8,128)(2,1)} %copy-done.17, ...), custom_call_target="tpu_custom_call" | custom-call | flops 3221225472 | bytes 9437184 | tf_op jit(solution)/shard_map/pallas_call | solution.py:138
  369.6 17.7 %shard_map.383 = (bf16[768,256]{1,0:T(8,128)(2,1)}, bf16[768,256]{1,0:T(8,128)(2,1)}, bf16[768,256]{1,0:T(8,128)(2,1)}, bf16[768,256]{1,0:T(8,128)(2,1)}, f32[25...) custom-call(s32[8]{0:T(128)S(1)} %concatenate.77.info, ...), custom_call_target="tpu_custom_call" | custom-call | flops 10200547328 | bytes 6291456 | tf_op jit(solution)/shard_map/pallas_call | solution.py:138
  387.3 6.9 %shard_map.384 = (f32[1024,512]{1,0:T(8,128)}, bf16[1024,512]{1,0:T(8,128)(2,1)}) custom-call(s32[1]{0:T(128)} %bitcast.section, bf16[768,256]{1,0:T(8,128)(2,1)} %get-tuple-element.592.refs_0_, bf16[768,256]{1,0:T(8,128)(2,1)} %get-tuple-element.593.refs_1_, bf16[768,256]{1,0:T(8,128)(2,1)} %get-tuple-element.594.refs_2_, ...), custom_call_target="tpu_custom_call" | custom-call | flops 2147483648 | bytes 8388608 | tf_op jit(solution)/shard_map/pallas_call | solution.py:138
  400.6 9.3 %collective-permute-done.52.refs_2_ = bf16[256,1024]{1,0:T(8,128)(2,1)S(1)} collective-permute-done((bf16[256,1024]{1,0:T(8,128)(2,1)S(1)}, bf16[256,1024]{1,0:T(8,128)(2,1)S(1)}, u32[]{:S(2)}, u32[]{:S(2)}) %collective-permute-start.52) | collective-permute-done | bytes 524320 | tf_op jit(solution)/shard_map/ppermute | solution.py:30
  409.9 10.3 %collective-permute-done.53.refs_3_ = bf16[256,1024]{1,0:T(8,128)(2,1)S(1)} collective-permute-done((bf16[256,1024]{1,0:T(8,128)(2,1)S(1)}, bf16[256,1024]{1,0:T(8,128)(2,1)S(1)}, u32[]{:S(2)}, u32[]{:S(2)}) %collective-permute-start.53) | collective-permute-done | bytes 524320 | tf_op jit(solution)/shard_map/ppermute | solution.py:30
  443.0 9.9 %shard_map.387 = (bf16[1024,256]{1,0:T(8,128)(2,1)}, bf16[1024,256]{1,0:T(8,128)(2,1)}, bf16[1024,256]{1,0:T(8,128)(2,1)}, bf16[1024,256]{1,0:T(8,128)(2,1)}, f3...) custom-call(bf16[256,1024]{1,0:T(8,128)(2,1)S(1)} %collective-permute-done.56.refs_0_.refs_6_, ...), custom_call_target="tpu_custom_call" | custom-call | flops 3221225472 | bytes 6291456 | tf_op jit(solution)/shard_map/pallas_call | solution.py:138
  463.4 7.6 %shard_map.389 = bf16[3,512,1024]{2,1,0:T(8,128)(2,1)} custom-call(bf16[256,1024]{1,0:T(8,128)(2,1)} %get-tuple-element.638.refs_0_, bf16[256,1024]{1,0:T(8,128)(2,1)} %copy-done.10, bf16[256,1024]{1,0:T(8,128)(2,1)} %copy-done.11, bf16[128,1024]{1,0:T(8,128)(2,1)} %copy-done.14, bf16[128,1024]{1,0:T(8,128)(2,1)} %copy-done.15, ...), custom_call_target="tpu_custom_call" | custom-call | flops 3221225472 | bytes 9437184 | tf_op jit(solution)/shard_map/pallas_call | solution.py:138
  484.1 8.6 %shard_map.391 = bf16[3,512,1024]{2,1,0:T(8,128)(2,1)} custom-call(bf16[256,1024]{1,0:T(8,128)(2,1)} %get-tuple-element.638.refs_0_, bf16[256,1024]{1,0:T(8,128)(2,1)} %copy-done.10, bf16[256,1024]{1,0:T(8,128)(2,1)} %copy-done.11, bf16[128,1024]{1,0:T(8,128)(2,1)} %copy-done.14, bf16[128,1024]{1,0:T(8,128)(2,1)} %copy-done.15, ...), custom_call_target="tpu_custom_call" | custom-call | flops 3221225472 | bytes 9437184 | tf_op jit(solution)/shard_map/pallas_call | solution.py:138
  500.7 11.4 %collective-permute-done.63.refs_25_.refs_14_ = bf16[256,1024]{1,0:T(8,128)(2,1)S(1)} collective-permute-done((bf16[256,1024]{1,0:T(8,128)(2,1)}, bf16[256,1024]{1,0:T(8,128)(2,1)S(1)}, u32[]{:S(2)}, u32[]{:S(2)}) %collective-permute-start.63) | collective-permute-done | bytes 524320 | tf_op jit(solution)/shard_map/ppermute | solution.py:30
  522.2 17.7 %shard_map.392 = (bf16[768,256]{1,0:T(8,128)(2,1)}, bf16[768,256]{1,0:T(8,128)(2,1)}, bf16[768,256]{1,0:T(8,128)(2,1)}, bf16[768,256]{1,0:T(8,128)(2,1)}, f32[25...) custom-call(s32[8]{0:T(128)S(1)} %concatenate.77.info, ...), custom_call_target="tpu_custom_call" | custom-call | flops 10200547328 | bytes 6291456 | tf_op jit(solution)/shard_map/pallas_call | solution.py:138
  542.0 7.2 %shard_map.393 = (f32[1024,512]{1,0:T(8,128)}, bf16[1024,512]{1,0:T(8,128)(2,1)}) custom-call(s32[1]{0:T(128)} %bitcast.section, bf16[768,256]{1,0:T(8,128)(2,1)} %get-tuple-element.680.refs_0_, bf16[768,256]{1,0:T(8,128)(2,1)} %get-tuple-element.681.refs_1_, bf16[768,256]{1,0:T(8,128)(2,1)} %get-tuple-element.682.refs_2_, ...), custom_call_target="tpu_custom_call" | custom-call | flops 2147483648 | bytes 8388608 | tf_op jit(solution)/shard_map/pallas_call | solution.py:138
  565.8 9.6 %collective-permute-done.78 = f32[2,2048]{1,0:T(2,128)S(1)} collective-permute-done((f32[2,2048]{1,0:T(2,128)S(1)}, f32[2,2048]{1,0:T(2,128)S(1)}, u32[]{:S(2)}, u32[]{:S(2)}) %collective-permute-start.78) | collective-permute-done | bytes 16416 | tf_op jit(solution)/shard_map/ppermute | solution.py:30
  624.7 7.4 %collective-permute-start.87 = (f32[1]{0:T(128)}, f32[1]{0:T(128)}, u32[]{:S(2)}, u32[]{:S(2)}) collective-permute-start(f32[1]{0:T(128)} %add.277), channel_id=1, source_target_pairs={{0,4},{4,0},{8,12},{12,8},{1,5},{5,1},{9,13},{13,9},{2,6},{6,2},{1... | collective-permute-start | bytes 20 | tf_op jit(solution)/shard_map/ppermute | solution.py:30
  (482 shorter events, 410.0 us)
Async XLA Ops:
  7.2 109.4 %all-gather.4.cloned.1.call-start = ((), (), s32[]{:S(2)}) async-start(), calls=%async_computation.3 | async-start | bytes 3932160 | tf_op jit(solution)/shard_map/all_gather | solution.py:907
  8.5 61.2 %collective-permute-start.1 = (bf16[256,1024]{1,0:T(8,128)(2,1)S(1)}, bf16[256,1024]{1,0:T(8,128)(2,1)S(1)}, u32[]{:S(2)}, u32[]{:S(2)}) collective-permute-start(bf16[256,1024]{1,0:T(8,128)(2,1)S(1)} %dynamic-slice_bitcast_fusion.1.refs_0_.hidden.refs_8_), channel_id=1, source_target_pairs={{0,2},{1,3},{2,0},{3,1},{4,6},{5,7},{6,4},{7,5},{8,10},{9,11},{10,... | collective-permute-start | bytes 1572872 | tf_op jit(solution)/shard_map/ppermute | solution.py:30
  11.5 59.0 %collective-permute-start = (bf16[256,1024]{1,0:T(8,128)(2,1)S(1)}, bf16[256,1024]{1,0:T(8,128)(2,1)S(1)}, u32[]{:S(2)}, u32[]{:S(2)}) collective-permute-start(bf16[256,1024]{1,0:T(8,128)(2,1)S(1)} %dynamic-slice_bitcast_fusion.1.refs_0_.hidden.refs_8_), channel_id=1, source_target_pairs={{0,1},{1,0},{2,3},{3,2},{4,5},{5,4},{6,7},{7,6},{8,9},{9,8},{10,11... | collective-permute-start | bytes 1572872 | tf_op jit(solution)/shard_map/ppermute | solution.py:30
  14.5 28.0 %collective-permute-start.9 = (bf16[1088]{0:T(1024)(128)(2,1)S(1)}, bf16[1088]{0:T(1024)(128)(2,1)S(1)}, u32[]{:S(2)}, u32[]{:S(2)}) collective-permute-start(bf16[1088]{0:T(1024)(128)(2,1)S(1)} %pad_maximum_fusion.11), channel_id=1, source_target_pairs={{0,16},{16,0},{1,17},{17,1},{2,18},{18,2},{3,19},{19,3},{4,20},{20... | collective-permute-start | bytes 6536 | tf_op jit(solution)/shard_map/ppermute | solution.py:30
  40.7 134.5 %all-gather.6.cloned.1.call-start = ((), (), s32[]{:S(2)}) async-start(), calls=%async_computation.4 | async-start | bytes 1310720 | tf_op jit(solution)/shard_map/all_gather | solution.py:889
  46.4 22.0 %collective-permute-start.11 = (bf16[2,2176]{1,0:T(2,128)(2,1)S(1)}, bf16[2,2176]{1,0:T(2,128)(2,1)S(1)}, u32[]{:S(2)}, u32[]{:S(2)}) collective-permute-start(bf16[2,2176]{1,0:T(2,128)(2,1)S(1)} %pad_maximum_fusion.7), channel_id=1, source_target_pairs={{0,8},{4,12},{8,0},{12,4},{1,9},{5,13},{9,1},{13,5},{2,10},{6,14},... | collective-permute-start | bytes 26120 | tf_op jit(solution)/shard_map/ppermute | solution.py:30
  48.8 19.3 %collective-permute-start.7 = (bf16[4,64,512]{2,1,0:T(8,128)(2,1)}, bf16[4,64,512]{2,1,0:T(8,128)(2,1)S(1)}, u32[]{:S(2)}, u32[]{:S(2)}) collective-permute-start(bf16[4,64,512]{2,1,0:T(8,128)(2,1)} %collective-permute-done.6), channel_id=1, source_target_pairs={{0,4},{16,24},{4,12},{20,16},{12,8},{28,20},{8,0},{24,28},{1,5},{1... | collective-permute-start | bytes 786440 | tf_op jit(solution)/shard_map/ppermute | solution.py:51
  92.4 24.3 %collective-permute-start.14 = (bf16[256,1024]{1,0:T(8,128)(2,1)S(1)}, bf16[256,1024]{1,0:T(8,128)(2,1)S(1)}, u32[]{:S(2)}, u32[]{:S(2)}) collective-permute-start(bf16[256,1024]{1,0:T(8,128)(2,1)S(1)} %get-tuple-element.388), channel_id=1, source_target_pairs={{0,2},{1,3},{2,0},{3,1},{4,6},{5,7},{6,4},{7,5},{8,10},{9,11},{10,... | collective-permute-start | bytes 1572872 | tf_op jit(solution)/shard_map/ppermute | solution.py:30
  116.7 104.1 %all-gather.8.cloned.1.call-start = ((), (), s32[]{:S(2)}) async-start(), calls=%async_computation.5 | async-start | bytes 3932160 | tf_op jit(solution)/shard_map/all_gather | solution.py:907
  117.5 437.5 %reduce-scatter.6.cloned.1.call-start = ((), (), s32[]{:S(2)}) async-start(), calls=%async_computation.7 | async-start | bytes 1310720 | tf_op jit(solution)/shard_map/reduce_scatter | solution.py:937
  147.9 24.0 %collective-permute-start.22 = (bf16[256,1024]{1,0:T(8,128)(2,1)S(1)}, bf16[256,1024]{1,0:T(8,128)(2,1)S(1)}, u32[]{:S(2)}, u32[]{:S(2)}) collective-permute-start(bf16[256,1024]{1,0:T(8,128)(2,1)S(1)} %get-tuple-element.434), channel_id=1, source_target_pairs={{0,2},{1,3},{2,0},{3,1},{4,6},{5,7},{6,4},{7,5},{8,10},{9,11},{10,... | collective-permute-start | bytes 1572872 | tf_op jit(solution)/shard_map/ppermute | solution.py:30
  210.7 23.1 %collective-permute-start.31 = (bf16[256,1024]{1,0:T(8,128)(2,1)S(1)}, bf16[256,1024]{1,0:T(8,128)(2,1)S(1)}, u32[]{:S(2)}, u32[]{:S(2)}) collective-permute-start(bf16[256,1024]{1,0:T(8,128)(2,1)S(1)} %get-tuple-element.478), channel_id=1, source_target_pairs={{0,2},{1,3},{2,0},{3,1},{4,6},{5,7},{6,4},{7,5},{8,10},{9,11},{10,... | collective-permute-start | bytes 1572872 | tf_op jit(solution)/shard_map/ppermute | solution.py:30
  263.8 23.9 %collective-permute-start.38 = (bf16[256,1024]{1,0:T(8,128)(2,1)S(1)}, bf16[256,1024]{1,0:T(8,128)(2,1)S(1)}, u32[]{:S(2)}, u32[]{:S(2)}) collective-permute-start(bf16[256,1024]{1,0:T(8,128)(2,1)S(1)} %get-tuple-element.510), channel_id=1, source_target_pairs={{0,2},{1,3},{2,0},{3,1},{4,6},{5,7},{6,4},{7,5},{8,10},{9,11},{10,... | collective-permute-start | bytes 1572872 | tf_op jit(solution)/shard_map/ppermute | solution.py:30
  320.4 21.0 %collective-permute-start.45 = (bf16[256,1024]{1,0:T(8,128)(2,1)S(1)}, bf16[256,1024]{1,0:T(8,128)(2,1)S(1)}, u32[]{:S(2)}, u32[]{:S(2)}) collective-permute-start(bf16[256,1024]{1,0:T(8,128)(2,1)S(1)} %get-tuple-element.541), channel_id=1, source_target_pairs={{0,2},{1,3},{2,0},{3,1},{4,6},{5,7},{6,4},{7,5},{8,10},{9,11},{10,... | collective-permute-start | bytes 1572872 | tf_op jit(solution)/shard_map/ppermute | solution.py:30
  395.7 24.5 %collective-permute-start.53 = (bf16[256,1024]{1,0:T(8,128)(2,1)S(1)}, bf16[256,1024]{1,0:T(8,128)(2,1)S(1)}, u32[]{:S(2)}, u32[]{:S(2)}) collective-permute-start(bf16[256,1024]{1,0:T(8,128)(2,1)S(1)} %get-tuple-element.590), channel_id=1, source_target_pairs={{0,1},{1,0},{2,3},{3,2},{4,5},{5,4},{6,7},{7,6},{8,9},{9,8},{10,11... | collective-permute-start | bytes 1572872 | tf_op jit(solution)/shard_map/ppermute | solution.py:30
  396.6 24.1 %collective-permute-start.54 = (bf16[256,1024]{1,0:T(8,128)(2,1)S(1)}, bf16[256,1024]{1,0:T(8,128)(2,1)S(1)}, u32[]{:S(2)}, u32[]{:S(2)}) collective-permute-start(bf16[256,1024]{1,0:T(8,128)(2,1)S(1)} %get-tuple-element.591), channel_id=1, source_target_pairs={{0,2},{1,3},{2,0},{3,1},{4,6},{5,7},{6,4},{7,5},{8,10},{9,11},{10,... | collective-permute-start | bytes 1572872 | tf_op jit(solution)/shard_map/ppermute | solution.py:30
  420.7 137.6 %reduce-scatter.4.cloned.1.call-start = ((), (), s32[]{:S(2)}) async-start(), calls=%async_computation.6 | async-start | bytes 3932160 | tf_op jit(solution)/shard_map/reduce_scatter | solution.py:937
  421.3 168.7 %reduce-scatter.8.cloned.1.call-start = ((), (), s32[]{:S(2)}) async-start(), calls=%async_computation.8 | async-start | bytes 3932160 | tf_op jit(solution)/shard_map/reduce_scatter | solution.py:937
  454.1 23.2 %collective-permute-start.61 = (bf16[256,1024]{1,0:T(8,128)(2,1)S(1)}, bf16[256,1024]{1,0:T(8,128)(2,1)S(1)}, u32[]{:S(2)}, u32[]{:S(2)}) collective-permute-start(bf16[256,1024]{1,0:T(8,128)(2,1)S(1)} %get-tuple-element.631), channel_id=1, source_target_pairs={{0,2},{1,3},{2,0},{3,1},{4,6},{5,7},{6,4},{7,5},{8,10},{9,11},{10,... | collective-permute-start | bytes 1572872 | tf_op jit(solution)/shard_map/ppermute | solution.py:30
  514.9 25.0 %collective-permute-start.68 = (f32[8448]{0:T(1024)S(1)}, f32[8448]{0:T(1024)S(1)}, u32[]{:S(2)}, u32[]{:S(2)}) collective-permute-start(f32[8448]{0:T(1024)S(1)} %constant_dynamic-update-slice_fusion.4), channel_id=1, source_target_pairs={{0,16},{16,0},{1,17},{17,1},{2,18},{18,2},{3,19},{19,3},{4,20},{20... | collective-permute-start | bytes 101384 | tf_op jit(solution)/shard_map/ppermute | solution.py:30
  549.2 56.8 %collective-permute-start.80 = (bf16[256,1024]{1,0:T(8,128)(2,1)S(1)}, bf16[256,1024]{1,0:T(8,128)(2,1)}, u32[]{:S(2)}, u32[]{:S(2)}) collective-permute-start(bf16[256,1024]{1,0:T(8,128)(2,1)S(1)} %get-tuple-element.701), channel_id=1, source_target_pairs={{0,3},{1,2},{2,1},{3,0},{4,7},{5,6},{6,5},{7,4},{8,11},{9,10},{10,... | collective-permute-start | bytes 1572872 | tf_op jit(solution)/shard_map/ppermute | solution.py:30
  550.7 55.3 %collective-permute-start.81 = (bf16[256,1024]{1,0:T(8,128)(2,1)S(1)}, bf16[256,1024]{1,0:T(8,128)(2,1)}, u32[]{:S(2)}, u32[]{:S(2)}) collective-permute-start(bf16[256,1024]{1,0:T(8,128)(2,1)S(1)} %get-tuple-element.702), channel_id=1, source_target_pairs={{0,1},{1,0},{2,3},{3,2},{4,5},{5,4},{6,7},{7,6},{8,9},{9,8},{10,11... | collective-permute-start | bytes 1572872 | tf_op jit(solution)/shard_map/ppermute | solution.py:30
  560.7 19.4 %collective-permute-start.72 = (bf16[4,64,512]{2,1,0:T(8,128)(2,1)S(1)}, bf16[4,64,512]{2,1,0:T(8,128)(2,1)S(1)}, u32[]{:S(2)}, u32[]{:S(2)}) collective-permute-start(bf16[4,64,512]{2,1,0:T(8,128)(2,1)S(1)} %get-tuple-element.750), channel_id=1, source_target_pairs={{0,4},{4,0},{8,12},{12,8},{1,5},{5,1},{9,13},{13,9},{2,6},{6,2},{1... | collective-permute-start | bytes 786440 | tf_op jit(solution)/shard_map/ppermute | solution.py:30
  609.5 48.7 %collective-permute-start.83 = (f32[256,1024]{1,0:T(8,128)S(1)}, f32[256,1024]{1,0:T(8,128)}, u32[]{:S(2)}, u32[]{:S(2)}) collective-permute-start(f32[256,1024]{1,0:T(8,128)S(1)} %get-tuple-element.734), channel_id=1, source_target_pairs={{0,16},{16,0},{1,17},{17,1},{2,18},{18,2},{3,19},{19,3},{4,20},{20... | collective-permute-start | bytes 3145736 | tf_op jit(solution)/shard_map/ppermute | solution.py:30
  (130 other events, 1344.1 us)
Sparse Core Ops, SparseCore 0:
  40.8 66.5 all-gather.3
  116.8 25.5 all-gather.5
  144.6 62.9 all-gather.7
  420.8 24.3 reduce-scatter.5
  447.5 58.8 reduce-scatter.3
  508.7 68.9 reduce-scatter.7
where the time goes:
time: 677 us; the launch traced here: 670 us
  Pallas kernels  265 us (39%)
  waiting for transfers between devices  214 us (32%)
  starting transfers between devices  93.6 us (14%)
  other arithmetic  46.6 us (7%)
  local copies, waits for them, and re-layouts  26 us (4%)
  between operations  24.4 us (4%)
    pallas_call x42, Pallas kernels, run(): pl.pallas_call(body, out_shape=[out if at in loose else pltpu.HBM(out.sha...  265 us
    ppermute x86, waiting for transfers between devices, exchange(): return lax.ppermute(block, axis, route)  183 us
    ppermute x86, starting transfers between devices, exchange(): return lax.ppermute(block, axis, route)  89 us
    ppermute x3, waiting for transfers between devices, ring_step(): return lax.ppermute(block, ('section', axis), route)  29.6 us
  transfers between devices with their start and end apart: 95, of which 53 were waited for; matrix products, arithmetic and copies ran while one was open for 8% of the time, Pallas kernels for 35%

commit v1 on v0

--- a/solution.py
+++ b/solution.py
@@ -616,8 +616,9 @@
     )(section, *low, *attended, *hidden, *grads)
 
 
-def adam_kernel(axis, factor, weight, first, second, gradient, first_out, second_out, weight_out):
-    clipped = gradient[...].astype(F32) * factor[0]
+def adam_kernel(axis, gradient_of, section, factor, weight, first, second, *refs):
+    first_out, second_out, weight_out = refs[4:]
+    clipped = gradient_of(section[0] == 0, [ref[...].astype(F32) for ref in refs[:4]]) * factor[0]
     first_new = BETA_FIRST * first[...] + (1.0 - BETA_FIRST) * clipped
     second_new = BETA_SECOND * second[...] + (1.0 - BETA_SECOND) * clipped * clipped
     first_out[...] = first_new
@@ -629,17 +630,41 @@
     weight_out[...] = moved * scale
 
 
-def adam_matrix(factor, weight, first, second, gradient, axis, block, place, grid):
-    spec = pl.BlockSpec(block, place)
+def adam_matrix(section, factor, arrays, halves, axis, gradient_of, block, half_block, place,
+                half_place, grid):
+    spec, half_spec = pl.BlockSpec(block, place), pl.BlockSpec(half_block, half_place)
+    dims, size = arrays[0].shape, arrays[0].size
     return call(
-        functools.partial(adam_kernel, axis),
-        [shape(weight.shape, F32)] * 3,
-        [SCALARS] + [spec] * 4,
-        20 * weight.size,
-        28 * weight.size,
+        functools.partial(adam_kernel, axis, gradient_of),
+        [shape(dims, F32)] * 3,
+        [SCALARS] * 2 + [spec] * 3 + [half_spec] * 4,
+        20 * size,
+        28 * size,
         grid=grid,
         out_specs=[spec] * 3,
-    )(factor, weight, first, second, gradient)
+    )(section, factor, *arrays, *halves)
+
+
+def half_of(is_first, parts, low_half):
+    here, there = jnp.where(is_first, parts[0], parts[1]), jnp.where(is_first, parts[2], parts[3])
+    return jnp.where(is_first == low_half, here, there)
+
+
+def by_columns(is_first, parts):
+    return jnp.concatenate(
+        [half_of(is_first, parts, True), half_of(is_first, parts, False)], axis=2
+    )
+
+
+def by_rows(steps, is_first, parts):
+    return half_of(is_first, parts, pl.program_id(0) < steps)
+
+
+def by_rows_turned(apart, is_first, parts):
+    if apart:
+        return half_of(is_first, parts, pl.program_id(1) == 0)[0].T[None]
+    both = [half_of(is_first, parts, low)[0] for low in (True, False)]
+    return jnp.concatenate(both, axis=0).T[None]
 
 
 def add_parts(parts):
@@ -973,20 +998,23 @@
     parts, attend_second = tie(parts, attend_second)
     attend_second = scatter(attend_second)
 
+    width_qk, width_rates = gains_second.shape[0], 2 * dp_size * mix_rates.shape[2]
+
     def start_small(small_first):
-        values = jnp.concatenate(
-            [small_vector(*small_first), small_vector(*small_second), gains_second]
-        )
-        return values, exchange(values, "section", 1)
+        values = jnp.stack([small_vector(*small_first), small_vector(*small_second)])
+        values = jnp.concatenate([values.reshape(-1), gains_second])
+        values = values + exchange(values, "section", 1)
+        values, gains = values[:-width_qk].reshape(2, -1), values[-width_qk:]
+        rates = sum_over(values[:, -width_rates:], "mp")
+        return jnp.concatenate([values[:, :-width_rates], rates], axis=1), gains
 
     def next_small(low, small, gains):
-        low, (values, coming) = tie(low, small)
-        values = jnp.concatenate([values + coming, gains])
-        return low, (values, exchange(values, "dp", 1))
+        low, (values, gains_two) = tie(low, small)
+        return low, (jnp.concatenate([values.reshape(-1), gains_two, gains]),)
 
     def last_small(other, small):
-        other, (values, coming) = tie(other, small)
-        values, bit = values + coming, 2
+        other, (values,) = tie(other, small)
+        bit = 1
         while 2 * bit < dp_size:
             values = values + exchange(values, "dp", bit)
             bit *= 2
@@ -997,8 +1025,11 @@
         (start_small, next_small, last_small),
     )
     feed_first = scatter(feed_first)
-    attend_first, feed_second, attend_second, small = tie(
-        attend_first, feed_second, attend_second, small
+    sent_second = [
+        lax.ppermute(part, "section", [(0, 1)]) for part in (attend_second, feed_second)
+    ]
+    attend_first, feed_second, attend_second, small, sent_second = tie(
+        attend_first, feed_second, attend_second, small, sent_second
     )
     attend_first = scatter_direct(attend_first)
 
@@ -1007,19 +1038,17 @@
     squares = sum(
         jnp.sum(jnp.square(part.astype(F32))) for part in (*reduced_first, *reduced_second)
     )
-    gradients = []
-    for one, two, dim in zip(reduced_first, reduced_second, (2, 1)):
-        own, other = jnp.where(is_first, one, two), jnp.where(is_first, two, one)
-        other = exchange(other, "section", 1)
-        gradients.append(jnp.concatenate(ordered(own, other), axis=dim))
+    halves_of = [
+        (one, two, lax.ppermute(one, "section", [(1, 0)]), theirs)
+        for one, two, theirs in zip(reduced_first, reduced_second, sent_second)
+    ]
 
     sums = small[0] + small[1]
-    width_qk, width_rates = gains_second.shape[0], 2 * dp_size * mix_rates.shape[2]
     layer_sums = sums[: -2 * width_qk].reshape(2, -1)
     gain_first = sums[-width_qk:]
     gain_sums = jnp.stack([gain_first + exchange(gain_first, "section", 1), sums[-2 * width_qk : -width_qk]])
     scale_sums, rate_sums = layer_sums[:, :-width_rates], layer_sums[:, -width_rates:]
-    rate_sums = sum_over(rate_sums, "mp").reshape(2, 2, -1)
+    rate_sums = rate_sums.reshape(2, 2, -1)
     unit_grads = jnp.concatenate([gain_sums, scale_sums], axis=1)
     unit_grads = jnp.where(is_first, unit_grads[0], unit_grads[1])
     unit_grads = lax.dynamic_slice_in_dim(unit_grads, dp_index * units_here, units_here, 0)
@@ -1029,11 +1058,6 @@
     rate_grads = lax.dynamic_slice_in_dim(rate_grads, dp_index * rates_here, rates_here, 1)[None]
 
     turn = lambda array: jnp.swapaxes(array, 1, 2)
-    attend_grad, feed_grad = gradients
-    feed_in_grad = turn(feed_grad[:2])
-    squares, attend_grad, feed_grad, feed_in_grad = tie(
-        squares, attend_grad, feed_grad, feed_in_grad
-    )
     leading = (mp_index == 0).astype(F32)
     squares = squares + jnp.sum(unit_grads * unit_grads)
     squares = squares + leading * jnp.sum(rate_grads * rate_grads)
@@ -1053,26 +1077,38 @@
     scalar = factor.reshape(1)
     head_rows, width = attention_out.shape[1:]
     feed_units = feedforward_out.shape[1]
-    rows, columns = min(32, head_rows), min(128, feed_units)
+    rows = min(32, head_rows)
     updates = []
-    new = adam_matrix(
-        scalar, turn(attention_in[0]), turn(first_attention_in[0]), turn(second_attention_in[0]),
-        attend_grad[:3], 2, (1, rows, width), lambda i, j: (i, j, 0), (3, head_rows // rows),
+    attend_halves, feed_halves = halves_of
+    unit_half = feed_units // 2
+    apart = unit_half % 128 == 0
+    turned = (
+        (1, width, unit_half if apart else feed_units), (1, unit_half, width),
+        lambda i, j: (i, 0, j), lambda i, j: (i, 0, 0), (2, 2 if apart else 1),
+    )
+    update = functools.partial(adam_matrix, section_ref, scalar)
+    new = update(
+        [turn(array[0]) for array in (attention_in, first_attention_in, second_attention_in)],
+        attend_halves, 2, by_columns, (1, rows, width), (1, rows, width // 2),
+        lambda i, j: (i, j, 0), lambda i, j: (i, j, 0), (3, head_rows // rows),
     )
     updates.extend(turn(part)[None] for part in new)
-    updates.extend(adam_matrix(
-        scalar, attention_out, first_attention_out, second_attention_out, attend_grad[3:],
-        2, (1, rows, width), lambda i: (0, i, 0), (head_rows // rows,),
+    updates.extend(update(
+        (attention_out, first_attention_out, second_attention_out),
+        attend_halves, 2, by_columns, (1, rows, width), (1, rows, width // 2),
+        lambda i: (0, i, 0), lambda i: (3, i, 0), (head_rows // rows,),
     ))
-    new = adam_matrix(
-        scalar, feedforward_in[0], first_feedforward_in[0], second_feedforward_in[0],
-        feed_in_grad, 1, (1, width, columns), lambda i, j: (i, 0, j), (2, feed_units // columns),
+    new = update(
+        [array[0] for array in (feedforward_in, first_feedforward_in, second_feedforward_in)],
+        feed_halves, 1, functools.partial(by_rows_turned, apart), *turned,
     )
     updates.extend(part[None] for part in new)
-    rows = min(64, feed_units)
-    updates.extend(adam_matrix(
-        scalar, feedforward_out, first_feedforward_out, second_feedforward_out, feed_grad[2:],
-        2, (1, rows, width), lambda i: (0, i, 0), (feed_units // rows,),
+    steps = max(1, feed_units // 128)
+    rows = feed_units // 2 // steps
+    updates.extend(update(
+        (feedforward_out, first_feedforward_out, second_feedforward_out),
+        feed_halves, 2, functools.partial(by_rows, steps), (1, rows, width), (1, rows, width),
+        lambda i: (0, i, 0), lambda i: (2, i % steps, 0), (2 * steps,),
     ))
     updates.extend(
         adam_update(

time: 677 us -> 689 us (1.018)
  starting transfers between devices: 93.6 us -> 111 us
    ppermute x86 -> x84, starting transfers between devices: 89 us -> 101 us  [exchange(): return lax.ppermute(block, axis, route)]
    ppermute x86 -> x84, waiting for transfers between devices: 183 us -> 187 us  [exchange(): return lax.ppermute(block, axis, route)]
    unnamed x127 -> x131, local copies, waits for them, and re-layouts: 12 us -> 13.8 us
  transfers between devices with their start and end apart: 95 -> 97, of which waited for: 53 -> 50; matrix products, arithmetic and copies ran while one was open for 8% -> 7% of each run, Pallas kernels for 35% -> 36%
where the time goes in v1:
time: 689 us; the launch traced here: 680 us
  Pallas kernels  261 us (38%)
  waiting for transfers between devices  217 us (31%)
  starting transfers between devices  111 us (16%)
  other arithmetic  43 us (6%)
  local copies, waits for them, and re-layouts  24.1 us (3%)
  between operations  23.9 us (3%)
    pallas_call x42, Pallas kernels, run(): pl.pallas_call(body, out_shape=[out if at in loose else pltpu.HBM(out.sha...  261 us
    ppermute x84, waiting for transfers between devices, exchange(): return lax.ppermute(block, axis, route)  187 us
    ppermute x84, starting transfers between devices, exchange(): return lax.ppermute(block, axis, route)  101 us
    ppermute x3, waiting for transfers between devices, ring_step(): return lax.ppermute(block, ('section', axis), route)  29.6 us
    unnamed x131, local copies, waits for them, and re-layouts  13.8 us
  transfers between devices with their start and end apart: 97, of which 50 were waited for; matrix products, arithmetic and copies ran while one was open for 7% of the time, Pallas kernels for 36%

profile of v1, /device:TPU:0, one launch (start us, length us, event | category | flops | bytes accessed | tf_op | source)
XLA Modules:
  0.0 679.8 jit_solution(17460942130063437625)
XLA Ops:
  23.2 8.5 %collective-permute-done.5 = bf16[4,64,512]{2,1,0:T(8,128)(2,1)} collective-permute-done((bf16[4,64,512]{2,1,0:T(8,128)(2,1)S(1)}, bf16[4,64,512]{2,1,0:T(8,128)(2,1)}, u32[]{:S(2)}, u32[]{:S(2)}) %collective-permute-start.5) | collective-permute-done | bytes 262176 | tf_op jit(solution)/shard_map/ppermute | solution.py:51
  52.9 15.2 %collective-permute-done.7 = bf16[4,64,512]{2,1,0:T(8,128)(2,1)S(1)} collective-permute-done((bf16[4,64,512]{2,1,0:T(8,128)(2,1)}, bf16[4,64,512]{2,1,0:T(8,128)(2,1)S(1)}, u32[]{:S(2)}, u32[]{:S(2)}) %collective-permute-start.7) | collective-permute-done | bytes 262176 | tf_op jit(solution)/shard_map/ppermute | solution.py:51
  104.9 10.7 %collective-permute-done.14.refs_3_ = bf16[256,1024]{1,0:T(8,128)(2,1)S(1)} collective-permute-done((bf16[256,1024]{1,0:T(8,128)(2,1)S(1)}, bf16[256,1024]{1,0:T(8,128)(2,1)S(1)}, u32[]{:S(2)}, u32[]{:S(2)}) %collective-permute-start.14) | collective-permute-done | bytes 524320 | tf_op jit(solution)/shard_map/ppermute | solution.py:30
  137.8 7.6 %shard_map.362 = (bf16[256,1024]{1,0:T(8,128)(2,1)}, bf16[256,1024]{1,0:T(8,128)(2,1)}, bf16[1024,256]{1,0:T(8,128)(2,1)}, bf16[256,1024]{1,0:T(8,128)(2,1)}, bf...) custom-call(bf16[256,1024]{1,0:T(8,128)(2,1)S(1)} %collective-permut, ...), custom_call_target="tpu_custom_call" | custom-call | flops 3221225472 | bytes 6291456 | tf_op jit(solution)/shard_map/pallas_call | solution.py:138
  161.1 9.2 %collective-permute-done.23.refs_3_ = bf16[256,1024]{1,0:T(8,128)(2,1)S(1)} collective-permute-done((bf16[256,1024]{1,0:T(8,128)(2,1)S(1)}, bf16[256,1024]{1,0:T(8,128)(2,1)S(1)}, u32[]{:S(2)}, u32[]{:S(2)}) %collective-permute-start.23) | collective-permute-done | bytes 524320 | tf_op jit(solution)/shard_map/ppermute | solution.py:30
  221.6 9.4 %collective-permute-done.31.refs_3_ = bf16[256,1024]{1,0:T(8,128)(2,1)S(1)} collective-permute-done((bf16[256,1024]{1,0:T(8,128)(2,1)S(1)}, bf16[256,1024]{1,0:T(8,128)(2,1)S(1)}, u32[]{:S(2)}, u32[]{:S(2)}) %collective-permute-start.31) | collective-permute-done | bytes 524320 | tf_op jit(solution)/shard_map/ppermute | solution.py:30
  252.5 7.5 %shard_map.373 = (bf16[256,1024]{1,0:T(8,128)(2,1)}, bf16[256,1024]{1,0:T(8,128)(2,1)}, bf16[1024,256]{1,0:T(8,128)(2,1)}, bf16[256,1024]{1,0:T(8,128)(2,1)}, bf...) custom-call(bf16[256,1024]{1,0:T(8,128)(2,1)S(1)} %collective-permut, ...), custom_call_target="tpu_custom_call" | custom-call | flops 3221225472 | bytes 6291456 | tf_op jit(solution)/shard_map/pallas_call | solution.py:138
  275.0 9.5 %collective-permute-done.38.refs_2_ = bf16[256,1024]{1,0:T(8,128)(2,1)S(1)} collective-permute-done((bf16[256,1024]{1,0:T(8,128)(2,1)S(1)}, bf16[256,1024]{1,0:T(8,128)(2,1)S(1)}, u32[]{:S(2)}, u32[]{:S(2)}) %collective-permute-start.38) | collective-permute-done | bytes 524320 | tf_op jit(solution)/shard_map/ppermute | solution.py:30
  294.4 7.3 %shard_map.377 = (bf16[1024,256]{1,0:T(8,128)(2,1)}, bf16[1024,256]{1,0:T(8,128)(2,1)}, f32[2,1024]{1,0:T(2,128)}, f32[256,1024]{1,0:T(8,128)}) custom-call(bf16[256,1024]{1,0:T(8,128)(2,1)S(1)} %copy-done.6, bf16[3,512,1024]{2,1,0:T(8,128)(2,1)} %all-gather.8.cloned.1.call-done.refs_1_.refs_2_, ...), custom_call_target="tpu_custom_call" | custom-call | flops 1610612736 | bytes 6291456 | tf_op jit(solution)/shard_map/pallas_call | solution.py:138
  306.4 9.8 %shard_map.378 = (bf16[1024,256]{1,0:T(8,128)(2,1)}, bf16[1024,256]{1,0:T(8,128)(2,1)}, bf16[1024,256]{1,0:T(8,128)(2,1)}, bf16[1024,256]{1,0:T(8,128)(2,1)}, f3...) custom-call(bf16[256,1024]{1,0:T(8,128)(2,1)S(1)} %collective-permute-done.40.refs_0_.refs_6_, ...), custom_call_target="tpu_custom_call" | custom-call | flops 3221225472 | bytes 6291456 | tf_op jit(solution)/shard_map/pallas_call | solution.py:138
  326.4 7.5 %shard_map.380 = bf16[3,512,1024]{2,1,0:T(8,128)(2,1)} custom-call(bf16[256,1024]{1,0:T(8,128)(2,1)} %get-tuple-element.545.refs_0_, bf16[256,1024]{1,0:T(8,128)(2,1)} %copy-done.12, bf16[256,1024]{1,0:T(8,128)(2,1)} %copy-done.13, bf16[128,1024]{1,0:T(8,128)(2,1)} %copy-done.16, bf16[128,1024]{1,0:T(8,128)(2,1)} %copy-done.17, ...), custom_call_target="tpu_custom_call" | custom-call | flops 3221225472 | bytes 9437184 | tf_op jit(solution)/shard_map/pallas_call | solution.py:138
  345.2 8.7 %shard_map.382 = bf16[3,512,1024]{2,1,0:T(8,128)(2,1)} custom-call(bf16[256,1024]{1,0:T(8,128)(2,1)} %get-tuple-element.545.refs_0_, bf16[256,1024]{1,0:T(8,128)(2,1)} %copy-done.12, bf16[256,1024]{1,0:T(8,128)(2,1)} %copy-done.13, bf16[128,1024]{1,0:T(8,128)(2,1)} %copy-done.16, bf16[128,1024]{1,0:T(8,128)(2,1)} %copy-done.17, ...), custom_call_target="tpu_custom_call" | custom-call | flops 3221225472 | bytes 9437184 | tf_op jit(solution)/shard_map/pallas_call | solution.py:138
  360.2 12.1 %collective-permute-done.47.refs_25_.refs_14_ = bf16[256,1024]{1,0:T(8,128)(2,1)S(1)} collective-permute-done((bf16[256,1024]{1,0:T(8,128)(2,1)}, bf16[256,1024]{1,0:T(8,128)(2,1)S(1)}, u32[]{:S(2)}, u32[]{:S(2)}) %collective-permute-start.47) | collective-permute-done | bytes 524320 | tf_op jit(solution)/shard_map/ppermute | solution.py:30
  382.4 15.3 %shard_map.383 = (bf16[768,256]{1,0:T(8,128)(2,1)}, bf16[768,256]{1,0:T(8,128)(2,1)}, bf16[768,256]{1,0:T(8,128)(2,1)}, bf16[768,256]{1,0:T(8,128)(2,1)}, f32[25...) custom-call(s32[8]{0:T(128)S(1)} %concatenate.80.info, ...), custom_call_target="tpu_custom_call" | custom-call | flops 10200547328 | bytes 6291456 | tf_op jit(solution)/shard_map/pallas_call | solution.py:138
  397.8 7.4 %shard_map.384 = (f32[1024,512]{1,0:T(8,128)}, bf16[1024,512]{1,0:T(8,128)(2,1)}) custom-call(s32[1]{0:T(128)} %bitcast.section, bf16[768,256]{1,0:T(8,128)(2,1)} %get-tuple-element.589.refs_0_, bf16[768,256]{1,0:T(8,128)(2,1)} %get-tuple-element.590.refs_1_, bf16[768,256]{1,0:T(8,128)(2,1)} %get-tuple-element.591.refs_2_, ...), custom_call_target="tpu_custom_call" | custom-call | flops 2147483648 | bytes 8388608 | tf_op jit(solution)/shard_map/pallas_call | solution.py:138
  411.5 9.3 %collective-permute-done.52.refs_2_ = bf16[256,1024]{1,0:T(8,128)(2,1)S(1)} collective-permute-done((bf16[256,1024]{1,0:T(8,128)(2,1)S(1)}, bf16[256,1024]{1,0:T(8,128)(2,1)S(1)}, u32[]{:S(2)}, u32[]{:S(2)}) %collective-permute-start.52) | collective-permute-done | bytes 524320 | tf_op jit(solution)/shard_map/ppermute | solution.py:30
  420.8 10.6 %collective-permute-done.53.refs_3_ = bf16[256,1024]{1,0:T(8,128)(2,1)S(1)} collective-permute-done((bf16[256,1024]{1,0:T(8,128)(2,1)S(1)}, bf16[256,1024]{1,0:T(8,128)(2,1)S(1)}, u32[]{:S(2)}, u32[]{:S(2)}) %collective-permute-start.53) | collective-permute-done | bytes 524320 | tf_op jit(solution)/shard_map/ppermute | solution.py:30
  453.2 9.9 %shard_map.387 = (bf16[1024,256]{1,0:T(8,128)(2,1)}, bf16[1024,256]{1,0:T(8,128)(2,1)}, bf16[1024,256]{1,0:T(8,128)(2,1)}, bf16[1024,256]{1,0:T(8,128)(2,1)}, f3...) custom-call(bf16[256,1024]{1,0:T(8,128)(2,1)S(1)} %collective-permute-done.56.refs_0_.refs_6_, ...), custom_call_target="tpu_custom_call" | custom-call | flops 3221225472 | bytes 6291456 | tf_op jit(solution)/shard_map/pallas_call | solution.py:138
  473.6 7.6 %shard_map.389 = bf16[3,512,1024]{2,1,0:T(8,128)(2,1)} custom-call(bf16[256,1024]{1,0:T(8,128)(2,1)} %get-tuple-element.635.refs_0_, bf16[256,1024]{1,0:T(8,128)(2,1)} %copy-done.10, bf16[256,1024]{1,0:T(8,128)(2,1)} %copy-done.11, bf16[128,1024]{1,0:T(8,128)(2,1)} %copy-done.14, bf16[128,1024]{1,0:T(8,128)(2,1)} %copy-done.15, ...), custom_call_target="tpu_custom_call" | custom-call | flops 3221225472 | bytes 9437184 | tf_op jit(solution)/shard_map/pallas_call | solution.py:138
  494.8 8.8 %shard_map.391 = bf16[3,512,1024]{2,1,0:T(8,128)(2,1)} custom-call(bf16[256,1024]{1,0:T(8,128)(2,1)} %get-tuple-element.635.refs_0_, bf16[256,1024]{1,0:T(8,128)(2,1)} %copy-done.10, bf16[256,1024]{1,0:T(8,128)(2,1)} %copy-done.11, bf16[128,1024]{1,0:T(8,128)(2,1)} %copy-done.14, bf16[128,1024]{1,0:T(8,128)(2,1)} %copy-done.15, ...), custom_call_target="tpu_custom_call" | custom-call | flops 3221225472 | bytes 9437184 | tf_op jit(solution)/shard_map/pallas_call | solution.py:138
  508.4 10.5 %collective-permute-done.69 = f32[2,2048]{1,0:T(2,128)S(1)} collective-permute-done((f32[2,2048]{1,0:T(2,128)S(1)}, f32[2,2048]{1,0:T(2,128)S(1)}, u32[]{:S(2)}, u32[]{:S(2)}) %collective-permute-start.69) | collective-permute-done | bytes 16416 | tf_op jit(solution)/shard_map/ppermute | solution.py:30
  530.5 17.7 %shard_map.392 = (bf16[768,256]{1,0:T(8,128)(2,1)}, bf16[768,256]{1,0:T(8,128)(2,1)}, bf16[768,256]{1,0:T(8,128)(2,1)}, bf16[768,256]{1,0:T(8,128)(2,1)}, f32[25...) custom-call(s32[8]{0:T(128)S(1)} %concatenate.80.info, ...), custom_call_target="tpu_custom_call" | custom-call | flops 10200547328 | bytes 6291456 | tf_op jit(solution)/shard_map/pallas_call | solution.py:138
  598.8 8.1 %collective-permute-done.77 = bf16[4,64,512]{2,1,0:T(8,128)(2,1)S(1)} collective-permute-done((bf16[4,64,512]{2,1,0:T(8,128)(2,1)}, bf16[4,64,512]{2,1,0:T(8,128)(2,1)S(1)}, u32[]{:S(2)}, u32[]{:S(2)}) %collective-permute-start.77) | collective-permute-done | bytes 262176 | tf_op jit(solution)/shard_map/ppermute | solution.py:30
  660.8 7.5 %shard_map.396 = (f32[2,1024,256]{2,1,0:T(8,128)}, f32[2,1024,256]{2,1,0:T(8,128)}, f32[2,1024,256]{2,1,0:T(8,128)}) custom-call(s32[1]{0:T(128)} %bitcast.section, f32[1]{0:T(128)} %bitcast.76.factor, f32[2,1024,256]{2,1,0:T(8,128)} %bitcast.152, f32[2,1024,256]{2,1,0:T(8,128)} %bitcast.157, f32[2,1024,256]{2,1,0:T(8,128)} %bitcast.158, ...), custom_call_target="tpu_custom_call" | custom-call | flops 10485760 | bytes 14680064 | tf_op jit(solution)/shard_map/pallas_call | solution.py:138
  (488 shorter events, 420.2 us)
Async XLA Ops:
  7.2 108.4 %all-gather.4.cloned.1.call-start = ((), (), s32[]{:S(2)}) async-start(), calls=%async_computation.3 | async-start | bytes 3932160 | tf_op jit(solution)/shard_map/all_gather | solution.py:932
  8.5 61.2 %collective-permute-start.1 = (bf16[256,1024]{1,0:T(8,128)(2,1)S(1)}, bf16[256,1024]{1,0:T(8,128)(2,1)S(1)}, u32[]{:S(2)}, u32[]{:S(2)}) collective-permute-start(bf16[256,1024]{1,0:T(8,128)(2,1)S(1)} %dynamic-slice_bitcast_fusion.1.refs_0_.hidden.refs_8_), channel_id=1, source_target_pairs={{0,2},{1,3},{2,0},{3,1},{4,6},{5,7},{6,4},{7,5},{8,10},{9,11},{10,... | collective-permute-start | bytes 1572872 | tf_op jit(solution)/shard_map/ppermute | solution.py:30
  11.5 59.0 %collective-permute-start = (bf16[256,1024]{1,0:T(8,128)(2,1)S(1)}, bf16[256,1024]{1,0:T(8,128)(2,1)S(1)}, u32[]{:S(2)}, u32[]{:S(2)}) collective-permute-start(bf16[256,1024]{1,0:T(8,128)(2,1)S(1)} %dynamic-slice_bitcast_fusion.1.refs_0_.hidden.refs_8_), channel_id=1, source_target_pairs={{0,1},{1,0},{2,3},{3,2},{4,5},{5,4},{6,7},{7,6},{8,9},{9,8},{10,11... | collective-permute-start | bytes 1572872 | tf_op jit(solution)/shard_map/ppermute | solution.py:30
  14.5 28.0 %collective-permute-start.9 = (bf16[1088]{0:T(1024)(128)(2,1)S(1)}, bf16[1088]{0:T(1024)(128)(2,1)S(1)}, u32[]{:S(2)}, u32[]{:S(2)}) collective-permute-start(bf16[1088]{0:T(1024)(128)(2,1)S(1)} %pad_maximum_fusion.13), channel_id=1, source_target_pairs={{0,16},{16,0},{1,17},{17,1},{2,18},{18,2},{3,19},{19,3},{4,20},{20... | collective-permute-start | bytes 6536 | tf_op jit(solution)/shard_map/ppermute | solution.py:30
  40.7 132.9 %all-gather.6.cloned.1.call-start = ((), (), s32[]{:S(2)}) async-start(), calls=%async_computation.4 | async-start | bytes 1310720 | tf_op jit(solution)/shard_map/all_gather | solution.py:914
  46.4 22.0 %collective-permute-start.11 = (bf16[2,2176]{1,0:T(2,128)(2,1)S(1)}, bf16[2,2176]{1,0:T(2,128)(2,1)S(1)}, u32[]{:S(2)}, u32[]{:S(2)}) collective-permute-start(bf16[2,2176]{1,0:T(2,128)(2,1)S(1)} %pad_maximum_fusion.9), channel_id=1, source_target_pairs={{0,8},{4,12},{8,0},{12,4},{1,9},{5,13},{9,1},{13,5},{2,10},{6,14},... | collective-permute-start | bytes 26120 | tf_op jit(solution)/shard_map/ppermute | solution.py:30
  91.4 24.3 %collective-permute-start.14 = (bf16[256,1024]{1,0:T(8,128)(2,1)S(1)}, bf16[256,1024]{1,0:T(8,128)(2,1)S(1)}, u32[]{:S(2)}, u32[]{:S(2)}) collective-permute-start(bf16[256,1024]{1,0:T(8,128)(2,1)S(1)} %get-tuple-element.385), channel_id=1, source_target_pairs={{0,2},{1,3},{2,0},{3,1},{4,6},{5,7},{6,4},{7,5},{8,10},{9,11},{10,... | collective-permute-start | bytes 1572872 | tf_op jit(solution)/shard_map/ppermute | solution.py:30
  115.7 102.0 %all-gather.8.cloned.1.call-start = ((), (), s32[]{:S(2)}) async-start(), calls=%async_computation.5 | async-start | bytes 3932160 | tf_op jit(solution)/shard_map/all_gather | solution.py:932
  116.4 440.9 %reduce-scatter.4.cloned.1.call-start = ((), (), s32[]{:S(2)}) async-start(), calls=%async_computation.6 | async-start | bytes 3932160 | tf_op jit(solution)/shard_map/reduce_scatter | solution.py:962
  207.8 23.2 %collective-permute-start.31 = (bf16[256,1024]{1,0:T(8,128)(2,1)S(1)}, bf16[256,1024]{1,0:T(8,128)(2,1)S(1)}, u32[]{:S(2)}, u32[]{:S(2)}) collective-permute-start(bf16[256,1024]{1,0:T(8,128)(2,1)S(1)} %get-tuple-element.475), channel_id=1, source_target_pairs={{0,2},{1,3},{2,0},{3,1},{4,6},{5,7},{6,4},{7,5},{8,10},{9,11},{10,... | collective-permute-start | bytes 1572872 | tf_op jit(solution)/shard_map/ppermute | solution.py:30
  260.8 23.6 %collective-permute-start.38 = (bf16[256,1024]{1,0:T(8,128)(2,1)S(1)}, bf16[256,1024]{1,0:T(8,128)(2,1)S(1)}, u32[]{:S(2)}, u32[]{:S(2)}) collective-permute-start(bf16[256,1024]{1,0:T(8,128)(2,1)S(1)} %get-tuple-element.507), channel_id=1, source_target_pairs={{0,2},{1,3},{2,0},{3,1},{4,6},{5,7},{6,4},{7,5},{8,10},{9,11},{10,... | collective-permute-start | bytes 1572872 | tf_op jit(solution)/shard_map/ppermute | solution.py:30
  316.9 20.7 %collective-permute-start.45 = (bf16[256,1024]{1,0:T(8,128)(2,1)S(1)}, bf16[256,1024]{1,0:T(8,128)(2,1)S(1)}, u32[]{:S(2)}, u32[]{:S(2)}) collective-permute-start(bf16[256,1024]{1,0:T(8,128)(2,1)S(1)} %get-tuple-element.538), channel_id=1, source_target_pairs={{0,2},{1,3},{2,0},{3,1},{4,6},{5,7},{6,4},{7,5},{8,10},{9,11},{10,... | collective-permute-start | bytes 1572872 | tf_op jit(solution)/shard_map/ppermute | solution.py:30
  353.9 206.0 %reduce-scatter.6.cloned.1.call-start = ((), (), s32[]{:S(2)}) async-start(), calls=%async_computation.7 | async-start | bytes 1310720 | tf_op jit(solution)/shard_map/reduce_scatter | solution.py:962
  406.6 24.8 %collective-permute-start.53 = (bf16[256,1024]{1,0:T(8,128)(2,1)S(1)}, bf16[256,1024]{1,0:T(8,128)(2,1)S(1)}, u32[]{:S(2)}, u32[]{:S(2)}) collective-permute-start(bf16[256,1024]{1,0:T(8,128)(2,1)S(1)} %get-tuple-element.587), channel_id=1, source_target_pairs={{0,1},{1,0},{2,3},{3,2},{4,5},{5,4},{6,7},{7,6},{8,9},{9,8},{10,11... | collective-permute-start | bytes 1572872 | tf_op jit(solution)/shard_map/ppermute | solution.py:30
  407.8 23.8 %collective-permute-start.54 = (bf16[256,1024]{1,0:T(8,128)(2,1)S(1)}, bf16[256,1024]{1,0:T(8,128)(2,1)S(1)}, u32[]{:S(2)}, u32[]{:S(2)}) collective-permute-start(bf16[256,1024]{1,0:T(8,128)(2,1)S(1)} %get-tuple-element.588), channel_id=1, source_target_pairs={{0,2},{1,3},{2,0},{3,1},{4,6},{5,7},{6,4},{7,5},{8,10},{9,11},{10,... | collective-permute-start | bytes 1572872 | tf_op jit(solution)/shard_map/ppermute | solution.py:30
  464.0 23.0 %collective-permute-start.61 = (bf16[256,1024]{1,0:T(8,128)(2,1)S(1)}, bf16[256,1024]{1,0:T(8,128)(2,1)S(1)}, u32[]{:S(2)}, u32[]{:S(2)}) collective-permute-start(bf16[256,1024]{1,0:T(8,128)(2,1)S(1)} %get-tuple-element.628), channel_id=1, source_target_pairs={{0,2},{1,3},{2,0},{3,1},{4,6},{5,7},{6,4},{7,5},{8,10},{9,11},{10,... | collective-permute-start | bytes 1572872 | tf_op jit(solution)/shard_map/ppermute | solution.py:30
  487.8 122.8 %reduce-scatter.8.cloned.1.call-start = ((), (), s32[]{:S(2)}) async-start(), calls=%async_computation.8 | async-start | bytes 3932160 | tf_op jit(solution)/shard_map/reduce_scatter | solution.py:962
  561.2 54.8 %collective-permute-start.80 = (bf16[256,1024]{1,0:T(8,128)(2,1)S(1)}, bf16[256,1024]{1,0:T(8,128)(2,1)}, u32[]{:S(2)}, u32[]{:S(2)}) collective-permute-start(bf16[256,1024]{1,0:T(8,128)(2,1)S(1)} %get-tuple-element.696), channel_id=1, source_target_pairs={{0,3},{1,2},{2,1},{3,0},{4,7},{5,6},{6,5},{7,4},{8,11},{9,10},{10,... | collective-permute-start | bytes 1572872 | tf_op jit(solution)/shard_map/ppermute | solution.py:30
  566.3 49.7 %collective-permute-start.81 = (bf16[256,1024]{1,0:T(8,128)(2,1)S(1)}, bf16[256,1024]{1,0:T(8,128)(2,1)}, u32[]{:S(2)}, u32[]{:S(2)}) collective-permute-start(bf16[256,1024]{1,0:T(8,128)(2,1)S(1)} %get-tuple-element.697), channel_id=1, source_target_pairs={{0,1},{1,0},{2,3},{3,2},{4,5},{5,4},{6,7},{7,6},{8,9},{9,8},{10,11... | collective-permute-start | bytes 1572872 | tf_op jit(solution)/shard_map/ppermute | solution.py:30
  575.7 40.3 %collective-permute-start.82 = (bf16[256,1024]{1,0:T(8,128)(2,1)S(1)}, bf16[256,1024]{1,0:T(8,128)(2,1)}, u32[]{:S(2)}, u32[]{:S(2)}) collective-permute-start(bf16[256,1024]{1,0:T(8,128)(2,1)S(1)} %get-tuple-element.698), channel_id=1, source_target_pairs={{0,2},{1,3},{2,0},{3,1},{4,6},{5,7},{6,4},{7,5},{8,10},{9,11},{10,... | collective-permute-start | bytes 1572872 | tf_op jit(solution)/shard_map/ppermute | solution.py:30
  585.3 21.6 %collective-permute-start.77 = (bf16[4,64,512]{2,1,0:T(8,128)(2,1)}, bf16[4,64,512]{2,1,0:T(8,128)(2,1)S(1)}, u32[]{:S(2)}, u32[]{:S(2)}) collective-permute-start(bf16[4,64,512]{2,1,0:T(8,128)(2,1)} %get-tuple-element.744), channel_id=1, source_target_pairs={{0,8},{4,12},{8,0},{12,4},{1,9},{5,13},{9,1},{13,5},{2,10},{6,14},... | collective-permute-start | bytes 786440 | tf_op jit(solution)/shard_map/ppermute | solution.py:30
  609.3 35.8 %collective-permute-start.89 = (bf16[4,64,512]{2,1,0:T(8,128)(2,1)}, bf16[4,64,512]{2,1,0:T(8,128)(2,1)S(1)}, u32[]{:S(2)}, u32[]{:S(2)}) collective-permute-start(bf16[4,64,512]{2,1,0:T(8,128)(2,1)} %get-tuple-element.733.refs_0_), channel_id=1, source_target_pairs={{16,0},{17,1},{18,2},{19,3},{20,4},{21,5},{22,6},{23,7},{24,8},{25... | collective-permute-start | bytes 786440 | tf_op jit(solution)/shard_map/ppermute | solution.py:1042
  620.0 48.3 %collective-permute-start.83 = (f32[256,1024]{1,0:T(8,128)}, f32[256,1024]{1,0:T(8,128)}, u32[]{:S(2)}, u32[]{:S(2)}) collective-permute-start(f32[256,1024]{1,0:T(8,128)} %get-tuple-element.728), channel_id=1, source_target_pairs={{0,16},{16,0},{1,17},{17,1},{2,18},{18,2},{3,19},{19,3},{4,20},{20... | collective-permute-start | bytes 3145736 | tf_op jit(solution)/shard_map/ppermute | solution.py:30
  621.8 33.0 %collective-permute-start.90 = (bf16[3,128,1024]{2,1,0:T(8,128)(2,1)S(1)}, bf16[3,128,1024]{2,1,0:T(8,128)(2,1)S(1)}, u32[]{:S(2)}, u32[]{:S(2)}) collective-permute-start(bf16[3,128,1024]{2,1,0:T(8,128)(2,1)S(1)} %copy-done.33), channel_id=1, source_target_pairs={{16,0},{17,1},{18,2},{19,3},{20,4},{21,5},{22,6},{23,7},{24,8},{25... | collective-permute-start | bytes 2359304 | tf_op jit(solution)/shard_map/ppermute | solution.py:1042
  (138 other events, 1420.2 us)
Sparse Core Ops, SparseCore 0:
  40.8 66.5 all-gather.3
  115.8 27.0 all-gather.5
  145.1 62.9 all-gather.7
  354.0 60.5 reduce-scatter.3
  487.9 30.0 reduce-scatter.5
  520.3 60.3 reduce-scatter.7

commit v2 on v1

--- a/solution.py
+++ b/solution.py
@@ -656,13 +656,11 @@
     )
 
 
-def by_rows(steps, is_first, parts):
-    return half_of(is_first, parts, pl.program_id(0) < steps)
-
-
-def by_rows_turned(apart, is_first, parts):
-    if apart:
-        return half_of(is_first, parts, pl.program_id(1) == 0)[0].T[None]
+def by_rows(is_first, parts):
+    return half_of(is_first, parts, pl.program_id(0) == 0)
+
+
+def by_rows_turned(is_first, parts):
     both = [half_of(is_first, parts, low)[0] for low in (True, False)]
     return jnp.concatenate(both, axis=0).T[None]
 
@@ -814,11 +812,13 @@
         hidden, branch, mixing[:1], (grad_middle, *parts)
     )
     grads = [grad_branch, to(grad_branch, 1), to(grad_branch, 2)]
-    feed_sums = feed_grads(0, *operands, other)
+    low_ups, _ = tie(low_ups, grad_branch)
+    feed_sums = feed_grads(0, blocks_middle, blocks_mixed, low_ups, low_gates, gated, other)
     grads, _ = tie(grads, feed_sums)
     grads += pass_halves(*grads[1:])
     small = (scale_grads[0] + scale_grads[1] + scale_grads[3], rate_one[0], rate_two[0])
     if hooks:
+        small, _ = tie(small, feed_sums)
         small = hooks[0](small)
     low, partial, gain_grad = attend_back(
         info, starts, query, keys, values, attended, logsums, raw, grads,
@@ -1077,14 +1077,12 @@
     scalar = factor.reshape(1)
     head_rows, width = attention_out.shape[1:]
     feed_units = feedforward_out.shape[1]
-    rows = min(32, head_rows)
+    rows = min(64, head_rows)
     updates = []
     attend_halves, feed_halves = halves_of
     unit_half = feed_units // 2
-    apart = unit_half % 128 == 0
     turned = (
-        (1, width, unit_half if apart else feed_units), (1, unit_half, width),
-        lambda i, j: (i, 0, j), lambda i, j: (i, 0, 0), (2, 2 if apart else 1),
+        (1, width, feed_units), (1, unit_half, width), lambda i: (i, 0, 0), lambda i: (i, 0, 0), (2,)
     )
     update = functools.partial(adam_matrix, section_ref, scalar)
     new = update(
@@ -1100,15 +1098,13 @@
     ))
     new = update(
         [array[0] for array in (feedforward_in, first_feedforward_in, second_feedforward_in)],
-        feed_halves, 1, functools.partial(by_rows_turned, apart), *turned,
+        feed_halves, 1, by_rows_turned, *turned,
     )
     updates.extend(part[None] for part in new)
-    steps = max(1, feed_units // 128)
-    rows = feed_units // 2 // steps
     updates.extend(update(
         (feedforward_out, first_feedforward_out, second_feedforward_out),
-        feed_halves, 2, functools.partial(by_rows, steps), (1, rows, width), (1, rows, width),
-        lambda i: (0, i, 0), lambda i: (2, i % steps, 0), (2 * steps,),
+        feed_halves, 2, by_rows, (1, unit_half, width), (1, unit_half, width),
+        lambda i: (0, i, 0), lambda i: (2, 0, 0), (2,),
     ))
     updates.extend(
         adam_update(

time: 689 us -> 666 us (0.967)
  starting transfers between devices: 111 us -> 97 us
  waiting for transfers between devices: 217 us -> 206 us
    ppermute x84, starting transfers between devices: 101 us -> 86.2 us  [exchange(): return lax.ppermute(block, axis, route)]
    ppermute x84, waiting for transfers between devices: 187 us -> 176 us  [exchange(): return lax.ppermute(block, axis, route)]
    unnamed x131 -> x133, local copies, waits for them, and re-layouts: 13.8 us -> 13.2 us
  transfers between devices with their start and end apart: 97 -> 97, of which waited for: 50 -> 51; matrix products, arithmetic and copies ran while one was open for 7% -> 8% of each run, Pallas kernels for 36% -> 39%
where the time goes in v2:
time: 666 us; the launch traced here: 658 us
  Pallas kernels  264 us (40%)
  waiting for transfers between devices  206 us (31%)
  starting transfers between devices  97 us (15%)
  other arithmetic  42.4 us (6%)
  between operations  24.6 us (4%)
  local copies, waits for them, and re-layouts  23.5 us (4%)
    pallas_call x42, Pallas kernels, run(): pl.pallas_call(body, out_shape=[out if at in loose else pltpu.HBM(out.sha...  264 us
    ppermute x84, waiting for transfers between devices, exchange(): return lax.ppermute(block, axis, route)  176 us
    ppermute x84, starting transfers between devices, exchange(): return lax.ppermute(block, axis, route)  86.2 us
    ppermute x3, waiting for transfers between devices, ring_step(): return lax.ppermute(block, ('section', axis), route)  29.6 us
  transfers between devices with their start and end apart: 97, of which 51 were waited for; matrix products, arithmetic and copies ran while one was open for 8% of the time, Pallas kernels for 39%

profile of v2, /device:TPU:0, one launch (start us, length us, event | category | flops | bytes accessed | tf_op | source)
XLA Modules:
  0.0 657.9 jit_solution(10237166794377993128)
XLA Ops:
  23.2 8.5 %collective-permute-done.5 = bf16[4,64,512]{2,1,0:T(8,128)(2,1)} collective-permute-done((bf16[4,64,512]{2,1,0:T(8,128)(2,1)S(1)}, bf16[4,64,512]{2,1,0:T(8,128)(2,1)}, u32[]{:S(2)}, u32[]{:S(2)}) %collective-permute-start.5) | collective-permute-done | bytes 262176 | tf_op jit(solution)/shard_map/ppermute | solution.py:51
  52.9 15.2 %collective-permute-done.7 = bf16[4,64,512]{2,1,0:T(8,128)(2,1)S(1)} collective-permute-done((bf16[4,64,512]{2,1,0:T(8,128)(2,1)}, bf16[4,64,512]{2,1,0:T(8,128)(2,1)S(1)}, u32[]{:S(2)}, u32[]{:S(2)}) %collective-permute-start.7) | collective-permute-done | bytes 262176 | tf_op jit(solution)/shard_map/ppermute | solution.py:51
  84.1 7.9 %shard_map.358 = (bf16[256,256]{1,0:T(8,128)(2,1)}, f32[8,256]{1,0:T(8,128)}, bf16[256,1024]{1,0:T(8,128)(2,1)S(1)}, bf16[256,256]{1,0:T(8,128)(2,1)}, f32[8,256]{1,0:T(8,128)}, /*index=5*/bf16[256,1024]{1,0:T(8,128)(2,1)S(1)}) custom-call(s32[8]{0:T(128)S(1)} %concatenate.80.info, s32[4,256]{1,0:T(4,128)} %copy-done.48, ...), custom_call_target="tpu_custom_call" | custom-call | flops 939524096 | bytes 524288 | tf_op jit(solution)/shard_map/pallas_call | solution.py:138
  106.9 9.7 %collective-permute-done.14.refs_3_ = bf16[256,1024]{1,0:T(8,128)(2,1)S(1)} collective-permute-done((bf16[256,1024]{1,0:T(8,128)(2,1)S(1)}, bf16[256,1024]{1,0:T(8,128)(2,1)S(1)}, u32[]{:S(2)}, u32[]{:S(2)}) %collective-permute-start.14) | collective-permute-done | bytes 524320 | tf_op jit(solution)/shard_map/ppermute | solution.py:30
  139.7 7.6 %shard_map.362 = (bf16[256,1024]{1,0:T(8,128)(2,1)}, bf16[256,1024]{1,0:T(8,128)(2,1)}, bf16[1024,256]{1,0:T(8,128)(2,1)}, bf16[256,1024]{1,0:T(8,128)(2,1)}, bf...) custom-call(bf16[256,1024]{1,0:T(8,128)(2,1)S(1)} %collective-permut, ...), custom_call_target="tpu_custom_call" | custom-call | flops 3221225472 | bytes 6291456 | tf_op jit(solution)/shard_map/pallas_call | solution.py:138
  162.3 9.5 %collective-permute-done.22.refs_2_ = bf16[256,1024]{1,0:T(8,128)(2,1)S(1)} collective-permute-done((bf16[256,1024]{1,0:T(8,128)(2,1)S(1)}, bf16[256,1024]{1,0:T(8,128)(2,1)S(1)}, u32[]{:S(2)}, u32[]{:S(2)}) %collective-permute-start.22) | collective-permute-done | bytes 524320 | tf_op jit(solution)/shard_map/ppermute | solution.py:30
  202.3 7.8 %shard_map.369 = (bf16[256,256]{1,0:T(8,128)(2,1)}, f32[8,256]{1,0:T(8,128)}, bf16[256,1024]{1,0:T(8,128)(2,1)S(1)}, bf16[256,256]{1,0:T(8,128)(2,1)}, f32[8,256]{1,0:T(8,128)}, /*index=5*/bf16[256,1024]{1,0:T(8,128)(2,1)S(1)}) custom-call(s32[8]{0:T(128)S(1)} %concatenate.80.info, s32[4,256]{1,0:T(4,128)} %copy-done.48, ...), custom_call_target="tpu_custom_call" | custom-call | flops 939524096 | bytes 524288 | tf_op jit(solution)/shard_map/pallas_call | solution.py:138
  225.0 8.7 %collective-permute-done.31.refs_3_ = bf16[256,1024]{1,0:T(8,128)(2,1)S(1)} collective-permute-done((bf16[256,1024]{1,0:T(8,128)(2,1)S(1)}, bf16[256,1024]{1,0:T(8,128)(2,1)S(1)}, u32[]{:S(2)}, u32[]{:S(2)}) %collective-permute-start.31) | collective-permute-done | bytes 524320 | tf_op jit(solution)/shard_map/ppermute | solution.py:30
  255.7 7.6 %shard_map.373 = (bf16[256,1024]{1,0:T(8,128)(2,1)}, bf16[256,1024]{1,0:T(8,128)(2,1)}, bf16[1024,256]{1,0:T(8,128)(2,1)}, bf16[256,1024]{1,0:T(8,128)(2,1)}, bf...) custom-call(bf16[256,1024]{1,0:T(8,128)(2,1)S(1)} %collective-permut, ...), custom_call_target="tpu_custom_call" | custom-call | flops 3221225472 | bytes 6291456 | tf_op jit(solution)/shard_map/pallas_call | solution.py:138
  278.2 9.4 %collective-permute-done.38.refs_2_ = bf16[256,1024]{1,0:T(8,128)(2,1)S(1)} collective-permute-done((bf16[256,1024]{1,0:T(8,128)(2,1)S(1)}, bf16[256,1024]{1,0:T(8,128)(2,1)S(1)}, u32[]{:S(2)}, u32[]{:S(2)}) %collective-permute-start.38) | collective-permute-done | bytes 524320 | tf_op jit(solution)/shard_map/ppermute | solution.py:30
  309.5 9.8 %shard_map.378 = (bf16[1024,256]{1,0:T(8,128)(2,1)}, bf16[1024,256]{1,0:T(8,128)(2,1)}, bf16[1024,256]{1,0:T(8,128)(2,1)}, bf16[1024,256]{1,0:T(8,128)(2,1)}, f3...) custom-call(bf16[256,1024]{1,0:T(8,128)(2,1)S(1)} %collective-permute-done.40.refs_0_.refs_6_, ...), custom_call_target="tpu_custom_call" | custom-call | flops 3221225472 | bytes 6291456 | tf_op jit(solution)/shard_map/pallas_call | solution.py:138
  329.6 7.6 %shard_map.380 = bf16[3,512,1024]{2,1,0:T(8,128)(2,1)} custom-call(bf16[256,1024]{1,0:T(8,128)(2,1)} %get-tuple-element.556.refs_0_, bf16[256,1024]{1,0:T(8,128)(2,1)} %copy-done.12, bf16[256,1024]{1,0:T(8,128)(2,1)} %copy-done.13, bf16[128,1024]{1,0:T(8,128)(2,1)} %copy-done.16, bf16[128,1024]{1,0:T(8,128)(2,1)} %copy-done.17, ...), custom_call_target="tpu_custom_call" | custom-call | flops 3221225472 | bytes 9437184 | tf_op jit(solution)/shard_map/pallas_call | solution.py:138
  349.4 8.6 %shard_map.382 = bf16[3,512,1024]{2,1,0:T(8,128)(2,1)} custom-call(bf16[256,1024]{1,0:T(8,128)(2,1)} %get-tuple-element.556.refs_0_, bf16[256,1024]{1,0:T(8,128)(2,1)} %copy-done.12, bf16[256,1024]{1,0:T(8,128)(2,1)} %copy-done.13, bf16[128,1024]{1,0:T(8,128)(2,1)} %copy-done.16, bf16[128,1024]{1,0:T(8,128)(2,1)} %copy-done.17, ...), custom_call_target="tpu_custom_call" | custom-call | flops 3221225472 | bytes 9437184 | tf_op jit(solution)/shard_map/pallas_call | solution.py:138
  369.5 17.7 %shard_map.383 = (bf16[768,256]{1,0:T(8,128)(2,1)}, bf16[768,256]{1,0:T(8,128)(2,1)}, bf16[768,256]{1,0:T(8,128)(2,1)}, bf16[768,256]{1,0:T(8,128)(2,1)}, f32[25...) custom-call(s32[8]{0:T(128)S(1)} %concatenate.80.info, ...), custom_call_target="tpu_custom_call" | custom-call | flops 10200547328 | bytes 6291456 | tf_op jit(solution)/shard_map/pallas_call | solution.py:138
  387.1 7.4 %shard_map.384 = (f32[1024,512]{1,0:T(8,128)}, bf16[1024,512]{1,0:T(8,128)(2,1)}) custom-call(s32[1]{0:T(128)} %bitcast.section, bf16[768,256]{1,0:T(8,128)(2,1)} %get-tuple-element.604.refs_0_, bf16[768,256]{1,0:T(8,128)(2,1)} %get-tuple-element.605.refs_1_, bf16[768,256]{1,0:T(8,128)(2,1)} %get-tuple-element.606.refs_2_, ...), custom_call_target="tpu_custom_call" | custom-call | flops 2147483648 | bytes 8388608 | tf_op jit(solution)/shard_map/pallas_call | solution.py:138
  401.0 9.3 %collective-permute-done.52.refs_2_ = bf16[256,1024]{1,0:T(8,128)(2,1)S(1)} collective-permute-done((bf16[256,1024]{1,0:T(8,128)(2,1)S(1)}, bf16[256,1024]{1,0:T(8,128)(2,1)S(1)}, u32[]{:S(2)}, u32[]{:S(2)}) %collective-permute-start.52) | collective-permute-done | bytes 524320 | tf_op jit(solution)/shard_map/ppermute | solution.py:30
  410.2 10.3 %collective-permute-done.53.refs_3_ = bf16[256,1024]{1,0:T(8,128)(2,1)S(1)} collective-permute-done((bf16[256,1024]{1,0:T(8,128)(2,1)S(1)}, bf16[256,1024]{1,0:T(8,128)(2,1)S(1)}, u32[]{:S(2)}, u32[]{:S(2)}) %collective-permute-start.53) | collective-permute-done | bytes 524320 | tf_op jit(solution)/shard_map/ppermute | solution.py:30
  442.3 9.8 %shard_map.387 = (bf16[1024,256]{1,0:T(8,128)(2,1)}, bf16[1024,256]{1,0:T(8,128)(2,1)}, bf16[1024,256]{1,0:T(8,128)(2,1)}, bf16[1024,256]{1,0:T(8,128)(2,1)}, f3...) custom-call(bf16[256,1024]{1,0:T(8,128)(2,1)S(1)} %collective-permute-done.56.refs_0_.refs_6_, ...), custom_call_target="tpu_custom_call" | custom-call | flops 3221225472 | bytes 6291456 | tf_op jit(solution)/shard_map/pallas_call | solution.py:138
  462.7 7.6 %shard_map.389 = bf16[3,512,1024]{2,1,0:T(8,128)(2,1)} custom-call(bf16[256,1024]{1,0:T(8,128)(2,1)} %get-tuple-element.650.refs_0_, bf16[256,1024]{1,0:T(8,128)(2,1)} %copy-done.10, bf16[256,1024]{1,0:T(8,128)(2,1)} %copy-done.11, bf16[128,1024]{1,0:T(8,128)(2,1)} %copy-done.14, bf16[128,1024]{1,0:T(8,128)(2,1)} %copy-done.15, ...), custom_call_target="tpu_custom_call" | custom-call | flops 3221225472 | bytes 9437184 | tf_op jit(solution)/shard_map/pallas_call | solution.py:138
  483.2 8.6 %shard_map.391 = bf16[3,512,1024]{2,1,0:T(8,128)(2,1)} custom-call(bf16[256,1024]{1,0:T(8,128)(2,1)} %get-tuple-element.650.refs_0_, bf16[256,1024]{1,0:T(8,128)(2,1)} %copy-done.10, bf16[256,1024]{1,0:T(8,128)(2,1)} %copy-done.11, bf16[128,1024]{1,0:T(8,128)(2,1)} %copy-done.14, bf16[128,1024]{1,0:T(8,128)(2,1)} %copy-done.15, ...), custom_call_target="tpu_custom_call" | custom-call | flops 3221225472 | bytes 9437184 | tf_op jit(solution)/shard_map/pallas_call | solution.py:138
  495.9 11.3 %collective-permute-done.69 = f32[2,2048]{1,0:T(2,128)S(1)} collective-permute-done((f32[2,2048]{1,0:T(2,128)S(1)}, f32[2,2048]{1,0:T(2,128)S(1)}, u32[]{:S(2)}, u32[]{:S(2)}) %collective-permute-start.69) | collective-permute-done | bytes 16416 | tf_op jit(solution)/shard_map/ppermute | solution.py:30
  516.6 18.0 %shard_map.392 = (bf16[768,256]{1,0:T(8,128)(2,1)}, bf16[768,256]{1,0:T(8,128)(2,1)}, bf16[768,256]{1,0:T(8,128)(2,1)}, bf16[768,256]{1,0:T(8,128)(2,1)}, f32[25...) custom-call(s32[8]{0:T(128)S(1)} %concatenate.80.info, ...), custom_call_target="tpu_custom_call" | custom-call | flops 10200547328 | bytes 6291456 | tf_op jit(solution)/shard_map/pallas_call | solution.py:138
  566.2 10.1 %collective-permute-done.76 = bf16[4,64,512]{2,1,0:T(8,128)(2,1)S(1)} collective-permute-done((bf16[4,64,512]{2,1,0:T(8,128)(2,1)}, bf16[4,64,512]{2,1,0:T(8,128)(2,1)S(1)}, u32[]{:S(2)}, u32[]{:S(2)}) %collective-permute-start.76) | collective-permute-done | bytes 262176 | tf_op jit(solution)/shard_map/ppermute | solution.py:30
  578.0 9.7 %collective-permute-done.77 = bf16[4,64,512]{2,1,0:T(8,128)(2,1)S(1)} collective-permute-done((bf16[4,64,512]{2,1,0:T(8,128)(2,1)}, bf16[4,64,512]{2,1,0:T(8,128)(2,1)S(1)}, u32[]{:S(2)}, u32[]{:S(2)}) %collective-permute-start.77) | collective-permute-done | bytes 262176 | tf_op jit(solution)/shard_map/ppermute | solution.py:30
  (490 shorter events, 395.6 us)
Async XLA Ops:
  7.2 109.4 %all-gather.4.cloned.1.call-start = ((), (), s32[]{:S(2)}) async-start(), calls=%async_computation.3 | async-start | bytes 3932160 | tf_op jit(solution)/shard_map/all_gather | solution.py:932
  8.5 61.2 %collective-permute-start.1 = (bf16[256,1024]{1,0:T(8,128)(2,1)S(1)}, bf16[256,1024]{1,0:T(8,128)(2,1)S(1)}, u32[]{:S(2)}, u32[]{:S(2)}) collective-permute-start(bf16[256,1024]{1,0:T(8,128)(2,1)S(1)} %dynamic-slice_bitcast_fusion.1.refs_0_.hidden.refs_8_), channel_id=1, source_target_pairs={{0,2},{1,3},{2,0},{3,1},{4,6},{5,7},{6,4},{7,5},{8,10},{9,11},{10,... | collective-permute-start | bytes 1572872 | tf_op jit(solution)/shard_map/ppermute | solution.py:30
  11.5 59.0 %collective-permute-start = (bf16[256,1024]{1,0:T(8,128)(2,1)S(1)}, bf16[256,1024]{1,0:T(8,128)(2,1)S(1)}, u32[]{:S(2)}, u32[]{:S(2)}) collective-permute-start(bf16[256,1024]{1,0:T(8,128)(2,1)S(1)} %dynamic-slice_bitcast_fusion.1.refs_0_.hidden.refs_8_), channel_id=1, source_target_pairs={{0,1},{1,0},{2,3},{3,2},{4,5},{5,4},{6,7},{7,6},{8,9},{9,8},{10,11... | collective-permute-start | bytes 1572872 | tf_op jit(solution)/shard_map/ppermute | solution.py:30
  14.5 28.0 %collective-permute-start.9 = (bf16[1088]{0:T(1024)(128)(2,1)S(1)}, bf16[1088]{0:T(1024)(128)(2,1)S(1)}, u32[]{:S(2)}, u32[]{:S(2)}) collective-permute-start(bf16[1088]{0:T(1024)(128)(2,1)S(1)} %pad_maximum_fusion.13), channel_id=1, source_target_pairs={{0,16},{16,0},{1,17},{17,1},{2,18},{18,2},{3,19},{19,3},{4,20},{20... | collective-permute-start | bytes 6536 | tf_op jit(solution)/shard_map/ppermute | solution.py:30
  40.7 134.4 %all-gather.6.cloned.1.call-start = ((), (), s32[]{:S(2)}) async-start(), calls=%async_computation.4 | async-start | bytes 1310720 | tf_op jit(solution)/shard_map/all_gather | solution.py:914
  46.4 22.0 %collective-permute-start.11 = (bf16[2,2176]{1,0:T(2,128)(2,1)S(1)}, bf16[2,2176]{1,0:T(2,128)(2,1)S(1)}, u32[]{:S(2)}, u32[]{:S(2)}) collective-permute-start(bf16[2,2176]{1,0:T(2,128)(2,1)S(1)} %pad_maximum_fusion.9), channel_id=1, source_target_pairs={{0,8},{4,12},{8,0},{12,4},{1,9},{5,13},{9,1},{13,5},{2,10},{6,14},... | collective-permute-start | bytes 26120 | tf_op jit(solution)/shard_map/ppermute | solution.py:30
  92.0 24.6 %collective-permute-start.14 = (bf16[256,1024]{1,0:T(8,128)(2,1)S(1)}, bf16[256,1024]{1,0:T(8,128)(2,1)S(1)}, u32[]{:S(2)}, u32[]{:S(2)}) collective-permute-start(bf16[256,1024]{1,0:T(8,128)(2,1)S(1)} %get-tuple-element.396), channel_id=1, source_target_pairs={{0,2},{1,3},{2,0},{3,1},{4,6},{5,7},{6,4},{7,5},{8,10},{9,11},{10,... | collective-permute-start | bytes 1572872 | tf_op jit(solution)/shard_map/ppermute | solution.py:30
  116.7 104.5 %all-gather.8.cloned.1.call-start = ((), (), s32[]{:S(2)}) async-start(), calls=%async_computation.5 | async-start | bytes 3932160 | tf_op jit(solution)/shard_map/all_gather | solution.py:932
  117.4 426.3 %reduce-scatter.4.cloned.1.call-start = ((), (), s32[]{:S(2)}) async-start(), calls=%async_computation.6 | async-start | bytes 3932160 | tf_op jit(solution)/shard_map/reduce_scatter | solution.py:962
  147.8 24.0 %collective-permute-start.22 = (bf16[256,1024]{1,0:T(8,128)(2,1)S(1)}, bf16[256,1024]{1,0:T(8,128)(2,1)S(1)}, u32[]{:S(2)}, u32[]{:S(2)}) collective-permute-start(bf16[256,1024]{1,0:T(8,128)(2,1)S(1)} %get-tuple-element.442), channel_id=1, source_target_pairs={{0,2},{1,3},{2,0},{3,1},{4,6},{5,7},{6,4},{7,5},{8,10},{9,11},{10,... | collective-permute-start | bytes 1572872 | tf_op jit(solution)/shard_map/ppermute | solution.py:30
  210.2 23.6 %collective-permute-start.31 = (bf16[256,1024]{1,0:T(8,128)(2,1)S(1)}, bf16[256,1024]{1,0:T(8,128)(2,1)S(1)}, u32[]{:S(2)}, u32[]{:S(2)}) collective-permute-start(bf16[256,1024]{1,0:T(8,128)(2,1)S(1)} %get-tuple-element.486), channel_id=1, source_target_pairs={{0,2},{1,3},{2,0},{3,1},{4,6},{5,7},{6,4},{7,5},{8,10},{9,11},{10,... | collective-permute-start | bytes 1572872 | tf_op jit(solution)/shard_map/ppermute | solution.py:30
  263.7 23.9 %collective-permute-start.38 = (bf16[256,1024]{1,0:T(8,128)(2,1)S(1)}, bf16[256,1024]{1,0:T(8,128)(2,1)S(1)}, u32[]{:S(2)}, u32[]{:S(2)}) collective-permute-start(bf16[256,1024]{1,0:T(8,128)(2,1)S(1)} %get-tuple-element.518), channel_id=1, source_target_pairs={{0,2},{1,3},{2,0},{3,1},{4,6},{5,7},{6,4},{7,5},{8,10},{9,11},{10,... | collective-permute-start | bytes 1572872 | tf_op jit(solution)/shard_map/ppermute | solution.py:30
  363.1 183.2 %reduce-scatter.6.cloned.1.call-start = ((), (), s32[]{:S(2)}) async-start(), calls=%async_computation.7 | async-start | bytes 1310720 | tf_op jit(solution)/shard_map/reduce_scatter | solution.py:962
  396.0 24.5 %collective-permute-start.53 = (bf16[256,1024]{1,0:T(8,128)(2,1)S(1)}, bf16[256,1024]{1,0:T(8,128)(2,1)S(1)}, u32[]{:S(2)}, u32[]{:S(2)}) collective-permute-start(bf16[256,1024]{1,0:T(8,128)(2,1)S(1)} %get-tuple-element.602), channel_id=1, source_target_pairs={{0,1},{1,0},{2,3},{3,2},{4,5},{5,4},{6,7},{7,6},{8,9},{9,8},{10,11... | collective-permute-start | bytes 1572872 | tf_op jit(solution)/shard_map/ppermute | solution.py:30
  396.9 24.1 %collective-permute-start.54 = (bf16[256,1024]{1,0:T(8,128)(2,1)S(1)}, bf16[256,1024]{1,0:T(8,128)(2,1)S(1)}, u32[]{:S(2)}, u32[]{:S(2)}) collective-permute-start(bf16[256,1024]{1,0:T(8,128)(2,1)S(1)} %get-tuple-element.603), channel_id=1, source_target_pairs={{0,2},{1,3},{2,0},{3,1},{4,6},{5,7},{6,4},{7,5},{8,10},{9,11},{10,... | collective-permute-start | bytes 1572872 | tf_op jit(solution)/shard_map/ppermute | solution.py:30
  453.3 23.0 %collective-permute-start.61 = (bf16[256,1024]{1,0:T(8,128)(2,1)S(1)}, bf16[256,1024]{1,0:T(8,128)(2,1)S(1)}, u32[]{:S(2)}, u32[]{:S(2)}) collective-permute-start(bf16[256,1024]{1,0:T(8,128)(2,1)S(1)} %get-tuple-element.643), channel_id=1, source_target_pairs={{0,2},{1,3},{2,0},{3,1},{4,6},{5,7},{6,4},{7,5},{8,10},{9,11},{10,... | collective-permute-start | bytes 1572872 | tf_op jit(solution)/shard_map/ppermute | solution.py:30
  477.2 114.2 %reduce-scatter.8.cloned.1.call-start = ((), (), s32[]{:S(2)}) async-start(), calls=%async_computation.8 | async-start | bytes 3932160 | tf_op jit(solution)/shard_map/reduce_scatter | solution.py:962
  547.6 49.2 %collective-permute-start.80 = (bf16[256,1024]{1,0:T(8,128)(2,1)S(1)}, bf16[256,1024]{1,0:T(8,128)(2,1)}, u32[]{:S(2)}, u32[]{:S(2)}) collective-permute-start(bf16[256,1024]{1,0:T(8,128)(2,1)S(1)} %get-tuple-element.718), channel_id=1, source_target_pairs={{0,3},{1,2},{2,1},{3,0},{4,7},{5,6},{6,5},{7,4},{8,11},{9,10},{10,... | collective-permute-start | bytes 1572872 | tf_op jit(solution)/shard_map/ppermute | solution.py:30
  551.5 45.3 %collective-permute-start.81 = (bf16[256,1024]{1,0:T(8,128)(2,1)S(1)}, bf16[256,1024]{1,0:T(8,128)(2,1)}, u32[]{:S(2)}, u32[]{:S(2)}) collective-permute-start(bf16[256,1024]{1,0:T(8,128)(2,1)S(1)} %get-tuple-element.719), channel_id=1, source_target_pairs={{0,1},{1,0},{2,3},{3,2},{4,5},{5,4},{6,7},{7,6},{8,9},{9,8},{10,11... | collective-permute-start | bytes 1572872 | tf_op jit(solution)/shard_map/ppermute | solution.py:30
  557.1 39.7 %collective-permute-start.82 = (bf16[256,1024]{1,0:T(8,128)(2,1)S(1)}, bf16[256,1024]{1,0:T(8,128)(2,1)}, u32[]{:S(2)}, u32[]{:S(2)}) collective-permute-start(bf16[256,1024]{1,0:T(8,128)(2,1)S(1)} %get-tuple-element.720), channel_id=1, source_target_pairs={{0,2},{1,3},{2,0},{3,1},{4,6},{5,7},{6,4},{7,5},{8,10},{9,11},{10,... | collective-permute-start | bytes 1572872 | tf_op jit(solution)/shard_map/ppermute | solution.py:30
  566.1 21.6 %collective-permute-start.77 = (bf16[4,64,512]{2,1,0:T(8,128)(2,1)}, bf16[4,64,512]{2,1,0:T(8,128)(2,1)S(1)}, u32[]{:S(2)}, u32[]{:S(2)}) collective-permute-start(bf16[4,64,512]{2,1,0:T(8,128)(2,1)} %get-tuple-element.766), channel_id=1, source_target_pairs={{0,8},{4,12},{8,0},{12,4},{1,9},{5,13},{9,1},{13,5},{2,10},{6,14},... | collective-permute-start | bytes 786440 | tf_op jit(solution)/shard_map/ppermute | solution.py:30
  590.1 36.1 %collective-permute-start.89 = (bf16[4,64,512]{2,1,0:T(8,128)(2,1)}, bf16[4,64,512]{2,1,0:T(8,128)(2,1)S(1)}, u32[]{:S(2)}, u32[]{:S(2)}) collective-permute-start(bf16[4,64,512]{2,1,0:T(8,128)(2,1)} %get-tuple-element.755.refs_0_), channel_id=1, source_target_pairs={{16,0},{17,1},{18,2},{19,3},{20,4},{21,5},{22,6},{23,7},{24,8},{25... | collective-permute-start | bytes 786440 | tf_op jit(solution)/shard_map/ppermute | solution.py:1042
  600.8 45.5 %collective-permute-start.83 = (f32[256,1024]{1,0:T(8,128)}, f32[256,1024]{1,0:T(8,128)}, u32[]{:S(2)}, u32[]{:S(2)}) collective-permute-start(f32[256,1024]{1,0:T(8,128)} %get-tuple-element.750), channel_id=1, source_target_pairs={{0,16},{16,0},{1,17},{17,1},{2,18},{18,2},{3,19},{19,3},{4,20},{20... | collective-permute-start | bytes 3145736 | tf_op jit(solution)/shard_map/ppermute | solution.py:30
  602.4 32.4 %collective-permute-start.90 = (bf16[3,128,1024]{2,1,0:T(8,128)(2,1)S(1)}, bf16[3,128,1024]{2,1,0:T(8,128)(2,1)S(1)}, u32[]{:S(2)}, u32[]{:S(2)}) collective-permute-start(bf16[3,128,1024]{2,1,0:T(8,128)(2,1)S(1)} %copy-done.33), channel_id=1, source_target_pairs={{16,0},{17,1},{18,2},{19,3},{20,4},{21,5},{22,6},{23,7},{24,8},{25... | collective-permute-start | bytes 2359304 | tf_op jit(solution)/shard_map/ppermute | solution.py:1042
  (139 other events, 1422.7 us)
Sparse Core Ops, SparseCore 0:
  40.8 66.5 all-gather.3
  116.8 25.5 all-gather.5
  144.5 62.9 all-gather.7
  363.2 57.4 reduce-scatter.3
  477.3 24.5 reduce-scatter.5
  504.2 60.4 reduce-scatter.7

commit v3 on v2

--- a/solution.py
+++ b/solution.py
@@ -815,10 +815,10 @@
     low_ups, _ = tie(low_ups, grad_branch)
     feed_sums = feed_grads(0, blocks_middle, blocks_mixed, low_ups, low_gates, gated, other)
     grads, _ = tie(grads, feed_sums)
+    small = (scale_grads[0] + scale_grads[1] + scale_grads[3], rate_one[0], rate_two[0])
     grads += pass_halves(*grads[1:])
-    small = (scale_grads[0] + scale_grads[1] + scale_grads[3], rate_one[0], rate_two[0])
     if hooks:
-        small, _ = tie(small, feed_sums)
+        small, grads = tie(small, grads)
         small = hooks[0](small)
     low, partial, gain_grad = attend_back(
         info, starts, query, keys, values, attended, logsums, raw, grads,
@@ -963,14 +963,14 @@
 
     def scatter_direct(sums):
         if dp_size != 4:
-            return scatter(sums)
+            return scatter(sums), sums
         count = sums.shape[1] // dp_size
         parts = [
             lax.dynamic_slice_in_dim(sums, (dp_index ^ bits) * count, count, 1)
             for bits in range(dp_size)
         ]
         parts[1:] = [exchange(part, "dp", bits) for bits, part in enumerate(parts[1:], 1)]
-        return sum(part.astype(F32) for part in parts).astype(BF16)
+        return sum(part.astype(F32) for part in tie(*parts)).astype(BF16), parts[1]
 
     def small_vector(scales, rate_one, rate_two):
         return jnp.concatenate([units_back(scales[0]), units_back(scales[1]), rate_one, rate_two])
@@ -1001,24 +1001,18 @@
     width_qk, width_rates = gains_second.shape[0], 2 * dp_size * mix_rates.shape[2]
 
     def start_small(small_first):
-        values = jnp.stack([small_vector(*small_first), small_vector(*small_second)])
-        values = jnp.concatenate([values.reshape(-1), gains_second])
-        values = values + exchange(values, "section", 1)
-        values, gains = values[:-width_qk].reshape(2, -1), values[-width_qk:]
-        rates = sum_over(values[:, -width_rates:], "mp")
-        return jnp.concatenate([values[:, :-width_rates], rates], axis=1), gains
+        values = jnp.concatenate(
+            [small_vector(*small_first), small_vector(*small_second), gains_second]
+        )
+        return values, exchange(values, "section", 1)
 
     def next_small(low, small, gains):
-        low, (values, gains_two) = tie(low, small)
-        return low, (jnp.concatenate([values.reshape(-1), gains_two, gains]),)
+        low, (values, coming) = tie(low, small)
+        return low, (jnp.concatenate([values + coming, gains]),)
 
     def last_small(other, small):
         other, (values,) = tie(other, small)
-        bit = 1
-        while 2 * bit < dp_size:
-            values = values + exchange(values, "dp", bit)
-            bit *= 2
-        return other, (values, exchange(values, "dp", bit))
+        return other, (values, exchange(values, "dp", 1))
 
     parts, feed_first, attend_first, _, small = layer_backward(
         stored_first, parts, True, first, tables, weights_first, section_ref,
@@ -1028,10 +1022,12 @@
     sent_second = [
         lax.ppermute(part, "section", [(0, 1)]) for part in (attend_second, feed_second)
     ]
-    attend_first, feed_second, attend_second, small, sent_second = tie(
-        attend_first, feed_second, attend_second, small, sent_second
-    )
-    attend_first = scatter_direct(attend_first)
+    attend_first, came = scatter_direct(attend_first)
+    small, _ = tie(small, came)
+    sums, bit = small[0] + small[1], 2
+    while bit < dp_size:
+        sums = sums + exchange(sums, "dp", bit)
+        bit *= 2
 
     reduced_first = (attend_first, feed_first)
     reduced_second = (attend_second, feed_second)
@@ -1043,12 +1039,12 @@
         for one, two, theirs in zip(reduced_first, reduced_second, sent_second)
     ]
 
-    sums = small[0] + small[1]
     layer_sums = sums[: -2 * width_qk].reshape(2, -1)
     gain_first = sums[-width_qk:]
     gain_sums = jnp.stack([gain_first + exchange(gain_first, "section", 1), sums[-2 * width_qk : -width_qk]])
     scale_sums, rate_sums = layer_sums[:, :-width_rates], layer_sums[:, -width_rates:]
-    rate_sums = rate_sums.reshape(2, 2, -1)
+    near_rates, *far_rates = [rate_sums] + [to(rate_sums, at) for at in (1, 2, 3)]
+    rate_sums = ((near_rates + far_rates[0]) + (far_rates[1] + far_rates[2])).reshape(2, 2, -1)
     unit_grads = jnp.concatenate([gain_sums, scale_sums], axis=1)
     unit_grads = jnp.where(is_first, unit_grads[0], unit_grads[1])
     unit_grads = lax.dynamic_slice_in_dim(unit_grads, dp_index * units_here, units_here, 0)
@@ -1062,9 +1058,9 @@
     squares = squares + jnp.sum(unit_grads * unit_grads)
     squares = squares + leading * jnp.sum(rate_grads * rate_grads)
     squares = squares.reshape(1)
+    squares = sum_over(squares + exchange(squares, "section", 1), "mp")
     squares, parts = tie(squares, parts)
-    squares = squares + exchange(squares, "section", 1)
-    squares = sum_over(sum_over(squares, "mp"), "dp")
+    squares = sum_over(squares, "dp")
     gradient_norm = jnp.sqrt(squares[0])
     factor = CLIP_NORM / jnp.maximum(gradient_norm, CLIP_NORM)
 

time: 666 us -> 681 us (1.023)
  waiting for transfers between devices: 206 us -> 221 us
    ppermute x84 -> x85, waiting for transfers between devices: 176 us -> 190 us  [exchange(): return lax.ppermute(block, axis, route)]
    ppermute x84 -> x85, starting transfers between devices: 86.2 us -> 84.4 us  [exchange(): return lax.ppermute(block, axis, route)]
  transfers between devices with their start and end apart: 97 -> 98, of which waited for: 51 -> 53; matrix products, arithmetic and copies ran while one was open for 8% -> 7% of each run, Pallas kernels for 39% -> 35%
where the time goes in v3:
time: 681 us; the launch traced here: 670 us
  Pallas kernels  264 us (39%)
  waiting for transfers between devices  221 us (32%)
  starting transfers between devices  96 us (14%)
  other arithmetic  42.6 us (6%)
  between operations  24.2 us (4%)
  local copies, waits for them, and re-layouts  21.9 us (3%)
    pallas_call x42, Pallas kernels, run(): pl.pallas_call(body, out_shape=[out if at in loose else pltpu.HBM(out.sha...  264 us
    ppermute x85, waiting for transfers between devices, exchange(): return lax.ppermute(block, axis, route)  190 us
    ppermute x85, starting transfers between devices, exchange(): return lax.ppermute(block, axis, route)  84.4 us
    ppermute x3, waiting for transfers between devices, ring_step(): return lax.ppermute(block, ('section', axis), route)  29.6 us
  transfers between devices with their start and end apart: 98, of which 53 were waited for; matrix products, arithmetic and copies ran while one was open for 7% of the time, Pallas kernels for 35%

profile of v3, /device:TPU:0, one launch (start us, length us, event | category | flops | bytes accessed | tf_op | source)
XLA Modules:
  0.0 669.8 jit_solution(9197990230359071860)
XLA Ops:
  23.2 8.5 %collective-permute-done.5 = bf16[4,64,512]{2,1,0:T(8,128)(2,1)} collective-permute-done((bf16[4,64,512]{2,1,0:T(8,128)(2,1)S(1)}, bf16[4,64,512]{2,1,0:T(8,128)(2,1)}, u32[]{:S(2)}, u32[]{:S(2)}) %collective-permute-start.5) | collective-permute-done | bytes 262176 | tf_op jit(solution)/shard_map/ppermute | solution.py:51
  52.9 15.2 %collective-permute-done.7 = bf16[4,64,512]{2,1,0:T(8,128)(2,1)S(1)} collective-permute-done((bf16[4,64,512]{2,1,0:T(8,128)(2,1)}, bf16[4,64,512]{2,1,0:T(8,128)(2,1)S(1)}, u32[]{:S(2)}, u32[]{:S(2)}) %collective-permute-start.7) | collective-permute-done | bytes 262176 | tf_op jit(solution)/shard_map/ppermute | solution.py:51
  84.2 7.9 %shard_map.358 = (bf16[256,256]{1,0:T(8,128)(2,1)}, f32[8,256]{1,0:T(8,128)}, bf16[256,1024]{1,0:T(8,128)(2,1)S(1)}, bf16[256,256]{1,0:T(8,128)(2,1)}, f32[8,256]{1,0:T(8,128)}, /*index=5*/bf16[256,1024]{1,0:T(8,128)(2,1)S(1)}) custom-call(s32[8]{0:T(128)S(1)} %concatenate.71.info, s32[4,256]{1,0:T(4,128)} %copy-done.43, ...), custom_call_target="tpu_custom_call" | custom-call | flops 939524096 | bytes 524288 | tf_op jit(solution)/shard_map/pallas_call | solution.py:138
  106.9 8.7 %collective-permute-done.14.refs_3_ = bf16[256,1024]{1,0:T(8,128)(2,1)S(1)} collective-permute-done((bf16[256,1024]{1,0:T(8,128)(2,1)S(1)}, bf16[256,1024]{1,0:T(8,128)(2,1)S(1)}, u32[]{:S(2)}, u32[]{:S(2)}) %collective-permute-start.14) | collective-permute-done | bytes 524320 | tf_op jit(solution)/shard_map/ppermute | solution.py:30
  137.8 7.6 %shard_map.362 = (bf16[256,1024]{1,0:T(8,128)(2,1)}, bf16[256,1024]{1,0:T(8,128)(2,1)}, bf16[1024,256]{1,0:T(8,128)(2,1)}, bf16[256,1024]{1,0:T(8,128)(2,1)}, bf...) custom-call(bf16[256,1024]{1,0:T(8,128)(2,1)S(1)} %collective-permut, ...), custom_call_target="tpu_custom_call" | custom-call | flops 3221225472 | bytes 6291456 | tf_op jit(solution)/shard_map/pallas_call | solution.py:138
  161.1 9.2 %collective-permute-done.23.refs_3_ = bf16[256,1024]{1,0:T(8,128)(2,1)S(1)} collective-permute-done((bf16[256,1024]{1,0:T(8,128)(2,1)S(1)}, bf16[256,1024]{1,0:T(8,128)(2,1)S(1)}, u32[]{:S(2)}, u32[]{:S(2)}) %collective-permute-start.23) | collective-permute-done | bytes 524320 | tf_op jit(solution)/shard_map/ppermute | solution.py:30
  200.8 7.8 %shard_map.369 = (bf16[256,256]{1,0:T(8,128)(2,1)}, f32[8,256]{1,0:T(8,128)}, bf16[256,1024]{1,0:T(8,128)(2,1)S(1)}, bf16[256,256]{1,0:T(8,128)(2,1)}, f32[8,256]{1,0:T(8,128)}, /*index=5*/bf16[256,1024]{1,0:T(8,128)(2,1)S(1)}) custom-call(s32[8]{0:T(128)S(1)} %concatenate.71.info, s32[4,256]{1,0:T(4,128)} %copy-done.43, ...), custom_call_target="tpu_custom_call" | custom-call | flops 939524096 | bytes 524288 | tf_op jit(solution)/shard_map/pallas_call | solution.py:138
  223.5 7.4 %collective-permute-done.31.refs_3_ = bf16[256,1024]{1,0:T(8,128)(2,1)S(1)} collective-permute-done((bf16[256,1024]{1,0:T(8,128)(2,1)S(1)}, bf16[256,1024]{1,0:T(8,128)(2,1)S(1)}, u32[]{:S(2)}, u32[]{:S(2)}) %collective-permute-start.31) | collective-permute-done | bytes 524320 | tf_op jit(solution)/shard_map/ppermute | solution.py:30
  252.5 7.6 %shard_map.373 = (bf16[256,1024]{1,0:T(8,128)(2,1)}, bf16[256,1024]{1,0:T(8,128)(2,1)}, bf16[1024,256]{1,0:T(8,128)(2,1)}, bf16[256,1024]{1,0:T(8,128)(2,1)}, bf...) custom-call(bf16[256,1024]{1,0:T(8,128)(2,1)S(1)} %collective-permut, ...), custom_call_target="tpu_custom_call" | custom-call | flops 3221225472 | bytes 6291456 | tf_op jit(solution)/shard_map/pallas_call | solution.py:138
  275.0 9.5 %collective-permute-done.38.refs_2_ = bf16[256,1024]{1,0:T(8,128)(2,1)S(1)} collective-permute-done((bf16[256,1024]{1,0:T(8,128)(2,1)S(1)}, bf16[256,1024]{1,0:T(8,128)(2,1)S(1)}, u32[]{:S(2)}, u32[]{:S(2)}) %collective-permute-start.38) | collective-permute-done | bytes 524320 | tf_op jit(solution)/shard_map/ppermute | solution.py:30
  294.5 7.3 %shard_map.377 = (bf16[1024,256]{1,0:T(8,128)(2,1)}, bf16[1024,256]{1,0:T(8,128)(2,1)}, f32[2,1024]{1,0:T(2,128)}, f32[256,1024]{1,0:T(8,128)}) custom-call(bf16[256,1024]{1,0:T(8,128)(2,1)S(1)} %copy-done.6, bf16[3,512,1024]{2,1,0:T(8,128)(2,1)} %all-gather.8.cloned.1.call-done.refs_1_.refs_2_, ...), custom_call_target="tpu_custom_call" | custom-call | flops 1610612736 | bytes 6291456 | tf_op jit(solution)/shard_map/pallas_call | solution.py:138
  306.5 9.8 %shard_map.378 = (bf16[1024,256]{1,0:T(8,128)(2,1)}, bf16[1024,256]{1,0:T(8,128)(2,1)}, bf16[1024,256]{1,0:T(8,128)(2,1)}, bf16[1024,256]{1,0:T(8,128)(2,1)}, f3...) custom-call(bf16[256,1024]{1,0:T(8,128)(2,1)S(1)} %collective-permute-done.40.refs_0_.refs_6_, ...), custom_call_target="tpu_custom_call" | custom-call | flops 3221225472 | bytes 6291456 | tf_op jit(solution)/shard_map/pallas_call | solution.py:138
  326.5 7.6 %shard_map.380 = bf16[3,512,1024]{2,1,0:T(8,128)(2,1)} custom-call(bf16[256,1024]{1,0:T(8,128)(2,1)} %get-tuple-element.559.refs_0_, bf16[256,1024]{1,0:T(8,128)(2,1)} %copy-done.12, bf16[256,1024]{1,0:T(8,128)(2,1)} %copy-done.13, bf16[128,1024]{1,0:T(8,128)(2,1)} %copy-done.16, bf16[128,1024]{1,0:T(8,128)(2,1)} %copy-done.17, ...), custom_call_target="tpu_custom_call" | custom-call | flops 3221225472 | bytes 9437184 | tf_op jit(solution)/shard_map/pallas_call | solution.py:138
  345.9 8.7 %shard_map.382 = bf16[3,512,1024]{2,1,0:T(8,128)(2,1)} custom-call(bf16[256,1024]{1,0:T(8,128)(2,1)} %get-tuple-element.559.refs_0_, bf16[256,1024]{1,0:T(8,128)(2,1)} %copy-done.12, bf16[256,1024]{1,0:T(8,128)(2,1)} %copy-done.13, bf16[128,1024]{1,0:T(8,128)(2,1)} %copy-done.16, bf16[128,1024]{1,0:T(8,128)(2,1)} %copy-done.17, ...), custom_call_target="tpu_custom_call" | custom-call | flops 3221225472 | bytes 9437184 | tf_op jit(solution)/shard_map/pallas_call | solution.py:138
  366.0 17.7 %shard_map.383 = (bf16[768,256]{1,0:T(8,128)(2,1)}, bf16[768,256]{1,0:T(8,128)(2,1)}, bf16[768,256]{1,0:T(8,128)(2,1)}, bf16[768,256]{1,0:T(8,128)(2,1)}, f32[25...) custom-call(s32[8]{0:T(128)S(1)} %concatenate.71.info, ...), custom_call_target="tpu_custom_call" | custom-call | flops 10200547328 | bytes 6291456 | tf_op jit(solution)/shard_map/pallas_call | solution.py:138
  397.1 9.3 %collective-permute-done.52.refs_2_ = bf16[256,1024]{1,0:T(8,128)(2,1)S(1)} collective-permute-done((bf16[256,1024]{1,0:T(8,128)(2,1)S(1)}, bf16[256,1024]{1,0:T(8,128)(2,1)S(1)}, u32[]{:S(2)}, u32[]{:S(2)}) %collective-permute-start.52) | collective-permute-done | bytes 524320 | tf_op jit(solution)/shard_map/ppermute | solution.py:30
  406.3 10.5 %collective-permute-done.53.refs_3_ = bf16[256,1024]{1,0:T(8,128)(2,1)S(1)} collective-permute-done((bf16[256,1024]{1,0:T(8,128)(2,1)S(1)}, bf16[256,1024]{1,0:T(8,128)(2,1)S(1)}, u32[]{:S(2)}, u32[]{:S(2)}) %collective-permute-start.53) | collective-permute-done | bytes 524320 | tf_op jit(solution)/shard_map/ppermute | solution.py:30
  439.7 9.9 %shard_map.387 = (bf16[1024,256]{1,0:T(8,128)(2,1)}, bf16[1024,256]{1,0:T(8,128)(2,1)}, bf16[1024,256]{1,0:T(8,128)(2,1)}, bf16[1024,256]{1,0:T(8,128)(2,1)}, f3...) custom-call(bf16[256,1024]{1,0:T(8,128)(2,1)S(1)} %collective-permute-done.56.refs_0_.refs_6_, ...), custom_call_target="tpu_custom_call" | custom-call | flops 3221225472 | bytes 6291456 | tf_op jit(solution)/shard_map/pallas_call | solution.py:138
  460.0 7.7 %shard_map.389 = bf16[3,512,1024]{2,1,0:T(8,128)(2,1)} custom-call(bf16[256,1024]{1,0:T(8,128)(2,1)} %get-tuple-element.657.refs_0_, bf16[256,1024]{1,0:T(8,128)(2,1)} %copy-done.10, bf16[256,1024]{1,0:T(8,128)(2,1)} %copy-done.11, bf16[128,1024]{1,0:T(8,128)(2,1)} %copy-done.14, bf16[128,1024]{1,0:T(8,128)(2,1)} %copy-done.15, ...), custom_call_target="tpu_custom_call" | custom-call | flops 3221225472 | bytes 9437184 | tf_op jit(solution)/shard_map/pallas_call | solution.py:138
  481.8 8.5 %shard_map.391 = bf16[3,512,1024]{2,1,0:T(8,128)(2,1)} custom-call(bf16[256,1024]{1,0:T(8,128)(2,1)} %get-tuple-element.657.refs_0_, bf16[256,1024]{1,0:T(8,128)(2,1)} %copy-done.10, bf16[256,1024]{1,0:T(8,128)(2,1)} %copy-done.11, bf16[128,1024]{1,0:T(8,128)(2,1)} %copy-done.14, bf16[128,1024]{1,0:T(8,128)(2,1)} %copy-done.15, ...), custom_call_target="tpu_custom_call" | custom-call | flops 3221225472 | bytes 9437184 | tf_op jit(solution)/shard_map/pallas_call | solution.py:138
  503.7 18.0 %shard_map.392 = (bf16[768,256]{1,0:T(8,128)(2,1)}, bf16[768,256]{1,0:T(8,128)(2,1)}, bf16[768,256]{1,0:T(8,128)(2,1)}, bf16[768,256]{1,0:T(8,128)(2,1)}, f32[25...) custom-call(s32[8]{0:T(128)S(1)} %concatenate.71.info, ...), custom_call_target="tpu_custom_call" | custom-call | flops 10200547328 | bytes 6291456 | tf_op jit(solution)/shard_map/pallas_call | solution.py:138
  523.7 7.0 %shard_map.393 = (f32[1024,512]{1,0:T(8,128)}, bf16[1024,512]{1,0:T(8,128)(2,1)}) custom-call(s32[1]{0:T(128)} %bitcast.section, bf16[768,256]{1,0:T(8,128)(2,1)} %get-tuple-element.708.refs_0_, bf16[768,256]{1,0:T(8,128)(2,1)} %get-tuple-element.709.refs_1_, bf16[768,256]{1,0:T(8,128)(2,1)} %get-tuple-element.710.refs_2_, ...), custom_call_target="tpu_custom_call" | custom-call | flops 2147483648 | bytes 8388608 | tf_op jit(solution)/shard_map/pallas_call | solution.py:138
  544.2 21.9 %collective-permute-done.73 = f32[8704]{0:T(1024)S(1)} collective-permute-done((f32[8704]{0:T(1024)S(1)}, f32[8704]{0:T(1024)S(1)}, u32[]{:S(2)}, u32[]{:S(2)}) %collective-permute-start.73) | collective-permute-done | bytes 34848 | tf_op jit(solution)/shard_map/ppermute | solution.py:30
  575.3 15.2 %collective-permute-done.74 = f32[8704]{0:T(1024)S(1)} collective-permute-done((f32[8704]{0:T(1024)S(1)}, f32[8704]{0:T(1024)S(1)}, u32[]{:S(2)}, u32[]{:S(2)}) %collective-permute-start.74) | collective-permute-done | bytes 34848 | tf_op jit(solution)/shard_map/ppermute | solution.py:30
  (478 shorter events, 397.2 us)
Async XLA Ops:
  7.2 108.4 %all-gather.4.cloned.1.call-start = ((), (), s32[]{:S(2)}) async-start(), calls=%async_computation.3 | async-start | bytes 3932160 | tf_op jit(solution)/shard_map/all_gather | solution.py:932
  8.5 61.2 %collective-permute-start.1 = (bf16[256,1024]{1,0:T(8,128)(2,1)S(1)}, bf16[256,1024]{1,0:T(8,128)(2,1)S(1)}, u32[]{:S(2)}, u32[]{:S(2)}) collective-permute-start(bf16[256,1024]{1,0:T(8,128)(2,1)S(1)} %dynamic-slice_bitcast_fusion.1.refs_0_.hidden.refs_8_), channel_id=1, source_target_pairs={{0,2},{1,3},{2,0},{3,1},{4,6},{5,7},{6,4},{7,5},{8,10},{9,11},{10,... | collective-permute-start | bytes 1572872 | tf_op jit(solution)/shard_map/ppermute | solution.py:30
  11.5 59.0 %collective-permute-start = (bf16[256,1024]{1,0:T(8,128)(2,1)S(1)}, bf16[256,1024]{1,0:T(8,128)(2,1)S(1)}, u32[]{:S(2)}, u32[]{:S(2)}) collective-permute-start(bf16[256,1024]{1,0:T(8,128)(2,1)S(1)} %dynamic-slice_bitcast_fusion.1.refs_0_.hidden.refs_8_), channel_id=1, source_target_pairs={{0,1},{1,0},{2,3},{3,2},{4,5},{5,4},{6,7},{7,6},{8,9},{9,8},{10,11... | collective-permute-start | bytes 1572872 | tf_op jit(solution)/shard_map/ppermute | solution.py:30
  14.5 28.0 %collective-permute-start.9 = (bf16[1088]{0:T(1024)(128)(2,1)S(1)}, bf16[1088]{0:T(1024)(128)(2,1)S(1)}, u32[]{:S(2)}, u32[]{:S(2)}) collective-permute-start(bf16[1088]{0:T(1024)(128)(2,1)S(1)} %pad_maximum_fusion.9), channel_id=1, source_target_pairs={{0,16},{16,0},{1,17},{17,1},{2,18},{18,2},{3,19},{19,3},{4,20},{20... | collective-permute-start | bytes 6536 | tf_op jit(solution)/shard_map/ppermute | solution.py:30
  40.7 132.9 %all-gather.6.cloned.1.call-start = ((), (), s32[]{:S(2)}) async-start(), calls=%async_computation.4 | async-start | bytes 1310720 | tf_op jit(solution)/shard_map/all_gather | solution.py:914
  92.1 23.5 %collective-permute-start.14 = (bf16[256,1024]{1,0:T(8,128)(2,1)S(1)}, bf16[256,1024]{1,0:T(8,128)(2,1)S(1)}, u32[]{:S(2)}, u32[]{:S(2)}) collective-permute-start(bf16[256,1024]{1,0:T(8,128)(2,1)S(1)} %get-tuple-element.400), channel_id=1, source_target_pairs={{0,2},{1,3},{2,0},{3,1},{4,6},{5,7},{6,4},{7,5},{8,10},{9,11},{10,... | collective-permute-start | bytes 1572872 | tf_op jit(solution)/shard_map/ppermute | solution.py:30
  115.7 104.0 %all-gather.8.cloned.1.call-start = ((), (), s32[]{:S(2)}) async-start(), calls=%async_computation.5 | async-start | bytes 3932160 | tf_op jit(solution)/shard_map/all_gather | solution.py:932
  116.4 424.0 %reduce-scatter.6.cloned.1.call-start = ((), (), s32[]{:S(2)}) async-start(), calls=%async_computation.7 | async-start | bytes 1310720 | tf_op jit(solution)/shard_map/reduce_scatter | solution.py:962
  208.7 22.2 %collective-permute-start.31 = (bf16[256,1024]{1,0:T(8,128)(2,1)S(1)}, bf16[256,1024]{1,0:T(8,128)(2,1)S(1)}, u32[]{:S(2)}, u32[]{:S(2)}) collective-permute-start(bf16[256,1024]{1,0:T(8,128)(2,1)S(1)} %get-tuple-element.489), channel_id=1, source_target_pairs={{0,2},{1,3},{2,0},{3,1},{4,6},{5,7},{6,4},{7,5},{8,10},{9,11},{10,... | collective-permute-start | bytes 1572872 | tf_op jit(solution)/shard_map/ppermute | solution.py:30
  260.9 23.6 %collective-permute-start.38 = (bf16[256,1024]{1,0:T(8,128)(2,1)S(1)}, bf16[256,1024]{1,0:T(8,128)(2,1)S(1)}, u32[]{:S(2)}, u32[]{:S(2)}) collective-permute-start(bf16[256,1024]{1,0:T(8,128)(2,1)S(1)} %get-tuple-element.521), channel_id=1, source_target_pairs={{0,2},{1,3},{2,0},{3,1},{4,6},{5,7},{6,4},{7,5},{8,10},{9,11},{10,... | collective-permute-start | bytes 1572872 | tf_op jit(solution)/shard_map/ppermute | solution.py:30
  392.1 24.8 %collective-permute-start.53 = (bf16[256,1024]{1,0:T(8,128)(2,1)S(1)}, bf16[256,1024]{1,0:T(8,128)(2,1)S(1)}, u32[]{:S(2)}, u32[]{:S(2)}) collective-permute-start(bf16[256,1024]{1,0:T(8,128)(2,1)S(1)} %get-tuple-element.605), channel_id=1, source_target_pairs={{0,1},{1,0},{2,3},{3,2},{4,5},{5,4},{6,7},{7,6},{8,9},{9,8},{10,11... | collective-permute-start | bytes 1572872 | tf_op jit(solution)/shard_map/ppermute | solution.py:30
  393.2 23.9 %collective-permute-start.54 = (bf16[256,1024]{1,0:T(8,128)(2,1)S(1)}, bf16[256,1024]{1,0:T(8,128)(2,1)S(1)}, u32[]{:S(2)}, u32[]{:S(2)}) collective-permute-start(bf16[256,1024]{1,0:T(8,128)(2,1)S(1)} %get-tuple-element.606), channel_id=1, source_target_pairs={{0,2},{1,3},{2,0},{3,1},{4,6},{5,7},{6,4},{7,5},{8,10},{9,11},{10,... | collective-permute-start | bytes 1572872 | tf_op jit(solution)/shard_map/ppermute | solution.py:30
  417.2 149.6 %reduce-scatter.8.cloned.1.call-start = ((), (), s32[]{:S(2)}) async-start(), calls=%async_computation.8 | async-start | bytes 3932160 | tf_op jit(solution)/shard_map/reduce_scatter | solution.py:962
  417.8 184.8 %reduce-scatter.4.cloned.1.call-start = ((), (), s32[]{:S(2)}) async-start(), calls=%async_computation.6 | async-start | bytes 3932160 | tf_op jit(solution)/shard_map/reduce_scatter | solution.py:962
  450.5 23.1 %collective-permute-start.61 = (bf16[256,1024]{1,0:T(8,128)(2,1)S(1)}, bf16[256,1024]{1,0:T(8,128)(2,1)S(1)}, u32[]{:S(2)}, u32[]{:S(2)}) collective-permute-start(bf16[256,1024]{1,0:T(8,128)(2,1)S(1)} %get-tuple-element.645), channel_id=1, source_target_pairs={{0,2},{1,3},{2,0},{3,1},{4,6},{5,7},{6,4},{7,5},{8,10},{9,11},{10,... | collective-permute-start | bytes 1572872 | tf_op jit(solution)/shard_map/ppermute | solution.py:30
  535.7 30.4 %collective-permute-start.70 = (bf16[4,64,512]{2,1,0:T(8,128)(2,1)S(1)}, bf16[4,64,512]{2,1,0:T(8,128)(2,1)S(1)}, u32[]{:S(2)}, u32[]{:S(2)}) collective-permute-start(bf16[4,64,512]{2,1,0:T(8,128)(2,1)S(1)} %get-tuple-element.774), channel_id=1, source_target_pairs={{0,4},{4,0},{8,12},{12,8},{1,5},{5,1},{9,13},{13,9},{2,6},{6,2},{1... | collective-permute-start | bytes 786440 | tf_op jit(solution)/shard_map/ppermute | solution.py:30
  535.7 30.4 %collective-permute-start.73 = (f32[8704]{0:T(1024)S(1)}, f32[8704]{0:T(1024)S(1)}, u32[]{:S(2)}, u32[]{:S(2)}) collective-permute-start(f32[8704]{0:T(1024)S(1)} %pad_maximum_fusion.3), channel_id=1, source_target_pairs={{0,4},{4,0},{8,12},{12,8},{1,5},{5,1},{9,13},{13,9},{2,6},{6,2},{1... | collective-permute-start | bytes 104456 | tf_op jit(solution)/shard_map/ppermute | solution.py:30
  537.7 31.2 %collective-permute-start.71 = (bf16[4,64,512]{2,1,0:T(8,128)(2,1)S(1)}, bf16[4,64,512]{2,1,0:T(8,128)(2,1)}, u32[]{:S(2)}, u32[]{:S(2)}) collective-permute-start(bf16[4,64,512]{2,1,0:T(8,128)(2,1)S(1)} %get-tuple-element.773), channel_id=1, source_target_pairs={{0,8},{4,12},{8,0},{12,4},{1,9},{5,13},{9,1},{13,5},{2,10},{6,14},... | collective-permute-start | bytes 786440 | tf_op jit(solution)/shard_map/ppermute | solution.py:30
  539.0 36.3 %collective-permute-start.72 = (bf16[4,64,512]{2,1,0:T(8,128)(2,1)S(1)}, bf16[4,64,512]{2,1,0:T(8,128)(2,1)}, u32[]{:S(2)}, u32[]{:S(2)}) collective-permute-start(bf16[4,64,512]{2,1,0:T(8,128)(2,1)S(1)} %get-tuple-element.772), channel_id=1, source_target_pairs={{0,12},{4,8},{8,4},{12,0},{1,13},{5,9},{9,5},{13,1},{2,14},{6,10},... | collective-permute-start | bytes 786440 | tf_op jit(solution)/shard_map/ppermute | solution.py:30
  542.1 96.6 %collective-permute-start.89 = (bf16[4,64,512]{2,1,0:T(8,128)(2,1)}, bf16[4,64,512]{2,1,0:T(8,128)(2,1)}, u32[]{:S(2)}, u32[]{:S(2)}) collective-permute-start(bf16[4,64,512]{2,1,0:T(8,128)(2,1)} %reduce-scatter.6.cloned.1.call-done.refs_1_), channel_id=1, source_target_pairs={{0,16},{1,17},{2,18},{3,19},{4,20},{5,21},{6,22},{7,23},{8,24},{9,... | collective-permute-start | bytes 786440 | tf_op jit(solution)/shard_map/ppermute | solution.py:1023
  566.1 53.3 %collective-permute-start.82 = (bf16[256,1024]{1,0:T(8,128)(2,1)S(1)}, bf16[256,1024]{1,0:T(8,128)(2,1)S(1)}, u32[]{:S(2)}, u32[]{:S(2)}) collective-permute-start(bf16[256,1024]{1,0:T(8,128)(2,1)S(1)} %get-tuple-element.728), channel_id=1, source_target_pairs={{0,3},{1,2},{2,1},{3,0},{4,7},{5,6},{6,5},{7,4},{8,11},{9,10},{10,... | collective-permute-start | bytes 1572872 | tf_op jit(solution)/shard_map/ppermute | solution.py:30
  566.1 24.4 %collective-permute-start.74 = (f32[8704]{0:T(1024)S(1)}, f32[8704]{0:T(1024)S(1)}, u32[]{:S(2)}, u32[]{:S(2)}) collective-permute-start(f32[8704]{0:T(1024)S(1)} %add.265), channel_id=1, source_target_pairs={{0,8},{4,12},{8,0},{12,4},{1,9},{5,13},{9,1},{13,5},{2,10},{6,14},... | collective-permute-start | bytes 104456 | tf_op jit(solution)/shard_map/ppermute | solution.py:30
  597.0 22.4 %collective-permute-start.83 = (bf16[256,1024]{1,0:T(8,128)(2,1)S(1)}, bf16[256,1024]{1,0:T(8,128)(2,1)S(1)}, u32[]{:S(2)}, u32[]{:S(2)}) collective-permute-start(bf16[256,1024]{1,0:T(8,128)(2,1)S(1)} %get-tuple-element.729), channel_id=1, source_target_pairs={{0,1},{1,0},{2,3},{3,2},{4,5},{5,4},{6,7},{7,6},{8,9},{9,8},{10,11... | collective-permute-start | bytes 1572872 | tf_op jit(solution)/shard_map/ppermute | solution.py:30
  624.2 34.0 %collective-permute-start.85 = (f32[256,1024]{1,0:T(8,128)}, f32[256,1024]{1,0:T(8,128)}, u32[]{:S(2)}, u32[]{:S(2)}) collective-permute-start(f32[256,1024]{1,0:T(8,128)} %get-tuple-element.758), channel_id=1, source_target_pairs={{0,16},{16,0},{1,17},{17,1},{2,18},{18,2},{3,19},{19,3},{4,20},{20... | collective-permute-start | bytes 3145736 | tf_op jit(solution)/shard_map/ppermute | solution.py:30
  (134 other events, 1383.4 us)
Sparse Core Ops, SparseCore 0:
  40.8 66.5 all-gather.3
  115.8 26.9 all-gather.5
  144.9 63.0 all-gather.7
  417.3 26.2 reduce-scatter.5
  445.8 58.9 reduce-scatter.7
  507.0 78.5 reduce-scatter.3

commit v4 on v3

--- a/solution.py
+++ b/solution.py
@@ -1012,7 +1012,11 @@
 
     def last_small(other, small):
         other, (values,) = tie(other, small)
-        return other, (values, exchange(values, "dp", 1))
+        bit = 1
+        while 2 * bit < dp_size:
+            values = values + exchange(values, "dp", bit)
+            bit *= 2
+        return other, (values, exchange(values, "dp", bit))
 
     parts, feed_first, attend_first, _, small = layer_backward(
         stored_first, parts, True, first, tables, weights_first, section_ref,
@@ -1022,12 +1026,12 @@
     sent_second = [
         lax.ppermute(part, "section", [(0, 1)]) for part in (attend_second, feed_second)
     ]
+    attend_first, feed_second, attend_second, small, sent_second = tie(
+        attend_first, feed_second, attend_second, small, sent_second
+    )
     attend_first, came = scatter_direct(attend_first)
-    small, _ = tie(small, came)
-    sums, bit = small[0] + small[1], 2
-    while bit < dp_size:
-        sums = sums + exchange(sums, "dp", bit)
-        bit *= 2
+    (sums, coming), _ = tie(small, came)
+    sums = sums + coming
 
     reduced_first = (attend_first, feed_first)
     reduced_second = (attend_second, feed_second)
@@ -1058,9 +1062,9 @@
     squares = squares + jnp.sum(unit_grads * unit_grads)
     squares = squares + leading * jnp.sum(rate_grads * rate_grads)
     squares = squares.reshape(1)
-    squares = sum_over(squares + exchange(squares, "section", 1), "mp")
     squares, parts = tie(squares, parts)
-    squares = sum_over(squares, "dp")
+    squares = squares + exchange(squares, "section", 1)
+    squares = sum_over(sum_over(squares, "mp"), "dp")
     gradient_norm = jnp.sqrt(squares[0])
     factor = CLIP_NORM / jnp.maximum(gradient_norm, CLIP_NORM)
 

time: 681 us -> 671 us (0.985)
  waiting for transfers between devices: 221 us -> 205 us
    ppermute x85, waiting for transfers between devices: 190 us -> 175 us  [exchange(): return lax.ppermute(block, axis, route)]
    unnamed x129 -> x135, local copies, waits for them, and re-layouts: 13.5 us -> 14.1 us
  transfers between devices with their start and end apart: 98 -> 98, of which waited for: 53 -> 52; matrix products, arithmetic and copies ran while one was open for 7% -> 7% of each run, Pallas kernels for 35% -> 39%
where the time goes in v4:
time: 671 us; the launch traced here: 660 us
  Pallas kernels  264 us (39%)
  waiting for transfers between devices  205 us (31%)
  starting transfers between devices  101 us (15%)
  other arithmetic  42.4 us (6%)
  between operations  23.8 us (4%)
  local copies, waits for them, and re-layouts  23.3 us (3%)
    pallas_call x42, Pallas kernels, run(): pl.pallas_call(body, out_shape=[out if at in loose else pltpu.HBM(out.sha...  264 us
    ppermute x85, waiting for transfers between devices, exchange(): return lax.ppermute(block, axis, route)  175 us
    ppermute x85, starting transfers between devices, exchange(): return lax.ppermute(block, axis, route)  91 us
    ppermute x3, waiting for transfers between devices, ring_step(): return lax.ppermute(block, ('section', axis), route)  29.6 us
    unnamed x135, local copies, waits for them, and re-layouts  14.1 us
  transfers between devices with their start and end apart: 98, of which 52 were waited for; matrix products, arithmetic and copies ran while one was open for 7% of the time, Pallas kernels for 39%

profile of v4, /device:TPU:0, one launch (start us, length us, event | category | flops | bytes accessed | tf_op | source)
XLA Modules:
  0.0 660.4 jit_solution(8573837007600601507)
XLA Ops:
  23.2 8.5 %collective-permute-done.5 = bf16[4,64,512]{2,1,0:T(8,128)(2,1)} collective-permute-done((bf16[4,64,512]{2,1,0:T(8,128)(2,1)S(1)}, bf16[4,64,512]{2,1,0:T(8,128)(2,1)}, u32[]{:S(2)}, u32[]{:S(2)}) %collective-permute-start.5) | collective-permute-done | bytes 262176 | tf_op jit(solution)/shard_map/ppermute | solution.py:51
  52.9 15.2 %collective-permute-done.7 = bf16[4,64,512]{2,1,0:T(8,128)(2,1)S(1)} collective-permute-done((bf16[4,64,512]{2,1,0:T(8,128)(2,1)}, bf16[4,64,512]{2,1,0:T(8,128)(2,1)S(1)}, u32[]{:S(2)}, u32[]{:S(2)}) %collective-permute-start.7) | collective-permute-done | bytes 262176 | tf_op jit(solution)/shard_map/ppermute | solution.py:51
  84.2 6.9 %shard_map.358 = (bf16[256,256]{1,0:T(8,128)(2,1)}, f32[8,256]{1,0:T(8,128)}, bf16[256,1024]{1,0:T(8,128)(2,1)S(1)}, bf16[256,256]{1,0:T(8,128)(2,1)}, f32[8,256]{1,0:T(8,128)}, /*index=5*/bf16[256,1024]{1,0:T(8,128)(2,1)S(1)}) custom-call(s32[8]{0:T(128)S(1)} %concatenate.71.info, s32[4,256]{1,0:T(4,128)} %copy-done.48, ...), custom_call_target="tpu_custom_call" | custom-call | flops 939524096 | bytes 524288 | tf_op jit(solution)/shard_map/pallas_call | solution.py:138
  105.8 10.9 %collective-permute-done.14.refs_3_ = bf16[256,1024]{1,0:T(8,128)(2,1)S(1)} collective-permute-done((bf16[256,1024]{1,0:T(8,128)(2,1)S(1)}, bf16[256,1024]{1,0:T(8,128)(2,1)S(1)}, u32[]{:S(2)}, u32[]{:S(2)}) %collective-permute-start.14) | collective-permute-done | bytes 524320 | tf_op jit(solution)/shard_map/ppermute | solution.py:30
  139.8 7.6 %shard_map.362 = (bf16[256,1024]{1,0:T(8,128)(2,1)}, bf16[256,1024]{1,0:T(8,128)(2,1)}, bf16[1024,256]{1,0:T(8,128)(2,1)}, bf16[256,1024]{1,0:T(8,128)(2,1)}, bf...) custom-call(bf16[256,1024]{1,0:T(8,128)(2,1)S(1)} %collective-permut, ...), custom_call_target="tpu_custom_call" | custom-call | flops 3221225472 | bytes 6291456 | tf_op jit(solution)/shard_map/pallas_call | solution.py:138
  162.3 9.5 %collective-permute-done.22.refs_2_ = bf16[256,1024]{1,0:T(8,128)(2,1)S(1)} collective-permute-done((bf16[256,1024]{1,0:T(8,128)(2,1)S(1)}, bf16[256,1024]{1,0:T(8,128)(2,1)S(1)}, u32[]{:S(2)}, u32[]{:S(2)}) %collective-permute-start.22) | collective-permute-done | bytes 524320 | tf_op jit(solution)/shard_map/ppermute | solution.py:30
  224.1 9.7 %collective-permute-done.31.refs_3_ = bf16[256,1024]{1,0:T(8,128)(2,1)S(1)} collective-permute-done((bf16[256,1024]{1,0:T(8,128)(2,1)S(1)}, bf16[256,1024]{1,0:T(8,128)(2,1)S(1)}, u32[]{:S(2)}, u32[]{:S(2)}) %collective-permute-start.31) | collective-permute-done | bytes 524320 | tf_op jit(solution)/shard_map/ppermute | solution.py:30
  255.7 7.5 %shard_map.373 = (bf16[256,1024]{1,0:T(8,128)(2,1)}, bf16[256,1024]{1,0:T(8,128)(2,1)}, bf16[1024,256]{1,0:T(8,128)(2,1)}, bf16[256,1024]{1,0:T(8,128)(2,1)}, bf...) custom-call(bf16[256,1024]{1,0:T(8,128)(2,1)S(1)} %collective-permut, ...), custom_call_target="tpu_custom_call" | custom-call | flops 3221225472 | bytes 6291456 | tf_op jit(solution)/shard_map/pallas_call | solution.py:138
  278.2 9.4 %collective-permute-done.38.refs_2_ = bf16[256,1024]{1,0:T(8,128)(2,1)S(1)} collective-permute-done((bf16[256,1024]{1,0:T(8,128)(2,1)S(1)}, bf16[256,1024]{1,0:T(8,128)(2,1)S(1)}, u32[]{:S(2)}, u32[]{:S(2)}) %collective-permute-start.38) | collective-permute-done | bytes 524320 | tf_op jit(solution)/shard_map/ppermute | solution.py:30
  297.5 7.3 %shard_map.377 = (bf16[1024,256]{1,0:T(8,128)(2,1)}, bf16[1024,256]{1,0:T(8,128)(2,1)}, f32[2,1024]{1,0:T(2,128)}, f32[256,1024]{1,0:T(8,128)}) custom-call(bf16[256,1024]{1,0:T(8,128)(2,1)S(1)} %copy-done.6, bf16[3,512,1024]{2,1,0:T(8,128)(2,1)} %all-gather.8.cloned.1.call-done.refs_1_.refs_2_, ...), custom_call_target="tpu_custom_call" | custom-call | flops 1610612736 | bytes 6291456 | tf_op jit(solution)/shard_map/pallas_call | solution.py:138
  309.5 9.8 %shard_map.378 = (bf16[1024,256]{1,0:T(8,128)(2,1)}, bf16[1024,256]{1,0:T(8,128)(2,1)}, bf16[1024,256]{1,0:T(8,128)(2,1)}, bf16[1024,256]{1,0:T(8,128)(2,1)}, f3...) custom-call(bf16[256,1024]{1,0:T(8,128)(2,1)S(1)} %collective-permute-done.40.refs_0_.refs_6_, ...), custom_call_target="tpu_custom_call" | custom-call | flops 3221225472 | bytes 6291456 | tf_op jit(solution)/shard_map/pallas_call | solution.py:138
  329.6 7.6 %shard_map.380 = bf16[3,512,1024]{2,1,0:T(8,128)(2,1)} custom-call(bf16[256,1024]{1,0:T(8,128)(2,1)} %get-tuple-element.566.refs_0_, bf16[256,1024]{1,0:T(8,128)(2,1)} %copy-done.12, bf16[256,1024]{1,0:T(8,128)(2,1)} %copy-done.13, bf16[128,1024]{1,0:T(8,128)(2,1)} %copy-done.16, bf16[128,1024]{1,0:T(8,128)(2,1)} %copy-done.17, ...), custom_call_target="tpu_custom_call" | custom-call | flops 3221225472 | bytes 9437184 | tf_op jit(solution)/shard_map/pallas_call | solution.py:138
  349.3 8.6 %shard_map.382 = bf16[3,512,1024]{2,1,0:T(8,128)(2,1)} custom-call(bf16[256,1024]{1,0:T(8,128)(2,1)} %get-tuple-element.566.refs_0_, bf16[256,1024]{1,0:T(8,128)(2,1)} %copy-done.12, bf16[256,1024]{1,0:T(8,128)(2,1)} %copy-done.13, bf16[128,1024]{1,0:T(8,128)(2,1)} %copy-done.16, bf16[128,1024]{1,0:T(8,128)(2,1)} %copy-done.17, ...), custom_call_target="tpu_custom_call" | custom-call | flops 3221225472 | bytes 9437184 | tf_op jit(solution)/shard_map/pallas_call | solution.py:138
  369.4 17.7 %shard_map.383 = (bf16[768,256]{1,0:T(8,128)(2,1)}, bf16[768,256]{1,0:T(8,128)(2,1)}, bf16[768,256]{1,0:T(8,128)(2,1)}, bf16[768,256]{1,0:T(8,128)(2,1)}, f32[25...) custom-call(s32[8]{0:T(128)S(1)} %concatenate.71.info, ...), custom_call_target="tpu_custom_call" | custom-call | flops 10200547328 | bytes 6291456 | tf_op jit(solution)/shard_map/pallas_call | solution.py:138
  387.1 7.4 %shard_map.384 = (f32[1024,512]{1,0:T(8,128)}, bf16[1024,512]{1,0:T(8,128)(2,1)}) custom-call(s32[1]{0:T(128)} %bitcast.section, bf16[768,256]{1,0:T(8,128)(2,1)} %get-tuple-element.614.refs_0_, bf16[768,256]{1,0:T(8,128)(2,1)} %get-tuple-element.615.refs_1_, bf16[768,256]{1,0:T(8,128)(2,1)} %get-tuple-element.616.refs_2_, ...), custom_call_target="tpu_custom_call" | custom-call | flops 2147483648 | bytes 8388608 | tf_op jit(solution)/shard_map/pallas_call | solution.py:138
  400.9 9.3 %collective-permute-done.52.refs_2_ = bf16[256,1024]{1,0:T(8,128)(2,1)S(1)} collective-permute-done((bf16[256,1024]{1,0:T(8,128)(2,1)S(1)}, bf16[256,1024]{1,0:T(8,128)(2,1)S(1)}, u32[]{:S(2)}, u32[]{:S(2)}) %collective-permute-start.52) | collective-permute-done | bytes 524320 | tf_op jit(solution)/shard_map/ppermute | solution.py:30
  410.1 10.4 %collective-permute-done.53.refs_3_ = bf16[256,1024]{1,0:T(8,128)(2,1)S(1)} collective-permute-done((bf16[256,1024]{1,0:T(8,128)(2,1)S(1)}, bf16[256,1024]{1,0:T(8,128)(2,1)S(1)}, u32[]{:S(2)}, u32[]{:S(2)}) %collective-permute-start.53) | collective-permute-done | bytes 524320 | tf_op jit(solution)/shard_map/ppermute | solution.py:30
  428.5 6.9 %shard_map.386 = (bf16[1024,256]{1,0:T(8,128)(2,1)}, bf16[1024,256]{1,0:T(8,128)(2,1)}, f32[2,1024]{1,0:T(2,128)}, f32[256,1024]{1,0:T(8,128)}) custom-call(bf16[256,1024]{1,0:T(8,128)(2,1)S(1)} %copy-done.4, bf16[3,512,1024]{2,1,0:T(8,128)(2,1)} %all-gather.4.cloned.1.call-done.refs_1_.refs_2_, ...), custom_call_target="tpu_custom_call" | custom-call | flops 1610612736 | bytes 6291456 | tf_op jit(solution)/shard_map/pallas_call | solution.py:138
  442.3 9.8 %shard_map.387 = (bf16[1024,256]{1,0:T(8,128)(2,1)}, bf16[1024,256]{1,0:T(8,128)(2,1)}, bf16[1024,256]{1,0:T(8,128)(2,1)}, bf16[1024,256]{1,0:T(8,128)(2,1)}, f3...) custom-call(bf16[256,1024]{1,0:T(8,128)(2,1)S(1)} %collective-permute-done.56.refs_0_.refs_6_, ...), custom_call_target="tpu_custom_call" | custom-call | flops 3221225472 | bytes 6291456 | tf_op jit(solution)/shard_map/pallas_call | solution.py:138
  462.6 7.6 %shard_map.389 = bf16[3,512,1024]{2,1,0:T(8,128)(2,1)} custom-call(bf16[256,1024]{1,0:T(8,128)(2,1)} %get-tuple-element.664.refs_0_, bf16[256,1024]{1,0:T(8,128)(2,1)} %copy-done.10, bf16[256,1024]{1,0:T(8,128)(2,1)} %copy-done.11, bf16[128,1024]{1,0:T(8,128)(2,1)} %copy-done.14, bf16[128,1024]{1,0:T(8,128)(2,1)} %copy-done.15, ...), custom_call_target="tpu_custom_call" | custom-call | flops 3221225472 | bytes 9437184 | tf_op jit(solution)/shard_map/pallas_call | solution.py:138
  485.2 8.7 %shard_map.391 = bf16[3,512,1024]{2,1,0:T(8,128)(2,1)} custom-call(bf16[256,1024]{1,0:T(8,128)(2,1)} %get-tuple-element.664.refs_0_, bf16[256,1024]{1,0:T(8,128)(2,1)} %copy-done.10, bf16[256,1024]{1,0:T(8,128)(2,1)} %copy-done.11, bf16[128,1024]{1,0:T(8,128)(2,1)} %copy-done.14, bf16[128,1024]{1,0:T(8,128)(2,1)} %copy-done.15, ...), custom_call_target="tpu_custom_call" | custom-call | flops 3221225472 | bytes 9437184 | tf_op jit(solution)/shard_map/pallas_call | solution.py:138
  508.5 18.1 %shard_map.392 = (bf16[768,256]{1,0:T(8,128)(2,1)}, bf16[768,256]{1,0:T(8,128)(2,1)}, bf16[768,256]{1,0:T(8,128)(2,1)}, bf16[768,256]{1,0:T(8,128)(2,1)}, f32[25...) custom-call(s32[8]{0:T(128)S(1)} %concatenate.71.info, ...), custom_call_target="tpu_custom_call" | custom-call | flops 10200547328 | bytes 6291456 | tf_op jit(solution)/shard_map/pallas_call | solution.py:138
  528.7 6.9 %shard_map.393 = (f32[1024,512]{1,0:T(8,128)}, bf16[1024,512]{1,0:T(8,128)(2,1)}) custom-call(s32[1]{0:T(128)} %bitcast.section, bf16[768,256]{1,0:T(8,128)(2,1)} %get-tuple-element.715.refs_0_, bf16[768,256]{1,0:T(8,128)(2,1)} %get-tuple-element.716.refs_1_, bf16[768,256]{1,0:T(8,128)(2,1)} %get-tuple-element.717.refs_2_, ...), custom_call_target="tpu_custom_call" | custom-call | flops 2147483648 | bytes 8388608 | tf_op jit(solution)/shard_map/pallas_call | solution.py:138
  559.9 14.3 %collective-permute-done.74 = bf16[4,64,512]{2,1,0:T(8,128)(2,1)S(1)} collective-permute-done((bf16[4,64,512]{2,1,0:T(8,128)(2,1)S(1)}, bf16[4,64,512]{2,1,0:T(8,128)(2,1)S(1)}, u32[]{:S(2)}, u32[]{:S(2)}) %collective-permute-start.74) | collective-permute-done | bytes 262176 | tf_op jit(solution)/shard_map/ppermute | solution.py:30
  (484 shorter events, 401.1 us)
Async XLA Ops:
  7.3 109.4 %all-gather.4.cloned.1.call-start = ((), (), s32[]{:S(2)}) async-start(), calls=%async_computation.3 | async-start | bytes 3932160 | tf_op jit(solution)/shard_map/all_gather | solution.py:932
  8.5 61.2 %collective-permute-start.1 = (bf16[256,1024]{1,0:T(8,128)(2,1)S(1)}, bf16[256,1024]{1,0:T(8,128)(2,1)S(1)}, u32[]{:S(2)}, u32[]{:S(2)}) collective-permute-start(bf16[256,1024]{1,0:T(8,128)(2,1)S(1)} %dynamic-slice_bitcast_fusion.1.refs_0_.hidden.refs_8_), channel_id=1, source_target_pairs={{0,2},{1,3},{2,0},{3,1},{4,6},{5,7},{6,4},{7,5},{8,10},{9,11},{10,... | collective-permute-start | bytes 1572872 | tf_op jit(solution)/shard_map/ppermute | solution.py:30
  11.5 59.0 %collective-permute-start = (bf16[256,1024]{1,0:T(8,128)(2,1)S(1)}, bf16[256,1024]{1,0:T(8,128)(2,1)S(1)}, u32[]{:S(2)}, u32[]{:S(2)}) collective-permute-start(bf16[256,1024]{1,0:T(8,128)(2,1)S(1)} %dynamic-slice_bitcast_fusion.1.refs_0_.hidden.refs_8_), channel_id=1, source_target_pairs={{0,1},{1,0},{2,3},{3,2},{4,5},{5,4},{6,7},{7,6},{8,9},{9,8},{10,11... | collective-permute-start | bytes 1572872 | tf_op jit(solution)/shard_map/ppermute | solution.py:30
  14.5 28.0 %collective-permute-start.9 = (bf16[1088]{0:T(1024)(128)(2,1)S(1)}, bf16[1088]{0:T(1024)(128)(2,1)S(1)}, u32[]{:S(2)}, u32[]{:S(2)}) collective-permute-start(bf16[1088]{0:T(1024)(128)(2,1)S(1)} %pad_maximum_fusion.9), channel_id=1, source_target_pairs={{0,16},{16,0},{1,17},{17,1},{2,18},{18,2},{3,19},{19,3},{4,20},{20... | collective-permute-start | bytes 6536 | tf_op jit(solution)/shard_map/ppermute | solution.py:30
  40.7 134.4 %all-gather.6.cloned.1.call-start = ((), (), s32[]{:S(2)}) async-start(), calls=%async_computation.4 | async-start | bytes 1310720 | tf_op jit(solution)/shard_map/all_gather | solution.py:914
  46.4 22.0 %collective-permute-start.11 = (bf16[2,2176]{1,0:T(2,128)(2,1)S(1)}, bf16[2,2176]{1,0:T(2,128)(2,1)S(1)}, u32[]{:S(2)}, u32[]{:S(2)}) collective-permute-start(bf16[2,2176]{1,0:T(2,128)(2,1)S(1)} %pad_maximum_fusion.5), channel_id=1, source_target_pairs={{0,8},{4,12},{8,0},{12,4},{1,9},{5,13},{9,1},{13,5},{2,10},{6,14},... | collective-permute-start | bytes 26120 | tf_op jit(solution)/shard_map/ppermute | solution.py:30
  92.4 24.3 %collective-permute-start.14 = (bf16[256,1024]{1,0:T(8,128)(2,1)S(1)}, bf16[256,1024]{1,0:T(8,128)(2,1)S(1)}, u32[]{:S(2)}, u32[]{:S(2)}) collective-permute-start(bf16[256,1024]{1,0:T(8,128)(2,1)S(1)} %get-tuple-element.407), channel_id=1, source_target_pairs={{0,2},{1,3},{2,0},{3,1},{4,6},{5,7},{6,4},{7,5},{8,10},{9,11},{10,... | collective-permute-start | bytes 1572872 | tf_op jit(solution)/shard_map/ppermute | solution.py:30
  116.7 104.0 %all-gather.8.cloned.1.call-start = ((), (), s32[]{:S(2)}) async-start(), calls=%async_computation.5 | async-start | bytes 3932160 | tf_op jit(solution)/shard_map/all_gather | solution.py:932
  117.4 418.7 %reduce-scatter.4.cloned.1.call-start = ((), (), s32[]{:S(2)}) async-start(), calls=%async_computation.6 | async-start | bytes 3932160 | tf_op jit(solution)/shard_map/reduce_scatter | solution.py:962
  147.8 24.0 %collective-permute-start.22 = (bf16[256,1024]{1,0:T(8,128)(2,1)S(1)}, bf16[256,1024]{1,0:T(8,128)(2,1)S(1)}, u32[]{:S(2)}, u32[]{:S(2)}) collective-permute-start(bf16[256,1024]{1,0:T(8,128)(2,1)S(1)} %get-tuple-element.452), channel_id=1, source_target_pairs={{0,2},{1,3},{2,0},{3,1},{4,6},{5,7},{6,4},{7,5},{8,10},{9,11},{10,... | collective-permute-start | bytes 1572872 | tf_op jit(solution)/shard_map/ppermute | solution.py:30
  210.6 23.1 %collective-permute-start.31 = (bf16[256,1024]{1,0:T(8,128)(2,1)S(1)}, bf16[256,1024]{1,0:T(8,128)(2,1)S(1)}, u32[]{:S(2)}, u32[]{:S(2)}) collective-permute-start(bf16[256,1024]{1,0:T(8,128)(2,1)S(1)} %get-tuple-element.496), channel_id=1, source_target_pairs={{0,2},{1,3},{2,0},{3,1},{4,6},{5,7},{6,4},{7,5},{8,10},{9,11},{10,... | collective-permute-start | bytes 1572872 | tf_op jit(solution)/shard_map/ppermute | solution.py:30
  263.7 23.9 %collective-permute-start.38 = (bf16[256,1024]{1,0:T(8,128)(2,1)S(1)}, bf16[256,1024]{1,0:T(8,128)(2,1)S(1)}, u32[]{:S(2)}, u32[]{:S(2)}) collective-permute-start(bf16[256,1024]{1,0:T(8,128)(2,1)S(1)} %get-tuple-element.528), channel_id=1, source_target_pairs={{0,2},{1,3},{2,0},{3,1},{4,6},{5,7},{6,4},{7,5},{8,10},{9,11},{10,... | collective-permute-start | bytes 1572872 | tf_op jit(solution)/shard_map/ppermute | solution.py:30
  358.0 180.3 %reduce-scatter.6.cloned.1.call-start = ((), (), s32[]{:S(2)}) async-start(), calls=%async_computation.7 | async-start | bytes 1310720 | tf_op jit(solution)/shard_map/reduce_scatter | solution.py:962
  396.0 24.5 %collective-permute-start.53 = (bf16[256,1024]{1,0:T(8,128)(2,1)S(1)}, bf16[256,1024]{1,0:T(8,128)(2,1)S(1)}, u32[]{:S(2)}, u32[]{:S(2)}) collective-permute-start(bf16[256,1024]{1,0:T(8,128)(2,1)S(1)} %get-tuple-element.612), channel_id=1, source_target_pairs={{0,1},{1,0},{2,3},{3,2},{4,5},{5,4},{6,7},{7,6},{8,9},{9,8},{10,11... | collective-permute-start | bytes 1572872 | tf_op jit(solution)/shard_map/ppermute | solution.py:30
  396.9 24.0 %collective-permute-start.54 = (bf16[256,1024]{1,0:T(8,128)(2,1)S(1)}, bf16[256,1024]{1,0:T(8,128)(2,1)S(1)}, u32[]{:S(2)}, u32[]{:S(2)}) collective-permute-start(bf16[256,1024]{1,0:T(8,128)(2,1)S(1)} %get-tuple-element.613), channel_id=1, source_target_pairs={{0,2},{1,3},{2,0},{3,1},{4,6},{5,7},{6,4},{7,5},{8,10},{9,11},{10,... | collective-permute-start | bytes 1572872 | tf_op jit(solution)/shard_map/ppermute | solution.py:30
  453.3 23.1 %collective-permute-start.61 = (bf16[256,1024]{1,0:T(8,128)(2,1)S(1)}, bf16[256,1024]{1,0:T(8,128)(2,1)S(1)}, u32[]{:S(2)}, u32[]{:S(2)}) collective-permute-start(bf16[256,1024]{1,0:T(8,128)(2,1)S(1)} %get-tuple-element.652), channel_id=1, source_target_pairs={{0,2},{1,3},{2,0},{3,1},{4,6},{5,7},{6,4},{7,5},{8,10},{9,11},{10,... | collective-permute-start | bytes 1572872 | tf_op jit(solution)/shard_map/ppermute | solution.py:30
  477.2 113.5 %reduce-scatter.8.cloned.1.call-start = ((), (), s32[]{:S(2)}) async-start(), calls=%async_computation.8 | async-start | bytes 3932160 | tf_op jit(solution)/shard_map/reduce_scatter | solution.py:962
  539.6 56.6 %collective-permute-start.81 = (bf16[256,1024]{1,0:T(8,128)(2,1)S(1)}, bf16[256,1024]{1,0:T(8,128)(2,1)}, u32[]{:S(2)}, u32[]{:S(2)}) collective-permute-start(bf16[256,1024]{1,0:T(8,128)(2,1)S(1)} %get-tuple-element.740), channel_id=1, source_target_pairs={{0,3},{1,2},{2,1},{3,0},{4,7},{5,6},{6,5},{7,4},{8,11},{9,10},{10,... | collective-permute-start | bytes 1572872 | tf_op jit(solution)/shard_map/ppermute | solution.py:30
  543.4 52.8 %collective-permute-start.82 = (bf16[256,1024]{1,0:T(8,128)(2,1)S(1)}, bf16[256,1024]{1,0:T(8,128)(2,1)}, u32[]{:S(2)}, u32[]{:S(2)}) collective-permute-start(bf16[256,1024]{1,0:T(8,128)(2,1)S(1)} %get-tuple-element.741), channel_id=1, source_target_pairs={{0,1},{1,0},{2,3},{3,2},{4,5},{5,4},{6,7},{7,6},{8,9},{9,8},{10,11... | collective-permute-start | bytes 1572872 | tf_op jit(solution)/shard_map/ppermute | solution.py:30
  553.7 22.6 %collective-permute-start.75 = (bf16[4,64,512]{2,1,0:T(8,128)(2,1)}, bf16[4,64,512]{2,1,0:T(8,128)(2,1)}, u32[]{:S(2)}, u32[]{:S(2)}) collective-permute-start(bf16[4,64,512]{2,1,0:T(8,128)(2,1)} %get-tuple-element.787), channel_id=1, source_target_pairs={{0,8},{4,12},{8,0},{12,4},{1,9},{5,13},{9,1},{13,5},{2,10},{6,14},... | collective-permute-start | bytes 786440 | tf_op jit(solution)/shard_map/ppermute | solution.py:30
  555.3 26.8 %collective-permute-start.76 = (bf16[4,64,512]{2,1,0:T(8,128)(2,1)}, bf16[4,64,512]{2,1,0:T(8,128)(2,1)}, u32[]{:S(2)}, u32[]{:S(2)}) collective-permute-start(bf16[4,64,512]{2,1,0:T(8,128)(2,1)} %get-tuple-element.786), channel_id=1, source_target_pairs={{0,12},{4,8},{8,4},{12,0},{1,13},{5,9},{9,5},{13,1},{2,14},{6,10},... | collective-permute-start | bytes 786440 | tf_op jit(solution)/shard_map/ppermute | solution.py:30
  587.0 42.6 %collective-permute-start.90 = (bf16[4,64,512]{2,1,0:T(8,128)(2,1)S(1)}, bf16[4,64,512]{2,1,0:T(8,128)(2,1)S(1)}, u32[]{:S(2)}, u32[]{:S(2)}) collective-permute-start(bf16[4,64,512]{2,1,0:T(8,128)(2,1)S(1)} %get-tuple-element.777.refs_0_), channel_id=1, source_target_pairs={{16,0},{17,1},{18,2},{19,3},{20,4},{21,5},{22,6},{23,7},{24,8},{25... | collective-permute-start | bytes 786440 | tf_op jit(solution)/shard_map/ppermute | solution.py:1042
  604.2 44.7 %collective-permute-start.84 = (f32[256,1024]{1,0:T(8,128)}, f32[256,1024]{1,0:T(8,128)}, u32[]{:S(2)}, u32[]{:S(2)}) collective-permute-start(f32[256,1024]{1,0:T(8,128)} %get-tuple-element.772), channel_id=1, source_target_pairs={{0,16},{16,0},{1,17},{17,1},{2,18},{18,2},{3,19},{19,3},{4,20},{20... | collective-permute-start | bytes 3145736 | tf_op jit(solution)/shard_map/ppermute | solution.py:30
  606.6 31.7 %collective-permute-start.91 = (bf16[3,128,1024]{2,1,0:T(8,128)(2,1)S(1)}, bf16[3,128,1024]{2,1,0:T(8,128)(2,1)}, u32[]{:S(2)}, u32[]{:S(2)}) collective-permute-start(bf16[3,128,1024]{2,1,0:T(8,128)(2,1)S(1)} %copy-done.34), channel_id=1, source_target_pairs={{16,0},{17,1},{18,2},{19,3},{20,4},{21,5},{22,6},{23,7},{24,8},{25... | collective-permute-start | bytes 2359304 | tf_op jit(solution)/shard_map/ppermute | solution.py:1042
  (137 other events, 1407.6 us)
Sparse Core Ops, SparseCore 0:
  40.8 66.5 all-gather.3
  116.8 26.0 all-gather.5
  145.1 62.9 all-gather.7
  358.1 57.4 reduce-scatter.3
  477.4 24.4 reduce-scatter.5
  504.1 67.7 reduce-scatter.7
